TPU v7x, 512 devices: a whole 4x4x16 slice. The times are simulated.
512 devices in a mesh: gx: 16 (over x, y_lo, core), gy: 16 (over z), gz: 2 (over y_hi).
Axes of the slice: x: 4, y: 4 (y_hi: 2, y_lo: 2; y = y_hi * 2 + y_lo), z: 16, core: 2. Of those that a mesh axis runs over, the one named last changes fastest.
Arguments:
- velocity: float32 [3, 32, 1536, 2048], P(None, 'gz', 'gy', 'gx'), may hold values from -6 to 6
- below: float32 [3, 2, 1536, 2048], P(None, None, 'gy', 'gx'), may hold values from -6 to 6
- above: float32 [3, 2, 1536, 2048], P(None, None, 'gy', 'gx'), may hold values from -6 to 6
- omega_x: int32 [2048, 256], P('gx'), may hold values from -1 to 1
- omega_y: int32 [1536, 256], P('gy'), may hold values from -1 to 1
- omega_z: int32 [32, 256], P('gz'), may hold values from -1 to 1
- phi_x: int32 [512, 2048], P(None, 'gx'), may hold values from -1 to 1
- phi_y: int32 [512, 1536], P(None, 'gy'), may hold values from -1 to 1
- phi_z: int32 [2, 32], P(None, 'gz'), may hold values from -1 to 1
Outputs:
- factor_x: float32 [2048, 256], P('gx')
- factor_y: float32 [1536, 256], P('gy')
- factor_z: float32 [32, 256], P('gz')
- core_sketch: float32 [512, 2, 512], P(('gx', 'gy', 'gz'))
All inputs are finite; a program needn't handle non-finite values.
Results may differ from a plain program's by a relative error of at most 0.000088.
Values sent between devices are 32-bit elements; how exact they have to be, the bound alone decides.
No kernel may reach another device: no remote copies, remote signals or barrier semaphores. Data moves between devices by JAX's collectives and lax.ppermute only.
A program may use at most 64 MiB of HBM per device.

v0:
```python
import math

import jax
import jax.numpy as jnp
from jax import lax
from jax.sharding import PartitionSpec as P

precise = lax.Precision.HIGHEST


def extended(cells, sides, width, closed):
    for axis, dim in sides:
        count = lax.axis_size(axis)
        ends = count if closed else count - 1
        head = lax.slice_in_dim(cells, 0, width, axis=dim)
        tail = lax.slice_in_dim(cells, cells.shape[dim] - width, cells.shape[dim], axis=dim)
        cells = jnp.concatenate(
            [
                lax.ppermute(tail, axis, [(i, (i + 1) % count) for i in range(ends)]),
                cells,
                lax.ppermute(head, axis, [((i + 1) % count, i) for i in range(ends)]),
            ],
            axis=dim,
        )
    return cells


def derivative(padded, direction):
    length = padded.shape[direction] - 4

    def window(offset):
        return lax.slice_in_dim(padded, offset, offset + length, axis=direction)

    return (window(0) - 8.0 * window(1) + 8.0 * window(3) - window(4)) / 12.0


def criterion(gradient):
    summed = jnp.zeros(gradient[0].shape[1:], gradient[0].dtype)
    for component in range(3):
        for direction in range(3):
            summed = summed + gradient[direction][component] * gradient[component][direction]
    return -0.5 * summed


def shards(velocity, below, above, omega_x, omega_y, omega_z, phi_x, phi_y, phi_z):
    count_x = lax.axis_size("gx")
    count_y = lax.axis_size("gy")
    count_z = lax.axis_size("gz")
    total_x = velocity.shape[3] * count_x
    total_y = velocity.shape[2] * count_y
    total_z = velocity.shape[1] * count_z
    planes = extended(velocity, (("gz", 1),), 2, False)
    position = lax.axis_index("gz")
    lower_rim = jnp.where(position == 0, below, planes[:, :2])
    upper_rim = jnp.where(position == count_z - 1, above, planes[:, -2:])
    planes = jnp.concatenate([lower_rim, planes[:, 2:-2], upper_rim], axis=1)
    sides = extended(velocity, (("gx", 3), ("gy", 2)), 2, True)
    gradient = [
        derivative(sides[:, :, 2:-2, :], 3),
        derivative(sides[:, :, :, 2:-2], 2),
        derivative(planes, 1),
    ]
    qfield = criterion(gradient)
    ternary_x = omega_x.astype(jnp.float32)
    ternary_y = omega_y.astype(jnp.float32)
    ternary_z = omega_z.astype(jnp.float32)
    contract_y = jnp.einsum("kji,jr->kir", qfield, ternary_y, precision=precise)
    partial_x = jnp.einsum("kir,kr->ir", contract_y, ternary_z, precision=precise)
    contract_x = jnp.einsum("kji,ir->kjr", qfield, ternary_x, precision=precise)
    partial_y = jnp.einsum("kjr,kr->jr", contract_x, ternary_z, precision=precise)
    partial_z = jnp.einsum("kjr,jr->kr", contract_x, ternary_y, precision=precise)
    factor_x = lax.psum(partial_x, ("gy", "gz")) / math.sqrt(total_y * total_z)
    summed_y = lax.psum(partial_y, ("gx", "gz"))
    summed_z = lax.psum(partial_z, ("gx", "gy"))
    factor_y = summed_y / math.sqrt(total_x * total_z)
    factor_z = summed_z / math.sqrt(total_x * total_y)
    sketch_x = phi_x.astype(jnp.float32)
    sketch_y = phi_y.astype(jnp.float32)
    sketch_z = phi_z.astype(jnp.float32)
    normalizer = 1.0 / math.sqrt(total_x * total_y * total_z)
    flattened = jnp.einsum("kji,ck->cji", qfield, sketch_z, precision=precise)
    leading = jnp.einsum("cji,ai->acj", flattened, sketch_x, precision=precise)
    core_sketch = lax.psum_scatter(
        jnp.einsum("acj,bj->acb", leading, sketch_y, precision=precise) * normalizer,
        ("gx", "gy", "gz"),
        scatter_dimension=0,
        tiled=True,
    )
    return (factor_x, factor_y, factor_z, core_sketch)


def solution(mesh):
    in_specs = (
        P(None, "gz", "gy", "gx"),
        P(None, None, "gy", "gx"),
        P(None, None, "gy", "gx"),
        P("gx", None),
        P("gy", None),
        P("gz", None),
        P(None, "gx"),
        P(None, "gy"),
        P(None, "gz"),
    )
    out_specs = (P("gx", None), P("gy", None), P("gz", None), P(("gx", "gy", "gz"), None, None))
    return jax.shard_map(shards, mesh=mesh, in_specs=in_specs, out_specs=out_specs, check_vma=False)
```

profile of v0, /device:TPU:16, one launch (start us, length us, event | category | flops | bytes accessed | tf_op | source)
XLA Modules:
  0.0 1196.2 jit_solution(4797968374673610699)
XLA Ops:
  7.2 0.0 all-reduce.7.cloned.1.call-start
  7.2 5.3 fusion.49
  12.5 3.2 copy.49
  15.7 4.8 collective-permute-start.1
  20.5 3.0 copy.48
  23.5 1.9 collective-permute-start
  25.4 0.0 copy-done
  25.5 5.2 collective-permute-start.5
  30.7 1.3 collective-permute-start.4
  32.0 0.0 collective-permute-done.1
  32.0 2.9 copy.24
  34.9 0.0 collective-permute-done
  34.9 2.9 copy.22
  37.9 2.3 pad_maximum_fusion.12
  40.1 8.7 collective-permute-start.3
  48.9 1.9 collective-permute-start.2
  50.8 0.0 copy-done.9
  50.8 0.0 copy-start.4
  50.8 0.0 copy-start.5
  50.9 0.5 collective-permute-done.3
  51.4 5.5 collective-permute-done.2
  56.9 6.7 fusion.16
  63.6 0.0 collective-permute-done.5
  63.6 0.0 copy-done.4
  63.7 0.0 collective-permute-done.4
  63.7 0.0 copy-done.5
  63.8 5.1 fusion.11
  68.8 0.0 copy-start.8
  68.9 0.7 fusion.23
  69.6 0.1 copy-done.8
  69.8 2.0 multiply_reduce_fusion.2
  71.8 0.0 all-reduce.7.cloned.1.call-update
  71.8 0.2 all-reduce.5.cloned.1.call-start
  72.1 1.0 convolution_bitcast_fusion.1
  73.0 0.0 copy-done.3
  73.1 2.5 multiply_reduce_fusion
  75.5 0.0 all-reduce.5.cloned.1.call-update
  75.6 0.0 all-reduce.9.cloned.1.call-start
  75.6 0.5 convolution_bitcast_fusion
  76.1 1.9 convolution_multiply_fusion
  78.0 2.9 copy.29
  80.9 0.0 all-reduce.9.cloned.1.call-update
  81.0 0.1 multiply_reduce_fusion.1
  81.1 1103.5 %psum.23 = f32[16,256]{1,0:T(8,128)S(1)} all-reduce(f32[16,256]{1,0:T(8,128)S(1)} %bitcast.80), channel_id=1, replica_groups=mesh['gx'=16,'gy'=16,'gz'=2] {'gx','gy'}, use_global_device_ids=true, to_apply=%region_2.3 | all-reduce | flops 4096 | bytes 32768 | tf_op jit(solution)/shard_map/psum | solution.py:74
  1184.7 0.6 broadcast_multiply_fusion.2
  1185.3 1.5 broadcast_multiply_fusion.1
  1186.8 1.6 broadcast_multiply_fusion
  1188.4 1.3 constant_dynamic-slice_fusion
  (21 shorter events, 0.2 us)
Async XLA Ops:
  7.2 1178.1 %all-reduce.7.cloned.1.call-start = ((), (), s32[]{:S(2)}) async-start(), calls=%async_computation.1 | async-start | bytes 196608 | tf_op jit(solution)/shard_map/psum | solution.py:73
  12.5 12.9 %copy-start = (f32[3,16,96,128]{3,2,1,0:T(8,128)S(1)}, f32[3,16,96,128]{3,2,1,0:T(8,128)}, u32[]{:S(2)}) copy-start(f32[3,16,96,128]{3,2,1,0:T(8,128)} %param.9) | copy-start | bytes 7077892
  15.7 16.3 %collective-permute-start.1 = (f32[3,16,96,2]{2,1,3,0:T(8,128)}, f32[3,16,96,2]{2,1,3,0:T(8,128)}, u32[]{:S(2)}, u32[]{:S(2)}) collective-permute-start(f32[3,16,96,2]{2,1,3,0:T(8,128)} %copy.49), channel_id=1, source_target_pairs={{32,0},{64,32},{96,64},{128,96},{160,128},{192,160},{224,192},{256... | collective-permute-start | bytes 110600 | tf_op jit(solution)/shard_map/ppermute | solution.py:21
  23.5 11.4 collective-permute-start
  25.5 38.2 %collective-permute-start.5 = (f32[3,2,96,128]{3,2,1,0:T(8,128)S(1)}, f32[3,2,96,128]{3,2,1,0:T(8,128)S(1)}, u32[]{:S(2)}, u32[]{:S(2)}) collective-permute-start(f32[3,2,96,128]{3,2,1,0:T(8,128)S(1)} %get-tuple-element.15), channel_id=1, source_target_pairs={{1,0},{3,2},{5,4},{7,6},{9,8},{11,10},{13,12},{15,14},{17,16},{19,... | collective-permute-start | bytes 884744 | tf_op jit(solution)/shard_map/ppermute | solution.py:21
  30.7 33.0 %collective-permute-start.4 = (f32[3,2,96,128]{3,2,1,0:T(8,128)S(1)}, f32[3,2,96,128]{3,2,1,0:T(8,128)S(1)}, u32[]{:S(2)}, u32[]{:S(2)}) collective-permute-start(f32[3,2,96,128]{3,2,1,0:T(8,128)S(1)} %get-tuple-element.14), channel_id=1, source_target_pairs={{0,1},{2,3},{4,5},{6,7},{8,9},{10,11},{12,13},{14,15},{16,17},{18,... | collective-permute-start | bytes 884744 | tf_op jit(solution)/shard_map/ppermute | solution.py:19
  37.9 13.0 %copy-start.9 = (s32[16,256]{1,0:T(8,128)S(1)}, s32[16,256]{1,0:T(8,128)}, u32[]{:S(2)}) copy-start(s32[16,256]{1,0:T(8,128)} %param.14) | copy-start | bytes 49156
  40.1 11.2 collective-permute-start.3
  48.9 8.0 collective-permute-start.2
  50.8 12.8 %copy-start.4 = (f32[3,2,96,128]{3,2,1,0:T(8,128)S(1)}, f32[3,2,96,128]{3,2,1,0:T(8,128)}, u32[]{:S(2)}) copy-start(f32[3,2,96,128]{3,2,1,0:T(8,128)} %param.11) | copy-start | bytes 884740
  50.8 12.9 %copy-start.5 = (f32[3,2,96,128]{3,2,1,0:T(8,128)S(1)}, f32[3,2,96,128]{3,2,1,0:T(8,128)}, u32[]{:S(2)}) copy-start(f32[3,2,96,128]{3,2,1,0:T(8,128)} %param.10) | copy-start | bytes 884740
  56.9 6.8 copy-start.1
  56.9 6.9 copy-start.2
  68.8 0.9 copy-start.8
  69.8 2.3 copy-start.10
  69.8 3.3 copy-start.3
  69.8 5.9 copy-start.6
  69.8 6.4 copy-start.7
  71.8 1115.0 %all-reduce.5.cloned.1.call-start = ((), (), s32[]{:S(2)}) async-start(), calls=%async_computation | async-start | bytes 262144 | tf_op jit(solution)/shard_map/psum | solution.py:72
  75.6 1112.8 %all-reduce.9.cloned.1.call-start = ((), (), s32[]{:S(2)}) async-start(), calls=%async_computation.2 | async-start | bytes 4194304
Sparse Core Ops, SparseCore 0:
  71.9 122.9 all-reduce.6
  198.7 301.0 all-reduce.4
  505.1 471.9 all-reduce.8
where the time goes:
time: 1200 us
  blocking collectives  1100 us (92%)
  starting transfers between devices  24.2 us (2%)
  local copies, waits for them, and re-layouts  21.7 us (2%)
  other arithmetic  18.7 us (2%)
  between operations  14 us (1%)
    psum x1, blocking collectives, shards(): summed_z = lax.psum(partial_z, ('gx', 'gy'))  1100 us
  transfers between devices with their start and end apart: 9, of which 2 were waited for; matrix products, arithmetic and copies ran while one was open for 3% of the time, Pallas kernels for 0%

commit v1 on v0

v1 whole, which is shorter than its diff:
```python
import math

import jax
import jax.numpy as jnp
from jax import lax
from jax.sharding import PartitionSpec as P


def shift_permute(cells, axis, step):
    count = lax.axis_size(axis)
    return lax.ppermute(cells, axis, [(i, (i + step) % count) for i in range(count)])


def extended(cells, axis, dim):
    length = cells.shape[dim]
    head = lax.slice_in_dim(cells, 0, 2, axis=dim)
    tail = lax.slice_in_dim(cells, length - 2, length, axis=dim)
    before = shift_permute(tail, axis, 1)
    after = shift_permute(head, axis, -1)
    return jnp.concatenate([before, cells, after], axis=dim)


def derivative(padded, direction):
    length = padded.shape[direction] - 4

    def window(offset):
        return lax.slice_in_dim(padded, offset, offset + length, axis=direction)

    return (window(0) - window(4)) + 8.0 * (window(3) - window(1))


def split(values):
    high = lax.reduce_precision(values, 8, 7)
    return high.astype(jnp.bfloat16), (values - high).astype(jnp.bfloat16)


def contract(spec, values, ternary):
    high, low = split(values)
    return jnp.einsum(spec, high, ternary, preferred_element_type=jnp.float32) + jnp.einsum(
        spec, low, ternary, preferred_element_type=jnp.float32
    )


def exchange(rows, axes):
    return lax.all_to_all(rows, axes, 0, 0, tiled=True)


def shards(velocity, below, above, omega_x, omega_y, omega_z, phi_x, phi_y, phi_z):
    total_x = 2048
    total_y = 1536
    total_z = 32
    gz = lax.axis_index("gz")
    near = jnp.where(gz == 0, velocity[:, 14:16], velocity[:, 0:2])
    far = shift_permute(near, "gz", 1)
    lower = jnp.where(gz == 0, below, far)
    upper = jnp.where(gz == 1, above, far)
    planes = jnp.concatenate([lower, velocity, upper], axis=1)
    grad = [
        derivative(extended(velocity, "gx", 3), 3),
        derivative(extended(velocity, "gy", 2), 2),
        derivative(planes, 1),
    ]
    diagonal = grad[0][0] * grad[0][0] + grad[1][1] * grad[1][1] + grad[2][2] * grad[2][2]
    mixed = grad[0][1] * grad[1][0] + grad[0][2] * grad[2][0] + grad[1][2] * grad[2][1]
    qfield = (-0.5 / 144.0) * (diagonal + 2.0 * mixed)

    wx = omega_x.astype(jnp.bfloat16)
    wy = omega_y.astype(jnp.bfloat16)
    wz = omega_z.astype(jnp.float32)
    contract_x = contract("kji,ir->kjr", qfield, wx)
    partial_y = jnp.sum(contract_x * wz[:, None, :], axis=0)
    partial_z = jnp.sum(contract_x * omega_y.astype(jnp.float32)[None], axis=1)
    flattened = jnp.einsum("kji,ck->cji", qfield, phi_z.astype(jnp.float32), precision=lax.Precision.HIGHEST)
    leading = contract("cji,ai->acj", flattened, phi_x.astype(jnp.bfloat16))
    leading = leading.reshape(16, 16, 2, 192).transpose(0, 2, 1, 3).reshape(32, 24, 128)
    factor_z_rows = jnp.broadcast_to(partial_z.reshape(16, 1, 2, 128), (16, 2, 2, 128)).reshape(32, 2, 128)
    send = jnp.concatenate([leading, partial_y.reshape(32, 6, 128), factor_z_rows], axis=1)
    got = exchange(send.reshape(1024, 128), ("gx", "gz")).reshape(16, 2, 32, 128)

    contract_y = contract("kji,jr->kir", qfield, wy)
    partial_x = jnp.sum(contract_y * wz[:, None, :], axis=0)

    summed = jnp.sum(got, axis=(0, 1))
    summed_z = jnp.sum(lax.dynamic_index_in_dim(got, gz, 1, keepdims=False)[:, 30:], axis=0)
    lead = summed[:24].reshape(16, 2, 96)
    core = contract("hcj,bj->hcb", lead, phi_y.astype(jnp.bfloat16)).reshape(16, 8, 128)
    send = jnp.concatenate(
        [core, partial_x.reshape(16, 16, 128), jnp.broadcast_to(summed_z[None], (16, 2, 128))], axis=1
    )
    got = jnp.sum(exchange(send.reshape(416, 128), "gy").reshape(16, 26, 128), axis=0)
    core_sketch = got[:8].reshape(1, 2, 512) * (1.0 / math.sqrt(total_x * total_y * total_z))
    other = shift_permute(got[8:24], "gz", 1)

    rows = jnp.concatenate([summed[24:30], got[24:26]], axis=0)
    got_y = exchange(jnp.broadcast_to(rows[None], (32, 8, 128)).reshape(256, 128), ("gx", "gz"))
    got_y = got_y.reshape(16, 2, 8, 128)
    factor_y = got_y[:, :, :6].reshape(96, 256) * (1.0 / math.sqrt(total_x * total_z))
    factor_z = lax.dynamic_index_in_dim(got_y, gz, 1, keepdims=False)[:, 6:].reshape(16, 256)
    factor_z = factor_z * (1.0 / math.sqrt(total_x * total_y))

    rows = got[8:24] + other
    got_x = exchange(jnp.broadcast_to(rows[None], (16, 16, 128)).reshape(256, 128), "gy")
    factor_x = got_x.reshape(128, 256) * (1.0 / math.sqrt(total_y * total_z))
    return (factor_x, factor_y, factor_z, core_sketch)


def solution(mesh):
    in_specs = (
        P(None, "gz", "gy", "gx"),
        P(None, None, "gy", "gx"),
        P(None, None, "gy", "gx"),
        P("gx", None),
        P("gy", None),
        P("gz", None),
        P(None, "gx"),
        P(None, "gy"),
        P(None, "gz"),
    )
    out_specs = (P("gx", None), P("gy", None), P("gz", None), P(("gx", "gy", "gz"), None, None))
    return jax.shard_map(shards, mesh=mesh, in_specs=in_specs, out_specs=out_specs, check_vma=False)
```

time: 1200 us -> 142 us (0.12)
  the two profiles are of different devices: /device:TPU:16 before, /device:TPU:1 now
where the time goes in v1:
time: 142 us; the launch traced here: 139 us
  starting transfers between devices  57.7 us (41%)
  waiting for transfers between devices  41.5 us (29%)
  local copies, waits for them, and re-layouts  24.4 us (17%)
  other arithmetic  11.1 us (8%)
  matrix products  3.47 us (2%)
    all_to_all x4, waiting for transfers between devices, exchange(): return lax.all_to_all(rows, axes, 0, 0, tiled=True)  41.5 us
    all_to_all x4, starting transfers between devices, exchange(): return lax.all_to_all(rows, axes, 0, 0, tiled=True)  31.7 us
    ppermute x6, starting transfers between devices, shift_permute(): lax.ppermute(cells, axis, [(i, (i + step) % count) for i in range(count)])  25.9 us
    unnamed x25, local copies, waits for them, and re-layouts  7.67 us
    ppermute x2, local copies, waits for them, and re-layouts, shift_permute(): lax.ppermute(cells, axis, [(i, (i + step) % count) for i in range(count)])  5.92 us
    slice x1, local copies, waits for them, and re-layouts, extended(): tail = lax.slice_in_dim(cells, length - 2, length, axis=dim)  5.28 us
    add x1, other arithmetic, derivative(): return window(0) - window(4) + 8.0 * (window(3) - window(1))  5.25 us
  transfers between devices with their start and end apart: 10, of which 4 were waited for; matrix products, arithmetic and copies ran while one was open for 17% of the time, Pallas kernels for 0%

profile of v1, /device:TPU:1, one launch (start us, length us, event | category | flops | bytes accessed | tf_op | source)
XLA Modules:
  0.0 139.2 jit_solution(3545860009258118553)
XLA Ops:
  0.6 1.8 %slice_select_fusion = f32[3,2,96,128]{3,2,1,0:T(8,128)} fusion(f32[3,16,96,128]{3,2,1,0:T(8,128)} %param.9, pred[]{:T(512)S(6)} %eq.7), kind=kLoop, calls=%fused_computation.59 | loop fusion | flops 73728 | bytes 884737 | tf_op jit(solution)/shard_map/jit(_where)/select_n | solution.py:53
  2.5 5.6 %collective-permute-start.4 = (f32[3,2,96,128]{3,2,1,0:T(8,128)}, f32[3,2,96,128]{3,2,1,0:T(8,128)S(1)}, u32[]{:S(2)}, u32[]{:S(2)}) collective-permute-start(f32[3,2,96,128]{3,2,1,0:T(8,128)} %slice_select_fusion), channel_id=1, source_target_pairs={{0,1},{1,0},{2,3},{3,2},{4,5},{5,4},{6,7},{7,6},{8,9},{9,8},{10,11... | collective-permute-start | bytes 884744 | tf_op jit(solution)/shard_map/ppermute | solution.py:11
  8.1 5.3 %fusion.57 = (f32[3,16,96,2]{3,2,1,0:T(8,128)}, f32[3,16,96,2]{3,2,1,0:T(8,128)}) fusion(f32[3,16,96,128]{3,2,1,0:T(8,128)} %param.9), kind=kLoop, calls=%fused_computation.103 | loop fusion | bytes 147456 | tf_op jit(solution)/shard_map/slice | solution.py:17
  13.4 3.2 %copy.75 = f32[3,16,96,2]{2,1,3,0:T(8,128)} copy(f32[3,16,96,2]{3,2,1,0:T(8,128)} %get-tuple-element.8) | data formatting | bytes 73728
  16.5 3.1 %collective-permute-start = (f32[3,16,96,2]{2,1,3,0:T(8,128)}, f32[3,16,96,2]{2,1,3,0:T(8,128)}, u32[]{:S(2)}, u32[]{:S(2)}) collective-permute-start(f32[3,16,96,2]{2,1,3,0:T(8,128)} %copy.75), channel_id=1, source_target_pairs={{0,32},{32,64},{64,96},{96,128},{128,160},{160,192},{192,224},{224... | collective-permute-start | bytes 110600 | tf_op jit(solution)/shard_map/ppermute | solution.py:11
  19.7 3.0 %copy.76 = f32[3,16,96,2]{2,1,3,0:T(8,128)} copy(f32[3,16,96,2]{3,2,1,0:T(8,128)} %get-tuple-element.9) | data formatting | bytes 73728
  22.7 3.8 %collective-permute-start.1 = (f32[3,16,96,2]{2,1,3,0:T(8,128)}, f32[3,16,96,2]{2,1,3,0:T(8,128)}, u32[]{:S(2)}, u32[]{:S(2)}) collective-permute-start(f32[3,16,96,2]{2,1,3,0:T(8,128)} %copy.76), channel_id=1, source_target_pairs={{0,480},{32,0},{64,32},{96,64},{128,96},{160,128},{192,160},{224,1... | collective-permute-start | bytes 110600 | tf_op jit(solution)/shard_map/ppermute | solution.py:11
  26.5 0.7 fusion.58
  27.2 9.2 %collective-permute-start.3 = (f32[3,16,2,128]{3,2,1,0:T(2,128)}, f32[3,16,2,128]{3,2,1,0:T(2,128)S(1)}, u32[]{:S(2)}, u32[]{:S(2)}) collective-permute-start(f32[3,16,2,128]{3,2,1,0:T(2,128)} %get-tuple-element.10), channel_id=1, source_target_pairs={{0,30},{2,0},{4,2},{6,4},{8,6},{10,8},{12,10},{14,12},{16,14},{18,... | collective-permute-start | bytes 147464 | tf_op jit(solution)/shard_map/ppermute | solution.py:11
  36.4 1.9 %collective-permute-start.2 = (f32[3,16,2,128]{3,2,1,0:T(2,128)}, f32[3,16,2,128]{3,2,1,0:T(2,128)S(1)}, u32[]{:S(2)}, u32[]{:S(2)}) collective-permute-start(f32[3,16,2,128]{3,2,1,0:T(2,128)} %get-tuple-element.11), channel_id=1, source_target_pairs={{0,2},{2,4},{4,6},{6,8},{8,10},{10,12},{12,14},{14,16},{16,18},{18... | collective-permute-start | bytes 147464 | tf_op jit(solution)/shard_map/ppermute | solution.py:11
  38.4 3.0 %copy.63 = f32[3,16,96,2]{3,2,1,0:T(8,128)} copy(f32[3,16,96,2]{2,1,3,0:T(8,128)} %collective-permute-done) | data formatting | bytes 73728 | tf_op jit(solution)/shard_map/ppermute | solution.py:11
  41.4 2.9 %copy.65 = f32[3,16,96,2]{3,2,1,0:T(8,128)} copy(f32[3,16,96,2]{2,1,3,0:T(8,128)} %collective-permute-done.1) | data formatting | bytes 73728 | tf_op jit(solution)/shard_map/ppermute | solution.py:11
  44.4 1.4 %constant_dynamic-update-slice_fusion.1 = (f32[3,16,98,128]{3,2,1,0:T(8,128)S(1)}, f32[3,16,96,128]{3,2,1,0:T(8,128)S(1)}) fusion(f32[3,16,96,128]{3,2,1,0:T(8,128)S(1)} %copy-done, f32[3,2,96,128]{3,2,1,0:T(8,128)S(1)} %get-tuple-element.14, f32[3,2,96,128]{3,2,1,0:T(8,128)S(1)} %get-tuple-element.15), kind=kLoop, calls=%fused_computation.97 | loop fusion | flops 4718591 | bytes 7667712
  45.9 0.1 copy-done.1
  46.1 0.7 copy-done.2
  46.8 5.2 %fusion.9 = (f32[3,16,96,128]{3,2,1,0:T(8,128)S(1)}, f32[3,16,96,128]{3,2,1,0:T(8,128)S(1)}) fusion(f32[3,16,96,128]{3,2,1,0:T(8,128)S(1)} %copy-done, f32[3,16,96,2]{3,2,1,0:T(8,128)S(1)} %copy-done.2, f32[3,16,96,2]{3,2,1,0:T(8,128)S(1)} %copy-done.1, f32[3,16,2,128]{3,2,1,0:T(2,128)S(1)} %collective-permute-done.2, ...), kind=kLoop, calls=%fused_computation.19 | loop fusion | flops 8257536 | bytes 11919360 | tf_op jit(solution)/shard_map/add | solution.py:29
  52.1 0.7 fusion.23
  52.8 1.0 fusion.27
  53.8 0.2 fusion.32
  54.1 0.2 fusion.17
  54.3 0.2 copy.68
  54.5 0.7 reshape.99
  55.3 0.3 reshape.100
  55.6 0.3 fusion.30
  55.9 0.5 multiply_reduce_fusion.2
  56.5 0.9 pad_maximum_fusion.5
  57.3 7.4 %all-to-all-start = ((f32[32,32,128]{2,1,0:T(8,128)}), f32[32,32,128]{2,1,0:T(8,128)S(1)}, u32[]{:S(2)}, u32[]{:S(2)}) async-start(f32[32,32,128]{2,1,0:T(8,128)} %pad_maximum_fusion.5), calls=%async_computation | async-start | bytes 1048576 | tf_op jit(solution)/shard_map/all_to_all | solution.py:45
  64.7 0.5 fusion.29
  65.2 0.5 multiply_reduce_fusion
  65.7 10.8 %all-to-all-done = f32[32,32,128]{2,1,0:T(8,128)S(1)} async-done(((f32[32,32,128]{2,1,0:T(8,128)}), f32[32,32,128]{2,1,0:T(8,128)S(1)}, u32[]{:S(2)}, u32[]{:S(2)}) %all-to-all-start) | async-done | bytes 524320 | tf_op jit(solution)/shard_map/all_to_all | solution.py:45
  76.6 0.1 reshape.103
  76.7 0.1 fusion.38
  76.8 0.1 convolution_add_fusion.2
  76.9 0.1 copy.72
  77.1 0.7 pad_maximum_fusion.6
  77.9 7.4 %all-to-all-start.1 = ((f32[16,26,128]{2,1,0:T(8,128)}), f32[16,26,128]{2,1,0:T(8,128)S(1)}, u32[]{:S(2)}, u32[]{:S(2)}) async-start(f32[16,26,128]{2,1,0:T(8,128)} %pad_maximum_fusion.6), calls=%async_computation.1 | async-start | bytes 524288 | tf_op jit(solution)/shard_map/all_to_all | solution.py:45
  85.3 13.0 %all-to-all-done.1 = f32[16,26,128]{2,1,0:T(8,128)S(1)} async-done(((f32[16,26,128]{2,1,0:T(8,128)}), f32[16,26,128]{2,1,0:T(8,128)S(1)}, u32[]{:S(2)}, u32[]{:S(2)}) %all-to-all-start.1) | async-done | bytes 213024 | tf_op jit(solution)/shard_map/all_to_all | solution.py:45
  98.4 2.2 %collective-permute-start.5 = (f32[16,128]{1,0:T(8,128)S(1)}, f32[16,128]{1,0:T(8,128)S(1)}, u32[]{:S(2)}, u32[]{:S(2)}) collective-permute-start(f32[16,128]{1,0:T(8,128)S(1)} %slice.179), channel_id=1, source_target_pairs={{0,1},{1,0},{2,3},{3,2},{4,5},{5,4},{6,7},{7,6},{8,9},{9,8},{10,11... | collective-permute-start | bytes 24584 | tf_op jit(solution)/shard_map/ppermute | solution.py:11
  100.6 0.7 broadcast_in_dim.14
  101.3 11.3 %all-to-all-start.3 = ((f32[32,8,128]{2,1,0:T(8,128)}), f32[32,8,128]{2,1,0:T(8,128)S(1)}, u32[]{:S(2)}, u32[]{:S(2)}) async-start(f32[32,8,128]{2,1,0:T(8,128)} %broadcast_in_dim.14), calls=%async_computation.3 | async-start | bytes 262144 | tf_op jit(solution)/shard_map/all_to_all | solution.py:45
  112.6 0.6 mul.147
  113.2 7.0 %all-to-all-done.3 = f32[32,8,128]{2,1,0:T(8,128)S(1)} async-done(((f32[32,8,128]{2,1,0:T(8,128)}), f32[32,8,128]{2,1,0:T(8,128)S(1)}, u32[]{:S(2)}, u32[]{:S(2)}) %all-to-all-start.3) | async-done | bytes 131104 | tf_op jit(solution)/shard_map/all_to_all | solution.py:45
  120.2 0.7 broadcast_in_dim.13
  120.9 5.6 %all-to-all-start.2 = ((f32[16,16,128]{2,1,0:T(8,128)}), f32[16,16,128]{2,1,0:T(8,128)S(1)}, u32[]{:S(2)}, u32[]{:S(2)}) async-start(f32[16,16,128]{2,1,0:T(8,128)} %broadcast_in_dim.13), calls=%async_computation.2 | async-start | bytes 262144 | tf_op jit(solution)/shard_map/all_to_all | solution.py:45
  126.5 0.7 mul.141
  127.2 0.6 copy.92
  127.9 10.7 %all-to-all-done.2 = f32[16,16,128]{2,1,0:T(8,128)S(1)} async-done(((f32[16,16,128]{2,1,0:T(8,128)}), f32[16,16,128]{2,1,0:T(8,128)S(1)}, u32[]{:S(2)}, u32[]{:S(2)}) %all-to-all-start.2) | async-done | bytes 131104 | tf_op jit(solution)/shard_map/all_to_all | solution.py:45
  138.6 0.7 mul.138
  (52 shorter events, 0.5 us)
Async XLA Ops:
  2.5 41.9 %collective-permute-start.4 = (f32[3,2,96,128]{3,2,1,0:T(8,128)}, f32[3,2,96,128]{3,2,1,0:T(8,128)S(1)}, u32[]{:S(2)}, u32[]{:S(2)}) collective-permute-start(f32[3,2,96,128]{3,2,1,0:T(8,128)} %slice_select_fusion), channel_id=1, source_target_pairs={{0,1},{1,0},{2,3},{3,2},{4,5},{5,4},{6,7},{7,6},{8,9},{9,8},{10,11... | collective-permute-start | bytes 884744 | tf_op jit(solution)/shard_map/ppermute | solution.py:11
  13.4 13.1 %copy-start = (f32[3,16,96,128]{3,2,1,0:T(8,128)S(1)}, f32[3,16,96,128]{3,2,1,0:T(8,128)}, u32[]{:S(2)}) copy-start(f32[3,16,96,128]{3,2,1,0:T(8,128)} %param.9) | copy-start | bytes 7077892
  13.4 25.0 %copy-start.9 = (s32[16,256]{1,0:T(8,128)S(1)}, s32[16,256]{1,0:T(8,128)}, u32[]{:S(2)}) copy-start(s32[16,256]{1,0:T(8,128)} %param.14) | copy-start | bytes 49156
  13.4 25.0 %copy-start.4 = (s32[96,256]{1,0:T(8,128)S(1)}, s32[96,256]{1,0:T(8,128)}, u32[]{:S(2)}) copy-start(s32[96,256]{1,0:T(8,128)} %param.13) | copy-start | bytes 294916
  16.5 21.9 %collective-permute-start = (f32[3,16,96,2]{2,1,3,0:T(8,128)}, f32[3,16,96,2]{2,1,3,0:T(8,128)}, u32[]{:S(2)}, u32[]{:S(2)}) collective-permute-start(f32[3,16,96,2]{2,1,3,0:T(8,128)} %copy.75), channel_id=1, source_target_pairs={{0,32},{32,64},{64,96},{96,128},{128,160},{160,192},{192,224},{224... | collective-permute-start | bytes 110600 | tf_op jit(solution)/shard_map/ppermute | solution.py:11
  22.7 18.7 %collective-permute-start.1 = (f32[3,16,96,2]{2,1,3,0:T(8,128)}, f32[3,16,96,2]{2,1,3,0:T(8,128)}, u32[]{:S(2)}, u32[]{:S(2)}) collective-permute-start(f32[3,16,96,2]{2,1,3,0:T(8,128)} %copy.76), channel_id=1, source_target_pairs={{0,480},{32,0},{64,32},{96,64},{128,96},{160,128},{192,160},{224,1... | collective-permute-start | bytes 110600 | tf_op jit(solution)/shard_map/ppermute | solution.py:11
  27.2 18.7 %collective-permute-start.3 = (f32[3,16,2,128]{3,2,1,0:T(2,128)}, f32[3,16,2,128]{3,2,1,0:T(2,128)S(1)}, u32[]{:S(2)}, u32[]{:S(2)}) collective-permute-start(f32[3,16,2,128]{3,2,1,0:T(2,128)} %get-tuple-element.10), channel_id=1, source_target_pairs={{0,30},{2,0},{4,2},{6,4},{8,6},{10,8},{12,10},{14,12},{16,14},{18,... | collective-permute-start | bytes 147464 | tf_op jit(solution)/shard_map/ppermute | solution.py:11
  36.4 9.5 %collective-permute-start.2 = (f32[3,16,2,128]{3,2,1,0:T(2,128)}, f32[3,16,2,128]{3,2,1,0:T(2,128)S(1)}, u32[]{:S(2)}, u32[]{:S(2)}) collective-permute-start(f32[3,16,2,128]{3,2,1,0:T(2,128)} %get-tuple-element.11), channel_id=1, source_target_pairs={{0,2},{2,4},{4,6},{6,8},{8,10},{10,12},{12,14},{14,16},{16,18},{18... | collective-permute-start | bytes 147464 | tf_op jit(solution)/shard_map/ppermute | solution.py:11
  38.4 6.0 %copy-start.7 = (f32[3,2,96,128]{3,2,1,0:T(8,128)S(1)}, f32[3,2,96,128]{3,2,1,0:T(8,128)}, u32[]{:S(2)}) copy-start(f32[3,2,96,128]{3,2,1,0:T(8,128)} %param.10) | copy-start | bytes 884740
  38.4 6.0 %copy-start.8 = (f32[3,2,96,128]{3,2,1,0:T(8,128)S(1)}, f32[3,2,96,128]{3,2,1,0:T(8,128)}, u32[]{:S(2)}) copy-start(f32[3,2,96,128]{3,2,1,0:T(8,128)} %param.11) | copy-start | bytes 884740
  44.4 1.7 %copy-start.1 = (f32[3,16,96,2]{3,2,1,0:T(8,128)S(1)}, f32[3,16,96,2]{3,2,1,0:T(8,128)}, u32[]{:S(2)}) copy-start(f32[3,16,96,2]{3,2,1,0:T(8,128)} %copy.63) | copy-start | bytes 110596
  44.4 2.4 %copy-start.2 = (f32[3,16,96,2]{3,2,1,0:T(8,128)S(1)}, f32[3,16,96,2]{3,2,1,0:T(8,128)}, u32[]{:S(2)}) copy-start(f32[3,16,96,2]{3,2,1,0:T(8,128)} %copy.65) | copy-start | bytes 110596
  52.1 0.8 copy-start.10
  52.1 1.8 %copy-start.3 = (s32[512,128]{1,0:T(8,128)S(1)}, s32[512,128]{1,0:T(8,128)}, u32[]{:S(2)}) copy-start(s32[512,128]{1,0:T(8,128)} %param.15) | copy-start | bytes 786436
  54.1 1.5 %copy-start.6 = (s32[128,256]{1,0:T(8,128)S(1)}, s32[128,256]{1,0:T(8,128)}, u32[]{:S(2)}) copy-start(s32[128,256]{1,0:T(8,128)} %param.12) | copy-start | bytes 393220
  57.3 19.2 %all-to-all-start = ((f32[32,32,128]{2,1,0:T(8,128)}), f32[32,32,128]{2,1,0:T(8,128)S(1)}, u32[]{:S(2)}, u32[]{:S(2)}) async-start(f32[32,32,128]{2,1,0:T(8,128)} %pad_maximum_fusion.5), calls=%async_computation | async-start | bytes 1048576 | tf_op jit(solution)/shard_map/all_to_all | solution.py:45
  65.2 11.5 %copy-start.5 = (s32[512,96]{0,1:T(8,128)S(1)}, s32[512,96]{0,1:T(8,128)}, u32[]{:S(2)}) copy-start(s32[512,96]{0,1:T(8,128)} %param.16) | copy-start | bytes 589828
  77.9 20.5 %all-to-all-start.1 = ((f32[16,26,128]{2,1,0:T(8,128)}), f32[16,26,128]{2,1,0:T(8,128)S(1)}, u32[]{:S(2)}, u32[]{:S(2)}) async-start(f32[16,26,128]{2,1,0:T(8,128)} %pad_maximum_fusion.6), calls=%async_computation.1 | async-start | bytes 524288 | tf_op jit(solution)/shard_map/all_to_all | solution.py:45
  98.4 14.8 %collective-permute-start.5 = (f32[16,128]{1,0:T(8,128)S(1)}, f32[16,128]{1,0:T(8,128)S(1)}, u32[]{:S(2)}, u32[]{:S(2)}) collective-permute-start(f32[16,128]{1,0:T(8,128)S(1)} %slice.179), channel_id=1, source_target_pairs={{0,1},{1,0},{2,3},{3,2},{4,5},{5,4},{6,7},{7,6},{8,9},{9,8},{10,11... | collective-permute-start | bytes 24584 | tf_op jit(solution)/shard_map/ppermute | solution.py:11
  101.3 19.0 %all-to-all-start.3 = ((f32[32,8,128]{2,1,0:T(8,128)}), f32[32,8,128]{2,1,0:T(8,128)S(1)}, u32[]{:S(2)}, u32[]{:S(2)}) async-start(f32[32,8,128]{2,1,0:T(8,128)} %broadcast_in_dim.14), calls=%async_computation.3 | async-start | bytes 262144 | tf_op jit(solution)/shard_map/all_to_all | solution.py:45
  120.9 17.6 %all-to-all-start.2 = ((f32[16,16,128]{2,1,0:T(8,128)}), f32[16,16,128]{2,1,0:T(8,128)S(1)}, u32[]{:S(2)}, u32[]{:S(2)}) async-start(f32[16,16,128]{2,1,0:T(8,128)} %broadcast_in_dim.13), calls=%async_computation.2 | async-start | bytes 262144 | tf_op jit(solution)/shard_map/all_to_all | solution.py:45

commit v2 on v1

v2 whole, which is shorter than its diff:
```python
import math

import jax
import jax.numpy as jnp
from jax import lax
from jax.experimental import pallas as pl
from jax.experimental.pallas import tpu as pltpu
from jax.sharding import PartitionSpec as P


def shift_permute(cells, axis, step):
    count = lax.axis_size(axis)
    return lax.ppermute(cells, axis, [(i, (i + step) % count) for i in range(count)])


def pack_kernel(vel, near, x_high, x_low, y_high, y_low):
    component = pl.program_id(0)
    gz = lax.axis_index("gz")
    lane = lax.broadcasted_iota(jnp.int32, (96, 128), 1)
    near[0] = vel[0, pl.ds(14 * (1 - gz), 2)]

    @pl.when(component == 0)
    def _():
        x_high[...] = jnp.zeros((96, 128), jnp.float32)
        x_low[...] = jnp.zeros((96, 128), jnp.float32)

    high = x_high[...]
    low = x_low[...]
    for k in range(16):
        spot = 2 * (16 * component + k)
        cells = vel[0, k]
        turned = pltpu.roll(cells, spot + 2, 1)
        high = jnp.where((lane >= spot) & (lane < spot + 2), turned, high)
        low = jnp.where((lane >= spot + 2) & (lane < spot + 4), turned, low)
        y_low[0, 2 * k : 2 * k + 2, :] = vel[0, k, 0:2, :]
        y_high[0, 2 * k : 2 * k + 2, :] = vel[0, k, 94:96, :]
    x_high[...] = high
    x_low[...] = low


def pack(velocity):
    rims = jax.ShapeDtypeStruct((96, 128), jnp.float32)
    rows = jax.ShapeDtypeStruct((3, 32, 128), jnp.float32)
    return pl.pallas_call(
        pack_kernel,
        grid=(3,),
        in_specs=[pl.BlockSpec((1, 16, 96, 128), lambda c: (c, 0, 0, 0))],
        out_specs=[
            pl.BlockSpec((1, 2, 96, 128), lambda c: (c, 0, 0, 0)),
            pl.BlockSpec((96, 128), lambda c: (0, 0)),
            pl.BlockSpec((96, 128), lambda c: (0, 0)),
            pl.BlockSpec((1, 32, 128), lambda c: (c, 0, 0)),
            pl.BlockSpec((1, 32, 128), lambda c: (c, 0, 0)),
        ],
        out_shape=[jax.ShapeDtypeStruct((3, 2, 96, 128), jnp.float32), rims, rims, rows, rows],
        name="pack_halos",
    )(velocity)


def field_kernel(
    phi_z, vel, far, below, above, x_left, x_right, y_before, y_after, wx, wy, wz, wyz, phx,
    send, part_x, padded, q_terms, flat, flat_terms, part_y, part_z, lead, sems,
):
    gz = lax.axis_index("gz")
    copies = [
        pltpu.make_async_copy(vel.at[c], padded.at[c, pl.ds(2, 16), pl.ds(8, 96), :], sems.at[c]) for c in range(3)
    ]
    for copy in copies:
        copy.start()

    def rims(lower, upper):
        pair = [
            pltpu.make_async_copy(lower, padded.at[:, pl.ds(0, 2), pl.ds(8, 96), :], sems.at[3]),
            pltpu.make_async_copy(upper, padded.at[:, pl.ds(18, 2), pl.ds(8, 96), :], sems.at[4]),
        ]
        for copy in pair:
            copy.start()
        for copy in pair:
            copy.wait()

    @pl.when(gz == 0)
    def _():
        rims(below, far)

    @pl.when(gz == 1)
    def _():
        rims(far, above)

    for copy in copies:
        copy.wait()
    for c in range(3):
        for k in range(16):
            padded[c, k + 2, 6:8, :] = y_before[c, 2 * k : 2 * k + 2, :]
            padded[c, k + 2, 104:106, :] = y_after[c, 2 * k : 2 * k + 2, :]
    flat[...] = jnp.zeros((256, 128), jnp.float32)
    part_y[...] = jnp.zeros((96, 256), jnp.float32)
    lane = lax.broadcasted_iota(jnp.int32, (16, 128), 1)

    def plane(k, carry):
        weight = [phi_z[c, k].astype(jnp.float32) for c in range(2)]
        for block in range(6):
            row = 16 * block
            at = row + 8
            along = [[], [], []]
            for c in range(3):
                spot = 2 * (16 * c + k)
                cells = padded[c, k + 2, at : at + 16, :]
                sides = jnp.where(lane < spot + 2, x_left[row : row + 16, :], x_right[row : row + 16, :])
                sides = pltpu.roll(sides, 126 - spot, 1)
                outer = pltpu.roll(jnp.where(lane >= 126, sides, cells), 2, 1) - pltpu.roll(
                    jnp.where(lane < 2, sides, cells), 126, 1
                )
                inner = pltpu.roll(jnp.where(lane < 1, sides, cells), 127, 1) - pltpu.roll(
                    jnp.where(lane >= 127, sides, cells), 1, 1
                )
                along[0].append(outer + 8.0 * inner)
                outer = padded[c, k + 2, at - 2 : at + 14, :] - padded[c, k + 2, at + 2 : at + 18, :]
                inner = padded[c, k + 2, at + 1 : at + 17, :] - padded[c, k + 2, at - 1 : at + 15, :]
                along[1].append(outer + 8.0 * inner)
                outer = padded[c, k, at : at + 16, :] - padded[c, k + 4, at : at + 16, :]
                inner = padded[c, k + 3, at : at + 16, :] - padded[c, k + 1, at : at + 16, :]
                along[2].append(outer + 8.0 * inner)
            diagonal = along[0][0] * along[0][0] + along[1][1] * along[1][1] + along[2][2] * along[2][2]
            mixed = along[0][1] * along[1][0] + along[0][2] * along[2][0] + along[1][2] * along[2][1]
            field = (-0.5 / 144.0) * (diagonal + 2.0 * mixed)
            high = field.astype(jnp.bfloat16)
            low = (field - high.astype(jnp.float32)).astype(jnp.bfloat16)
            place = pl.ds(pl.multiple_of(96 * k + row, 16), 16)
            q_terms[place, 0:128] = high
            q_terms[place, 128:256] = low
            for c in range(2):
                flat[96 * c + row : 96 * c + row + 16, :] += weight[c] * field
        return carry

    lax.fori_loop(0, 16, plane, 0)

    flat_high = flat[...].astype(jnp.bfloat16)
    flat_terms[:, 0:128] = flat_high
    flat_terms[:, 128:256] = (flat[...] - flat_high.astype(jnp.float32)).astype(jnp.bfloat16)
    lead[...] = lax.dot_general(
        phx[...], flat_terms[...], (((1,), (1,)), ((), ())), preferred_element_type=jnp.float32
    )
    lane8 = lax.broadcasted_iota(jnp.int32, (8, 128), 1)

    def products(k, carry):
        place = pl.ds(pl.multiple_of(96 * k, 96), 96)
        sums = jnp.dot(q_terms[place, :], wx[...], preferred_element_type=jnp.float32)
        part_y[...] += sums * wz[pl.ds(k, 1), :]
        part_z[pl.ds(k, 1), :] = jnp.sum(sums * wy[...], axis=0, keepdims=True)
        return carry

    lax.fori_loop(0, 16, products, 0)

    for chunk in range(32):
        base = 32 * chunk
        send[base : base + 16, :] = lead[16 * chunk : 16 * chunk + 16, 0:128]
        send[base + 16 : base + 24, :] = jnp.where(
            lane8 < 64,
            lead[16 * chunk : 16 * chunk + 8, 128:256],
            pltpu.roll(lead[16 * chunk + 8 : 16 * chunk + 16, 128:256], 64, 1),
        )
        for half in range(2):
            lanes = slice(128 * half, 128 * half + 128)
            send[base + 24 + 3 * half : base + 27 + 3 * half, :] = part_y[3 * chunk : 3 * chunk + 3, lanes]
            send[base + 30 + half : base + 31 + half, :] = part_z[chunk // 2 : chunk // 2 + 1, lanes]

    turned = jnp.dot(wyz[...], q_terms[...], preferred_element_type=jnp.float32)
    turned = turned[:, 0:128] + turned[:, 128:256]
    part_x[0] = turned[0:128, :].T
    part_x[1] = turned[128:256, :].T


def field(phi_z, velocity, far, below, above, sides, wx, wy, wz, wyz, phx):
    whole = pl.BlockSpec(memory_space=pltpu.VMEM)
    outside = pl.BlockSpec(memory_space=pl.ANY)
    return pl.pallas_call(
        field_kernel,
        in_specs=[pl.BlockSpec(memory_space=pltpu.SMEM)] + [outside] * 4 + [whole] * 9,
        out_specs=[whole] * 2,
        out_shape=[
            jax.ShapeDtypeStruct((1024, 128), jnp.float32),
            jax.ShapeDtypeStruct((2, 128, 128), jnp.float32),
        ],
        scratch_shapes=[
            pltpu.VMEM((3, 20, 112, 128), jnp.float32),
            pltpu.VMEM((1536, 256), jnp.bfloat16),
            pltpu.VMEM((256, 128), jnp.float32),
            pltpu.VMEM((256, 256), jnp.bfloat16),
            pltpu.VMEM((96, 256), jnp.float32),
            pltpu.VMEM((16, 256), jnp.float32),
            pltpu.VMEM((512, 256), jnp.float32),
            pltpu.SemaphoreType.DMA((5,)),
        ],
        compiler_params=pltpu.CompilerParams(vmem_limit_bytes=32 * 1024 * 1024),
        name="field_products",
    )(phi_z, velocity, far, below, above, *sides, wx, wy, wz, wyz, phx)


def split(values):
    high = lax.reduce_precision(values, 8, 7)
    return high.astype(jnp.bfloat16), (values - high).astype(jnp.bfloat16)


def exchange(rows, axes):
    return lax.all_to_all(rows, axes, 0, 0, tiled=True)


def shards(velocity, below, above, omega_x, omega_y, omega_z, phi_x, phi_y, phi_z):
    total_x = 2048
    total_y = 1536
    total_z = 32
    gz = lax.axis_index("gz")
    near, x_high, x_low, y_high, y_low = pack(velocity)
    far = shift_permute(near, "gz", 1)
    sides = [
        shift_permute(x_high, "gx", 1),
        shift_permute(x_low, "gx", -1),
        shift_permute(y_high, "gy", 1),
        shift_permute(y_low, "gy", -1),
    ]
    wx = omega_x.astype(jnp.bfloat16)
    wy = omega_y.astype(jnp.float32)
    wz = omega_z.astype(jnp.float32)
    wyz = (omega_z.T[:, :, None] * omega_y.T[:, None, :]).astype(jnp.bfloat16).reshape(256, 1536)
    phx = phi_x.reshape(16, 16, 2, 128).transpose(0, 2, 1, 3).reshape(512, 128).astype(jnp.bfloat16)
    send, part_x = field(
        phi_z, velocity, far, below, above, sides,
        jnp.concatenate([wx, wx], axis=0), wy, wz, wyz, jnp.concatenate([phx, phx], axis=1),
    )
    got = exchange(send, ("gx", "gz")).reshape(16, 2, 32, 128)
    mine = lax.dynamic_index_in_dim(part_x, gz, 0, keepdims=False)
    theirs = shift_permute(lax.dynamic_index_in_dim(part_x, 1 - gz, 0, keepdims=False), "gz", 1)
    part_x = mine + theirs

    summed = jnp.sum(got, axis=(0, 1))
    summed_z = jnp.sum(lax.dynamic_index_in_dim(got, gz, 1, keepdims=False)[:, 30:], axis=0)
    rest = jnp.concatenate([summed[16:24, :64], summed[16:24, 64:]], axis=0)
    lead_high, lead_low = split(jnp.concatenate([summed[:16], rest], axis=1))
    wide = phi_y.T.astype(jnp.bfloat16)
    none = jnp.zeros((96, 512), jnp.bfloat16)
    wide = jnp.concatenate(
        [jnp.concatenate([wide, none], axis=1), jnp.concatenate([none, wide], axis=1)], axis=0
    )
    core = jnp.dot(jnp.concatenate([lead_high, lead_low], axis=0), wide, preferred_element_type=jnp.float32)
    core = (core[:16] + core[16:]).reshape(16, 8, 128)
    send = jnp.concatenate(
        [core, part_x.reshape(16, 8, 128), jnp.broadcast_to(summed_z[None], (16, 2, 128))], axis=1
    )
    got = jnp.sum(exchange(send.reshape(288, 128), "gy").reshape(16, 18, 128), axis=0)
    core_sketch = got[:8].reshape(1, 2, 512) * (1.0 / math.sqrt(total_x * total_y * total_z))
    other = shift_permute(got[8:16], "gz", 1)

    rows = jnp.concatenate([summed[24:30], got[16:18]], axis=0)
    got_y = exchange(jnp.broadcast_to(rows[None], (32, 8, 128)).reshape(256, 128), ("gx", "gz"))
    got_y = got_y.reshape(16, 2, 8, 128)
    factor_y = got_y[:, :, :6].reshape(32, 2, 3, 128).transpose(0, 2, 1, 3).reshape(96, 256)
    factor_y = factor_y * (1.0 / math.sqrt(total_x * total_z))
    factor_z = lax.dynamic_index_in_dim(got_y, gz, 1, keepdims=False)[:, 6:].reshape(16, 256)
    factor_z = factor_z * (1.0 / math.sqrt(total_x * total_y))

    first = jnp.where(gz == 0, got[8:16], other)
    second = jnp.where(gz == 0, other, got[8:16])
    rows = jnp.concatenate([first, second], axis=0)
    got_x = exchange(jnp.broadcast_to(rows[None], (16, 16, 128)).reshape(256, 128), "gy")
    factor_x = got_x.reshape(16, 2, 8, 128).transpose(0, 2, 1, 3).reshape(128, 256)
    factor_x = factor_x * (1.0 / math.sqrt(total_y * total_z))
    return (factor_x, factor_y, factor_z, core_sketch)


def solution(mesh):
    in_specs = (
        P(None, "gz", "gy", "gx"),
        P(None, None, "gy", "gx"),
        P(None, None, "gy", "gx"),
        P("gx", None),
        P("gy", None),
        P("gz", None),
        P(None, "gx"),
        P(None, "gy"),
        P(None, "gz"),
    )
    out_specs = (P("gx", None), P("gy", None), P("gz", None), P(("gx", "gy", "gz"), None, None))
    return jax.shard_map(shards, mesh=mesh, in_specs=in_specs, out_specs=out_specs, check_vma=False)
```

time: 142 us -> 136 us (0.958)
  the two profiles are of different devices: /device:TPU:1 before, /device:TPU:32 now
where the time goes in v2:
time: 136 us; the launch traced here: 135 us
  starting transfers between devices  57 us (42%)
  waiting for transfers between devices  43 us (32%)
  Pallas kernels  18.5 us (14%)
  local copies, waits for them, and re-layouts  10.7 us (8%)
  other arithmetic  5.13 us (4%)
    all_to_all x4, waiting for transfers between devices, exchange(): return lax.all_to_all(rows, axes, 0, 0, tiled=True)  36.4 us
    all_to_all x4, starting transfers between devices, exchange(): return lax.all_to_all(rows, axes, 0, 0, tiled=True)  30.8 us
    ppermute x7, starting transfers between devices, shift_permute(): lax.ppermute(cells, axis, [(i, (i + step) % count) for i in range(count)])  26.2 us
    pallas_call x1, Pallas kernels, field(): pl.pallas_call(field_kernel, in_specs=[pl.BlockSpec(memory_space=pltpu.SM...  14.9 us
    ppermute x7, waiting for transfers between devices, shift_permute(): lax.ppermute(cells, axis, [(i, (i + step) % count) for i in range(count)])  6.68 us
    unnamed x25, local copies, waits for them, and re-layouts  6.24 us
    pallas_call x1, Pallas kernels, pack(): pl.pallas_call(pack_kernel, grid=(3,), in_specs=[pl.BlockSpec((1, 16, 96,...  3.56 us
  transfers between devices with their start and end apart: 11, of which 5 were waited for; matrix products, arithmetic and copies ran while one was open for 6% of the time, Pallas kernels for 0%

profile of v2, /device:TPU:32, one launch (start us, length us, event | category | flops | bytes accessed | tf_op | source)
XLA Modules:
  0.0 135.5 jit_solution(9191251060550316806)
XLA Ops:
  0.7 3.6 %pack_halos.1 = (f32[3,2,96,128]{3,2,1,0:T(8,128)}, f32[96,128]{1,0:T(8,128)}, f32[96,128]{1,0:T(8,128)}, f32[3,32,128]{2,1,0:T(8,128)}, f32[3,32,128]{2,1,0:T(8,128)}) custom-call(f32[3,16,96,128]{3,2,1,0:T(8,128)} %vel.3), custom_call_target="tpu_custom_call" | custom-call | tf_op jit(solution)/shard_map/pack_halos/pallas_call | solution.py:44
  4.2 5.1 %collective-permute-start = (f32[3,2,96,128]{3,2,1,0:T(8,128)}, f32[3,2,96,128]{3,2,1,0:T(8,128)}, u32[]{:S(2)}, u32[]{:S(2)}) collective-permute-start(f32[3,2,96,128]{3,2,1,0:T(8,128)} %get-tuple-element.11), channel_id=1, source_target_pairs={{0,1},{1,0},{2,3},{3,2},{4,5},{5,4},{6,7},{7,6},{8,9},{9,8},{10,11... | collective-permute-start | bytes 884744 | tf_op jit(solution)/shard_map/ppermute | solution.py:13
  9.3 1.9 %collective-permute-start.1 = (f32[96,128]{1,0:T(8,128)}, f32[96,128]{1,0:T(8,128)}, u32[]{:S(2)}, u32[]{:S(2)}) collective-permute-start(f32[96,128]{1,0:T(8,128)} %get-tuple-element.12), channel_id=1, source_target_pairs={{0,32},{32,64},{64,96},{96,128},{128,160},{160,192},{192,224},{224... | collective-permute-start | bytes 147464 | tf_op jit(solution)/shard_map/ppermute | solution.py:13
  11.3 5.8 %collective-permute-start.2 = (f32[96,128]{1,0:T(8,128)}, f32[96,128]{1,0:T(8,128)}, u32[]{:S(2)}, u32[]{:S(2)}) collective-permute-start(f32[96,128]{1,0:T(8,128)} %get-tuple-element.13), channel_id=1, source_target_pairs={{0,480},{32,0},{64,32},{96,64},{128,96},{160,128},{192,160},{224,1... | collective-permute-start | bytes 147464 | tf_op jit(solution)/shard_map/ppermute | solution.py:13
  17.0 3.8 %collective-permute-start.3 = (f32[3,32,128]{2,1,0:T(8,128)}, f32[3,32,128]{2,1,0:T(8,128)}, u32[]{:S(2)}, u32[]{:S(2)}) collective-permute-start(f32[3,32,128]{2,1,0:T(8,128)} %get-tuple-element.14), channel_id=1, source_target_pairs={{0,2},{2,4},{4,6},{6,8},{8,10},{10,12},{12,14},{14,16},{16,18},{18... | collective-permute-start | bytes 147464 | tf_op jit(solution)/shard_map/ppermute | solution.py:13
  20.9 2.3 %collective-permute-start.4 = (f32[3,32,128]{2,1,0:T(8,128)}, f32[3,32,128]{2,1,0:T(8,128)}, u32[]{:S(2)}, u32[]{:S(2)}) collective-permute-start(f32[3,32,128]{2,1,0:T(8,128)} %get-tuple-element.15), channel_id=1, source_target_pairs={{0,30},{2,0},{4,2},{6,4},{8,6},{10,8},{12,10},{14,12},{16,14},{18,... | collective-permute-start | bytes 147464 | tf_op jit(solution)/shard_map/ppermute | solution.py:13
  23.2 1.1 multiply_convert_fusion
  24.4 0.6 convert_element_type.41.wy
  25.0 1.4 %copy.24.wyz = bf16[256,1536]{1,0:T(8,128)(2,1)S(1)} copy(bf16[256,1536]{0,1:T(8,128)(2,1)} %bitcast.48) | data formatting | bytes 1572864 | tf_op jit(solution)/shard_map/convert_element_type | solution.py:224
  26.5 0.0 collective-permute-done.1.x_left
  26.5 0.0 collective-permute-done.2.x_right
  26.5 0.0 collective-permute-done.3.y_before
  26.5 0.7 collective-permute-done.4.y_after
  27.2 0.0 collective-permute-done.far
  27.2 0.0 copy-done
  27.2 0.9 copy-done.2
  28.1 1.0 copy-done.3
  29.0 1.0 copy-done.4
  30.0 0.7 copy-done.6
  30.7 14.9 %field_products.1 = (f32[1024,128]{1,0:T(8,128)S(1)}, f32[2,128,128]{2,1,0:T(8,128)S(1)}) custom-call(s32[2,16]{1,0:T(2,128)S(1)} %copy-done.6, f32[3,16,96,128]{3,2,1,0:T(8,128)S(1)} %copy-done, f32[3,2,96,128]{3,2,1,0:T(8,128)} %collective-permute-done.far, f32[3,2,96,128]{3,2,1,0:T(8,128)S(1)} %copy-done.3, f32[3,2,96,128]{3,2,1,0:T(8,128)S(1)} %copy-done.4, ...), custom_call_target="tpu_custom_call" | custom-call | tf_op jit(solution)/shard_map/field_products/pallas_call | solution.py:176
  45.6 0.8 copy-done.1
  46.4 0.7 copy-done.5
  47.0 4.5 %all-to-all-start = ((f32[32,32,128]{2,1,0:T(8,128)}), f32[32,32,128]{2,1,0:T(8,128)S(1)}, u32[]{:S(2)}, u32[]{:S(2)}) async-start(f32[32,32,128]{2,1,0:T(8,128)} %bitcast.46), calls=%async_computation | async-start | bytes 1048576 | tf_op jit(solution)/shard_map/all_to_all | solution.py:205
  51.6 0.9 dynamic-slice_bitcast_fusion.2
  52.4 5.2 %collective-permute-start.5 = (f32[128,128]{1,0:T(8,128)S(1)}, f32[128,128]{1,0:T(8,128)S(1)}, u32[]{:S(2)}, u32[]{:S(2)}) collective-permute-start(f32[128,128]{1,0:T(8,128)S(1)} %dynamic-slice_bitcast_fusion.2), channel_id=1, source_target_pairs={{0,1},{1,0},{2,3},{3,2},{4,5},{5,4},{6,7},{7,6},{8,9},{9,8},{10,11... | collective-permute-start | bytes 196616 | tf_op jit(solution)/shard_map/ppermute | solution.py:13
  57.6 0.9 convert_bitcast_fusion
  58.6 6.0 %collective-permute-done.5 = f32[128,128]{1,0:T(8,128)S(1)} collective-permute-done((f32[128,128]{1,0:T(8,128)S(1)}, f32[128,128]{1,0:T(8,128)S(1)}, u32[]{:S(2)}, u32[]{:S(2)}) %collective-permute-start.5) | collective-permute-done | bytes 65568 | tf_op jit(solution)/shard_map/ppermute | solution.py:13
  64.5 0.8 fusion.11
  65.4 0.0 all-to-all-done
  65.5 0.1 fusion.19
  65.5 0.1 fusion.3
  65.8 0.7 pad_maximum_fusion.1
  66.5 14.8 %all-to-all-start.1 = ((f32[16,18,128]{2,1,0:T(8,128)}), f32[16,18,128]{2,1,0:T(8,128)S(1)}, u32[]{:S(2)}, u32[]{:S(2)}) async-start(f32[16,18,128]{2,1,0:T(8,128)} %pad_maximum_fusion.1), calls=%async_computation.1 | async-start | bytes 393216 | tf_op jit(solution)/shard_map/all_to_all | solution.py:205
  81.4 16.1 %all-to-all-done.1 = f32[16,18,128]{2,1,0:T(8,128)S(1)} async-done(((f32[16,18,128]{2,1,0:T(8,128)}), f32[16,18,128]{2,1,0:T(8,128)S(1)}, u32[]{:S(2)}, u32[]{:S(2)}) %all-to-all-start.1) | async-done | bytes 147488 | tf_op jit(solution)/shard_map/all_to_all | solution.py:205
  97.5 2.1 %collective-permute-start.6 = (f32[8,128]{1,0:T(8,128)S(1)}, f32[8,128]{1,0:T(8,128)S(1)}, u32[]{:S(2)}, u32[]{:S(2)}) collective-permute-start(f32[8,128]{1,0:T(8,128)S(1)} %slice.56), channel_id=1, source_target_pairs={{0,1},{1,0},{2,3},{3,2},{4,5},{5,4},{6,7},{7,6},{8,9},{9,8},{10,11... | collective-permute-start | bytes 12296 | tf_op jit(solution)/shard_map/ppermute | solution.py:13
  99.6 0.7 broadcast_in_dim.8
  100.3 6.0 %all-to-all-start.3 = ((f32[32,8,128]{2,1,0:T(8,128)}), f32[32,8,128]{2,1,0:T(8,128)S(1)}, u32[]{:S(2)}, u32[]{:S(2)}) async-start(f32[32,8,128]{2,1,0:T(8,128)} %broadcast_in_dim.8), calls=%async_computation.3 | async-start | bytes 262144 | tf_op jit(solution)/shard_map/all_to_all | solution.py:205
  106.3 0.0 collective-permute-done.6
  106.3 0.6 mul.89
  106.9 7.3 %all-to-all-done.3 = f32[32,8,128]{2,1,0:T(8,128)S(1)} async-done(((f32[32,8,128]{2,1,0:T(8,128)}), f32[32,8,128]{2,1,0:T(8,128)S(1)}, u32[]{:S(2)}, u32[]{:S(2)}) %all-to-all-start.3) | async-done | bytes 131104 | tf_op jit(solution)/shard_map/all_to_all | solution.py:205
  114.2 0.7 broadcast_in_dim.7
  114.9 5.5 %all-to-all-start.2 = ((f32[16,16,128]{2,1,0:T(8,128)}), f32[16,16,128]{2,1,0:T(8,128)S(1)}, u32[]{:S(2)}, u32[]{:S(2)}) async-start(f32[16,16,128]{2,1,0:T(8,128)} %broadcast_in_dim.7), calls=%async_computation.2 | async-start | bytes 262144 | tf_op jit(solution)/shard_map/all_to_all | solution.py:205
  120.4 0.1 copy.26
  120.5 0.1 copy.27
  120.6 0.6 copy.35
  121.2 0.6 copy.36
  121.8 13.0 %all-to-all-done.2 = f32[16,16,128]{2,1,0:T(8,128)S(1)} async-done(((f32[16,16,128]{2,1,0:T(8,128)}), f32[16,16,128]{2,1,0:T(8,128)S(1)}, u32[]{:S(2)}, u32[]{:S(2)}) %all-to-all-start.2) | async-done | bytes 131104 | tf_op jit(solution)/shard_map/all_to_all | solution.py:205
  134.8 0.7 multiply_bitcast_fusion
  (39 shorter events, 0.4 us)
Async XLA Ops:
  0.6 22.6 %copy-start.10 = (s32[16,256]{1,0:T(8,128)S(1)}, s32[16,256]{1,0:T(8,128)}, u32[]{:S(2)}) copy-start(s32[16,256]{1,0:T(8,128)} %param.14) | copy-start | bytes 49156
  0.6 22.6 %copy-start.7 = (s32[96,256]{1,0:T(8,128)S(1)}, s32[96,256]{1,0:T(8,128)}, u32[]{:S(2)}) copy-start(s32[96,256]{1,0:T(8,128)} %param.13) | copy-start | bytes 294916
  0.7 23.6 %copy-start.8 = (s32[512,128]{1,0:T(8,128)S(1)}, s32[512,128]{1,0:T(8,128)}, u32[]{:S(2)}) copy-start(s32[512,128]{1,0:T(8,128)} %param.15) | copy-start | bytes 786436
  0.7 23.7 %copy-start.9 = (s32[128,256]{1,0:T(8,128)S(1)}, s32[128,256]{1,0:T(8,128)}, u32[]{:S(2)}) copy-start(s32[128,256]{1,0:T(8,128)} %param.12) | copy-start | bytes 393220
  4.2 22.9 %collective-permute-start = (f32[3,2,96,128]{3,2,1,0:T(8,128)}, f32[3,2,96,128]{3,2,1,0:T(8,128)}, u32[]{:S(2)}, u32[]{:S(2)}) collective-permute-start(f32[3,2,96,128]{3,2,1,0:T(8,128)} %get-tuple-element.11), channel_id=1, source_target_pairs={{0,1},{1,0},{2,3},{3,2},{4,5},{5,4},{6,7},{7,6},{8,9},{9,8},{10,11... | collective-permute-start | bytes 884744 | tf_op jit(solution)/shard_map/ppermute | solution.py:13
  9.3 17.1 %collective-permute-start.1 = (f32[96,128]{1,0:T(8,128)}, f32[96,128]{1,0:T(8,128)}, u32[]{:S(2)}, u32[]{:S(2)}) collective-permute-start(f32[96,128]{1,0:T(8,128)} %get-tuple-element.12), channel_id=1, source_target_pairs={{0,32},{32,64},{64,96},{96,128},{128,160},{160,192},{192,224},{224... | collective-permute-start | bytes 147464 | tf_op jit(solution)/shard_map/ppermute | solution.py:13
  11.3 15.2 %collective-permute-start.2 = (f32[96,128]{1,0:T(8,128)}, f32[96,128]{1,0:T(8,128)}, u32[]{:S(2)}, u32[]{:S(2)}) collective-permute-start(f32[96,128]{1,0:T(8,128)} %get-tuple-element.13), channel_id=1, source_target_pairs={{0,480},{32,0},{64,32},{96,64},{128,96},{160,128},{192,160},{224,1... | collective-permute-start | bytes 147464 | tf_op jit(solution)/shard_map/ppermute | solution.py:13
  17.0 9.4 %collective-permute-start.3 = (f32[3,32,128]{2,1,0:T(8,128)}, f32[3,32,128]{2,1,0:T(8,128)}, u32[]{:S(2)}, u32[]{:S(2)}) collective-permute-start(f32[3,32,128]{2,1,0:T(8,128)} %get-tuple-element.14), channel_id=1, source_target_pairs={{0,2},{2,4},{4,6},{6,8},{8,10},{10,12},{12,14},{14,16},{16,18},{18... | collective-permute-start | bytes 147464 | tf_op jit(solution)/shard_map/ppermute | solution.py:13
  20.9 6.3 %collective-permute-start.4 = (f32[3,32,128]{2,1,0:T(8,128)}, f32[3,32,128]{2,1,0:T(8,128)}, u32[]{:S(2)}, u32[]{:S(2)}) collective-permute-start(f32[3,32,128]{2,1,0:T(8,128)} %get-tuple-element.15), channel_id=1, source_target_pairs={{0,30},{2,0},{4,2},{6,4},{8,6},{10,8},{12,10},{14,12},{16,14},{18,... | collective-permute-start | bytes 147464 | tf_op jit(solution)/shard_map/ppermute | solution.py:13
  24.3 2.9 %copy-start = (f32[3,16,96,128]{3,2,1,0:T(8,128)S(1)}, f32[3,16,96,128]{3,2,1,0:T(8,128)}, u32[]{:S(2)}) copy-start(f32[3,16,96,128]{3,2,1,0:T(8,128)} %vel.3) | copy-start | bytes 7077892
  27.2 0.9 copy-start.2
  28.1 1.0 copy-start.3
  29.0 1.0 copy-start.4
  30.0 0.7 copy-start.6
  45.6 0.8 copy-start.1
  46.4 0.7 copy-start.5
  47.0 18.3 %all-to-all-start = ((f32[32,32,128]{2,1,0:T(8,128)}), f32[32,32,128]{2,1,0:T(8,128)S(1)}, u32[]{:S(2)}, u32[]{:S(2)}) async-start(f32[32,32,128]{2,1,0:T(8,128)} %bitcast.46), calls=%async_computation | async-start | bytes 1048576 | tf_op jit(solution)/shard_map/all_to_all | solution.py:205
  52.4 12.1 %collective-permute-start.5 = (f32[128,128]{1,0:T(8,128)S(1)}, f32[128,128]{1,0:T(8,128)S(1)}, u32[]{:S(2)}, u32[]{:S(2)}) collective-permute-start(f32[128,128]{1,0:T(8,128)S(1)} %dynamic-slice_bitcast_fusion.2), channel_id=1, source_target_pairs={{0,1},{1,0},{2,3},{3,2},{4,5},{5,4},{6,7},{7,6},{8,9},{9,8},{10,11... | collective-permute-start | bytes 196616 | tf_op jit(solution)/shard_map/ppermute | solution.py:13
  66.5 30.9 %all-to-all-start.1 = ((f32[16,18,128]{2,1,0:T(8,128)}), f32[16,18,128]{2,1,0:T(8,128)S(1)}, u32[]{:S(2)}, u32[]{:S(2)}) async-start(f32[16,18,128]{2,1,0:T(8,128)} %pad_maximum_fusion.1), calls=%async_computation.1 | async-start | bytes 393216 | tf_op jit(solution)/shard_map/all_to_all | solution.py:205
  97.5 8.8 %collective-permute-start.6 = (f32[8,128]{1,0:T(8,128)S(1)}, f32[8,128]{1,0:T(8,128)S(1)}, u32[]{:S(2)}, u32[]{:S(2)}) collective-permute-start(f32[8,128]{1,0:T(8,128)S(1)} %slice.56), channel_id=1, source_target_pairs={{0,1},{1,0},{2,3},{3,2},{4,5},{5,4},{6,7},{7,6},{8,9},{9,8},{10,11... | collective-permute-start | bytes 12296 | tf_op jit(solution)/shard_map/ppermute | solution.py:13
  100.3 14.0 %all-to-all-start.3 = ((f32[32,8,128]{2,1,0:T(8,128)}), f32[32,8,128]{2,1,0:T(8,128)S(1)}, u32[]{:S(2)}, u32[]{:S(2)}) async-start(f32[32,8,128]{2,1,0:T(8,128)} %broadcast_in_dim.8), calls=%async_computation.3 | async-start | bytes 262144 | tf_op jit(solution)/shard_map/all_to_all | solution.py:205
  114.9 19.9 %all-to-all-start.2 = ((f32[16,16,128]{2,1,0:T(8,128)}), f32[16,16,128]{2,1,0:T(8,128)S(1)}, u32[]{:S(2)}, u32[]{:S(2)}) async-start(f32[16,16,128]{2,1,0:T(8,128)} %broadcast_in_dim.7), calls=%async_computation.2 | async-start | bytes 262144 | tf_op jit(solution)/shard_map/all_to_all | solution.py:205

commit v3 on v2

v3 whole, which is shorter than its diff:
```python
import math

import jax
import jax.numpy as jnp
from jax import lax
from jax.experimental import pallas as pl
from jax.experimental.pallas import tpu as pltpu
from jax.sharding import PartitionSpec as P


def shift_permute(cells, axis, step):
    count = lax.axis_size(axis)
    return lax.ppermute(cells, axis, [(i, (i + step) % count) for i in range(count)])


def pack_kernel(vel, near, x_high, x_low, y_high, y_low, held, sems):
    gz = lax.axis_index("gz")
    copies = [
        pltpu.make_async_copy(
            vel.at[part // 2, pl.ds(8 * (part % 2), 8)], held.at[part // 2, pl.ds(8 * (part % 2), 8)], sems.at[part]
        )
        for part in range(6)
    ]
    for copy in copies:
        copy.start()
    lane = lax.broadcasted_iota(jnp.int32, (96, 128), 1)
    high = jnp.zeros((96, 128), jnp.float32)
    low = jnp.zeros((96, 128), jnp.float32)
    rims = []
    for part in range(6):
        copies[part].wait()
        c = part // 2
        if part % 2 == 1:
            rims.append(
                pltpu.make_async_copy(held.at[c, pl.ds(14 * (1 - gz), 2)], near.at[c], sems.at[6 + c])
            )
            rims[-1].start()
        for k in range(8 * (part % 2), 8 * (part % 2) + 8):
            spot = 2 * (16 * c + k)
            turned = pltpu.roll(held[c, k], spot + 2, 1)
            high = jnp.where((lane >= spot) & (lane < spot + 2), turned, high)
            low = jnp.where((lane >= spot + 2) & (lane < spot + 4), turned, low)
            y_low[c, 2 * k : 2 * k + 2, :] = held[c, k, 0:2, :]
            y_high[c, 2 * k : 2 * k + 2, :] = held[c, k, 94:96, :]
    x_high[...] = high
    x_low[...] = low
    for rim in rims:
        rim.wait()


def pack(velocity):
    rims = jax.ShapeDtypeStruct((96, 128), jnp.float32)
    rows = jax.ShapeDtypeStruct((3, 32, 128), jnp.float32)
    whole = pl.BlockSpec(memory_space=pltpu.VMEM)
    outside = pl.BlockSpec(memory_space=pl.ANY)
    return pl.pallas_call(
        pack_kernel,
        in_specs=[outside],
        out_specs=[outside] + [whole] * 4,
        out_shape=[jax.ShapeDtypeStruct((3, 2, 96, 128), jnp.float32), rims, rims, rows, rows],
        scratch_shapes=[pltpu.VMEM((3, 16, 96, 128), jnp.float32), pltpu.SemaphoreType.DMA((9,))],
        compiler_params=pltpu.CompilerParams(vmem_limit_bytes=60 * 1024 * 1024),
        name="pack_halos",
    )(velocity)


def field_kernel(
    phi_z, vel, far, below, above, x_left, x_right, y_before, y_after, omega_x, omega_y, omega_z, phi_x,
    send, mine, theirs,
    padded, sides, x_held, y_held, wx_held, wy_held, wz_held, px_held,
    q_terms, flat, flat_terms, wx, wyz, phx, part_y, part_z, lead, sems,
):
    gz = lax.axis_index("gz")
    middle = pl.ds(8, 96)
    x_copies = [
        pltpu.make_async_copy(x_left, x_held.at[0], sems.at[0]),
        pltpu.make_async_copy(x_right, x_held.at[1], sems.at[1]),
    ]
    y_copies = [
        pltpu.make_async_copy(y_before, y_held.at[0], sems.at[2]),
        pltpu.make_async_copy(y_after, y_held.at[1], sems.at[3]),
    ]
    cells_copies = [
        pltpu.make_async_copy(vel.at[c], padded.at[c, pl.ds(2, 16), middle, :], sems.at[4 + c]) for c in range(3)
    ]
    far_low = pltpu.make_async_copy(far, padded.at[:, pl.ds(0, 2), middle, :], sems.at[7])
    far_high = pltpu.make_async_copy(far, padded.at[:, pl.ds(18, 2), middle, :], sems.at[8])
    rim_low = pltpu.make_async_copy(below, padded.at[:, pl.ds(0, 2), middle, :], sems.at[7])
    rim_high = pltpu.make_async_copy(above, padded.at[:, pl.ds(18, 2), middle, :], sems.at[8])
    weight_copies = [
        pltpu.make_async_copy(omega_x, wx_held, sems.at[9]),
        pltpu.make_async_copy(omega_y, wy_held, sems.at[10]),
        pltpu.make_async_copy(omega_z, wz_held, sems.at[11]),
        pltpu.make_async_copy(phi_x, px_held, sems.at[12]),
    ]
    for copy in x_copies + cells_copies + y_copies:
        copy.start()

    @pl.when(gz == 0)
    def _():
        rim_low.start()
        far_high.start()

    @pl.when(gz == 1)
    def _():
        far_low.start()
        rim_high.start()

    for copy in weight_copies:
        copy.start()
    for copy in x_copies:
        copy.wait()

    lane_all = lax.broadcasted_iota(jnp.int32, (96, 128), 1)

    def place(k, carry):
        for c in range(3):
            spot = 2 * (16 * c + k)
            both = jnp.where(lane_all < spot + 2, x_held[0], x_held[1])
            sides[c, k] = pltpu.roll(both, 126 - spot, 1)
        return carry

    lax.fori_loop(0, 16, place, 0, unroll=2)

    for copy in y_copies + cells_copies:
        copy.wait()
    for c in range(3):
        for k in range(16):
            padded[c, k + 2, 6:8, :] = y_held[0, c, 2 * k : 2 * k + 2, :]
            padded[c, k + 2, 104:106, :] = y_held[1, c, 2 * k : 2 * k + 2, :]
    flat[...] = jnp.zeros((256, 128), jnp.float32)

    @pl.when(gz == 0)
    def _():
        rim_low.wait()
        far_high.wait()

    @pl.when(gz == 1)
    def _():
        far_low.wait()
        rim_high.wait()

    lane = lax.broadcasted_iota(jnp.int32, (16, 128), 1)

    def plane(k, carry):
        weight = [phi_z[c, k].astype(jnp.float32) for c in range(2)]
        for block in range(6):
            row = 16 * block
            at = row + 8
            along = [[], [], []]
            for c in range(3):
                cells = padded[c, k + 2, at : at + 16, :]
                rim = sides[c, k, row : row + 16, :]
                outer = pltpu.roll(jnp.where(lane >= 126, rim, cells), 2, 1) - pltpu.roll(
                    jnp.where(lane < 2, rim, cells), 126, 1
                )
                inner = pltpu.roll(jnp.where(lane < 1, rim, cells), 127, 1) - pltpu.roll(
                    jnp.where(lane >= 127, rim, cells), 1, 1
                )
                along[0].append(outer + 8.0 * inner)
                outer = padded[c, k + 2, at - 2 : at + 14, :] - padded[c, k + 2, at + 2 : at + 18, :]
                inner = padded[c, k + 2, at + 1 : at + 17, :] - padded[c, k + 2, at - 1 : at + 15, :]
                along[1].append(outer + 8.0 * inner)
                outer = padded[c, k, at : at + 16, :] - padded[c, k + 4, at : at + 16, :]
                inner = padded[c, k + 3, at : at + 16, :] - padded[c, k + 1, at : at + 16, :]
                along[2].append(outer + 8.0 * inner)
            diagonal = along[0][0] * along[0][0] + along[1][1] * along[1][1] + along[2][2] * along[2][2]
            mixed = along[0][1] * along[1][0] + along[0][2] * along[2][0] + along[1][2] * along[2][1]
            field = (-0.5 / 144.0) * (diagonal + 2.0 * mixed)
            high = field.astype(jnp.bfloat16)
            low = (field - high.astype(jnp.float32)).astype(jnp.bfloat16)
            rows = pl.ds(pl.multiple_of(96 * k + row, 16), 16)
            q_terms[rows, 0:128] = high
            q_terms[rows, 128:256] = low
            for c in range(2):
                flat[96 * c + row : 96 * c + row + 16, :] += weight[c] * field
        return carry

    lax.fori_loop(0, 16, plane, 0, unroll=2)

    for copy in weight_copies:
        copy.wait()
    wx[0:128, :] = wx_held[...].astype(jnp.float32).astype(jnp.bfloat16)
    wx[128:256, :] = wx_held[...].astype(jnp.float32).astype(jnp.bfloat16)
    phx[:, 0:128] = px_held[...].astype(jnp.float32).astype(jnp.bfloat16)
    phx[:, 128:256] = px_held[...].astype(jnp.float32).astype(jnp.bfloat16)
    wy = wy_held[...].astype(jnp.float32)
    wz = wz_held[...].astype(jnp.float32)

    flat_high = flat[...].astype(jnp.bfloat16)
    flat_terms[:, 0:128] = flat_high
    flat_terms[:, 128:256] = (flat[...] - flat_high.astype(jnp.float32)).astype(jnp.bfloat16)
    leading = lax.dot_general(
        phx[...], flat_terms[...], (((1,), (1,)), ((), ())), preferred_element_type=jnp.float32
    )
    lead[0] = leading[:, 0:128]
    lead[1] = leading[:, 128:256]

    total_y = jnp.zeros((96, 256), jnp.float32)
    for k in range(16):
        rows = slice(96 * k, 96 * k + 96)
        sums = jnp.dot(q_terms[rows, :], wx[...], preferred_element_type=jnp.float32)
        total_y = total_y + sums * wz[k : k + 1, :]
        part_z[k : k + 1, :] = jnp.sum(sums * wy, axis=0, keepdims=True)
        wyz[rows, :] = (wy * wz[k : k + 1, :]).astype(jnp.bfloat16)
    part_y[...] = total_y

    lane8 = lax.broadcasted_iota(jnp.int32, (8, 128), 1)
    for g in range(16):
        for z in range(2):
            base = 40 * (2 * g + z)
            near = 32 * g + z
            send[base : base + 16, :] = lead[0, pl.ds(near, 16, stride=2), :]
            send[base + 16 : base + 24, :] = jnp.where(
                lane8 < 64,
                lead[1, pl.ds(near, 8, stride=2), :],
                pltpu.roll(lead[1, pl.ds(near + 16, 8, stride=2), :], 64, 1),
            )
            for half in range(2):
                lanes = slice(128 * half, 128 * half + 128)
                send[base + 24 + 6 * half : base + 30 + 6 * half, :] = part_y[6 * g : 6 * g + 6, lanes]
                send[base + 36 + half : base + 37 + half, :] = part_z[g : g + 1, lanes]
            send[base + 38 : base + 40, :] = jnp.zeros((2, 128), jnp.float32)

    turned = lax.dot_general(
        q_terms[...], wyz[...], (((0,), (0,)), ((), ())), preferred_element_type=jnp.float32
    )
    turned = turned[0:128, :] + turned[128:256, :]
    mine[...] = jnp.where(gz == 0, turned[:, 0:128], turned[:, 128:256])
    theirs[...] = jnp.where(gz == 0, turned[:, 128:256], turned[:, 0:128])


def field(phi_z, velocity, far, below, above, sides, omega_x, omega_y, omega_z, phi_x):
    whole = pl.BlockSpec(memory_space=pltpu.VMEM)
    outside = pl.BlockSpec(memory_space=pl.ANY)
    half = jax.ShapeDtypeStruct((128, 128), jnp.float32)
    return pl.pallas_call(
        field_kernel,
        in_specs=[pl.BlockSpec(memory_space=pltpu.SMEM)] + [outside] * 12,
        out_specs=[whole] * 3,
        out_shape=[jax.ShapeDtypeStruct((1280, 128), jnp.float32), half, half],
        scratch_shapes=[
            pltpu.VMEM((3, 20, 112, 128), jnp.float32),
            pltpu.VMEM((3, 16, 96, 128), jnp.float32),
            pltpu.VMEM((2, 96, 128), jnp.float32),
            pltpu.VMEM((2, 3, 32, 128), jnp.float32),
            pltpu.VMEM((128, 256), jnp.int32),
            pltpu.VMEM((96, 256), jnp.int32),
            pltpu.VMEM((16, 256), jnp.int32),
            pltpu.VMEM((512, 128), jnp.int32),
            pltpu.VMEM((1536, 256), jnp.bfloat16),
            pltpu.VMEM((256, 128), jnp.float32),
            pltpu.VMEM((256, 256), jnp.bfloat16),
            pltpu.VMEM((256, 256), jnp.bfloat16),
            pltpu.VMEM((1536, 256), jnp.bfloat16),
            pltpu.VMEM((512, 256), jnp.bfloat16),
            pltpu.VMEM((96, 256), jnp.float32),
            pltpu.VMEM((16, 256), jnp.float32),
            pltpu.VMEM((2, 512, 128), jnp.float32),
            pltpu.SemaphoreType.DMA((13,)),
        ],
        compiler_params=pltpu.CompilerParams(vmem_limit_bytes=60 * 1024 * 1024),
        name="field_products",
    )(phi_z, velocity, far, below, above, *sides, omega_x, omega_y, omega_z, phi_x)


def split(values):
    high = lax.reduce_precision(values, 8, 7)
    return high.astype(jnp.bfloat16), (values - high).astype(jnp.bfloat16)


def exchange(rows, axes):
    return lax.all_to_all(rows, axes, 0, 0, tiled=True)


def shards(velocity, below, above, omega_x, omega_y, omega_z, phi_x, phi_y, phi_z):
    total_x = 2048
    total_y = 1536
    total_z = 32
    gz = lax.axis_index("gz")
    near, x_high, x_low, y_high, y_low = pack(velocity)
    far = shift_permute(near, "gz", 1)
    sides = [
        shift_permute(x_high, "gx", 1),
        shift_permute(x_low, "gx", -1),
        shift_permute(y_high, "gy", 1),
        shift_permute(y_low, "gy", -1),
    ]
    send, mine, theirs = field(phi_z, velocity, far, below, above, sides, omega_x, omega_y, omega_z, phi_x)
    got = exchange(send, ("gx", "gz")).reshape(16, 2, 40, 128)
    part_x = mine + shift_permute(theirs, "gz", 1)

    summed = jnp.sum(got, axis=(0, 1))
    summed_z = jnp.sum(lax.dynamic_index_in_dim(got, gz, 1, keepdims=False)[:, 36:38], axis=0)
    rest = jnp.concatenate([summed[16:24, :64], summed[16:24, 64:]], axis=0)
    lead_high, lead_low = split(jnp.concatenate([summed[:16], rest], axis=1))
    wide = phi_y.T.astype(jnp.bfloat16)
    none = jnp.zeros((96, 512), jnp.bfloat16)
    wide = jnp.concatenate(
        [jnp.concatenate([wide, none], axis=1), jnp.concatenate([none, wide], axis=1)], axis=0
    )
    core = jnp.dot(jnp.concatenate([lead_high, lead_low], axis=0), wide, preferred_element_type=jnp.float32)
    core = (core[:16] + core[16:]).reshape(16, 8, 128)
    send = jnp.concatenate(
        [core, part_x.reshape(16, 8, 128), jnp.broadcast_to(summed_z[None], (16, 2, 128))], axis=1
    )
    got = jnp.sum(exchange(send.reshape(288, 128), "gy").reshape(16, 18, 128), axis=0)
    core_sketch = got[:8].reshape(1, 2, 512) * (1.0 / math.sqrt(total_x * total_y * total_z))

    got_y = lax.all_gather(summed[24:40], "gx", axis=0, tiled=True).reshape(16, 16, 128)
    factor_y = got_y[:, :12].reshape(16, 2, 6, 128).transpose(0, 2, 1, 3).reshape(96, 256)
    factor_y = factor_y * (1.0 / math.sqrt(total_x * total_z))

    got_z = lax.all_gather(got[16:18], "gx", axis=0, tiled=True)
    factor_z = got_z.reshape(16, 256) * (1.0 / math.sqrt(total_x * total_y))

    got_x = exchange(jnp.broadcast_to(got[None, 8:16], (32, 8, 128)).reshape(256, 128), ("gy", "gz"))
    factor_x = got_x.reshape(16, 2, 8, 128).transpose(0, 2, 1, 3).reshape(128, 256)
    factor_x = factor_x * (1.0 / math.sqrt(total_y * total_z))
    return (factor_x, factor_y, factor_z, core_sketch)


def solution(mesh):
    in_specs = (
        P(None, "gz", "gy", "gx"),
        P(None, None, "gy", "gx"),
        P(None, None, "gy", "gx"),
        P("gx", None),
        P("gy", None),
        P("gz", None),
        P(None, "gx"),
        P(None, "gy"),
        P(None, "gz"),
    )
    out_specs = (P("gx", None), P("gy", None), P("gz", None), P(("gx", "gy", "gz"), None, None))
    return jax.shard_map(shards, mesh=mesh, in_specs=in_specs, out_specs=out_specs, check_vma=False)
```

time: 136 us -> 124 us (0.912)
  the two profiles are of different devices: /device:TPU:32 before, /device:TPU:1 now
where the time goes in v3:
time: 124 us; the launch traced here: 123 us
  starting transfers between devices  59.3 us (48%)
  blocking collectives  36.6 us (30%)
  Pallas kernels  10.7 us (9%)
  waiting for transfers between devices  8.8 us (7%)
  local copies, waits for them, and re-layouts  4.05 us (3%)
  other arithmetic  2.43 us (2%)
    all_to_all x3, starting transfers between devices, exchange(): return lax.all_to_all(rows, axes, 0, 0, tiled=True)  30.6 us
    ppermute x6, starting transfers between devices, shift_permute(): lax.ppermute(cells, axis, [(i, (i + step) % count) for i in range(count)])  28.7 us
    all_gather x1, blocking collectives, shards(): lax.all_gather(summed[24:40], 'gx', axis=0, tiled=True).reshape(16, 16, 128)  20.4 us
    all_gather x1, blocking collectives, shards(): got_z = lax.all_gather(got[16:18], 'gx', axis=0, tiled=True)  16.2 us
    pallas_call x1, Pallas kernels, field(): pl.pallas_call(field_kernel, in_specs=[pl.BlockSpec(memory_space=pltpu.SM...  7.49 us
    ppermute x6, waiting for transfers between devices, shift_permute(): lax.ppermute(cells, axis, [(i, (i + step) % count) for i in range(count)])  7.1 us
    pallas_call x1, Pallas kernels, pack(): pl.pallas_call(pack_kernel, in_specs=[outside], out_specs=[outside] + [wh...  3.26 us
    unnamed x16, local copies, waits for them, and re-layouts  2.59 us
  transfers between devices with their start and end apart: 9, of which 3 were waited for; matrix products, arithmetic and copies ran while one was open for 2% of the time, Pallas kernels for 0%

profile of v3, /device:TPU:1, one launch (start us, length us, event | category | flops | bytes accessed | tf_op | source)
XLA Modules:
  0.0 122.9 jit_solution(13874010270607208906)
XLA Ops:
  0.6 3.3 %pack_halos.1 = (f32[3,2,96,128]{3,2,1,0:T(8,128)}, f32[96,128]{1,0:T(8,128)}, f32[96,128]{1,0:T(8,128)}, f32[3,32,128]{2,1,0:T(8,128)}, f32[3,32,128]{2,1,0:T(8,128)}) custom-call(f32[3,16,96,128]{3,2,1,0:T(8,128)} %vel.3), custom_call_target="tpu_custom_call" | custom-call | tf_op jit(solution)/shard_map/pack_halos/pallas_call | solution.py:56
  3.9 5.7 %collective-permute-start = (f32[3,2,96,128]{3,2,1,0:T(8,128)}, f32[3,2,96,128]{3,2,1,0:T(8,128)S(1)}, u32[]{:S(2)}, u32[]{:S(2)}) collective-permute-start(f32[3,2,96,128]{3,2,1,0:T(8,128)} %get-tuple-element.12), channel_id=1, source_target_pairs={{0,1},{1,0},{2,3},{3,2},{4,5},{5,4},{6,7},{7,6},{8,9},{9,8},{10,11... | collective-permute-start | bytes 884744 | tf_op jit(solution)/shard_map/ppermute | solution.py:13
  9.6 3.1 %collective-permute-start.1 = (f32[96,128]{1,0:T(8,128)}, f32[96,128]{1,0:T(8,128)S(1)}, u32[]{:S(2)}, u32[]{:S(2)}) collective-permute-start(f32[96,128]{1,0:T(8,128)} %get-tuple-element.13), channel_id=1, source_target_pairs={{0,32},{32,64},{64,96},{96,128},{128,160},{160,192},{192,224},{224... | collective-permute-start | bytes 147464 | tf_op jit(solution)/shard_map/ppermute | solution.py:13
  12.7 3.8 %collective-permute-start.2 = (f32[96,128]{1,0:T(8,128)}, f32[96,128]{1,0:T(8,128)S(1)}, u32[]{:S(2)}, u32[]{:S(2)}) collective-permute-start(f32[96,128]{1,0:T(8,128)} %get-tuple-element.14), channel_id=1, source_target_pairs={{0,480},{32,0},{64,32},{96,64},{128,96},{160,128},{192,160},{224,1... | collective-permute-start | bytes 147464 | tf_op jit(solution)/shard_map/ppermute | solution.py:13
  16.5 1.9 %collective-permute-start.3 = (f32[3,32,128]{2,1,0:T(8,128)}, f32[3,32,128]{2,1,0:T(8,128)S(1)}, u32[]{:S(2)}, u32[]{:S(2)}) collective-permute-start(f32[3,32,128]{2,1,0:T(8,128)} %get-tuple-element.15), channel_id=1, source_target_pairs={{0,2},{2,4},{4,6},{6,8},{8,10},{10,12},{12,14},{14,16},{16,18},{18... | collective-permute-start | bytes 147464 | tf_op jit(solution)/shard_map/ppermute | solution.py:13
  18.5 0.0 copy-start.1
  18.5 9.3 %collective-permute-start.4 = (f32[3,32,128]{2,1,0:T(8,128)}, f32[3,32,128]{2,1,0:T(8,128)S(1)}, u32[]{:S(2)}, u32[]{:S(2)}) collective-permute-start(f32[3,32,128]{2,1,0:T(8,128)} %get-tuple-element.16), channel_id=1, source_target_pairs={{0,30},{2,0},{4,2},{6,4},{8,6},{10,8},{12,10},{14,12},{16,14},{18,... | collective-permute-start | bytes 147464 | tf_op jit(solution)/shard_map/ppermute | solution.py:13
  27.8 0.0 collective-permute-done.1.x_left
  27.8 0.0 copy-start.2
  27.9 0.0 collective-permute-done.2.x_right
  27.9 0.0 copy-start.3
  27.9 0.0 collective-permute-done.3.y_before
  27.9 0.0 copy-start.4
  27.9 1.4 %collective-permute-done.4.y_after = f32[3,32,128]{2,1,0:T(8,128)S(1)} collective-permute-done((f32[3,32,128]{2,1,0:T(8,128)}, f32[3,32,128]{2,1,0:T(8,128)S(1)}, u32[]{:S(2)}, u32[]{:S(2)}) %collective-permute-start.4) | collective-permute-done | bytes 49184 | tf_op jit(solution)/shard_map/ppermute | solution.py:13
  29.3 0.0 copy-start.5
  29.3 0.0 collective-permute-done.far
  29.3 0.0 copy-done.2
  29.3 0.0 copy-done.3
  29.3 0.0 copy-done.4
  29.3 0.6 copy-done.5
  29.9 0.0 copy-start
  29.9 0.7 copy-done
  30.6 7.5 %field_products.1 = (f32[1280,128]{1,0:T(8,128)}, f32[128,128]{1,0:T(8,128)}, f32[128,128]{1,0:T(8,128)}) custom-call(s32[2,16]{1,0:T(2,128)} %phi_z.1, f32[3,16,96,128]{3,2,1,0:T(8,128)} %vel.3, f32[3,2,96,128]{3,2,1,0:T(8,128)} %copy-done, f32[3,2,96,128]{3,2,1,0:T(8,128)} %below.1, f32[3,2,96,128]{3,2,1,0:T(8,128)} %above.1, f32[96,128]{1,0:T(8,128)} %copy-done.2, ...), custom_call_target="tpu_custom_call" | custom-call | tf_op jit(solution)/shard_map/field_products/pallas_call | solution.py:237
  38.1 8.0 %all-to-all-start = ((f32[32,40,128]{2,1,0:T(8,128)}), f32[32,40,128]{2,1,0:T(8,128)S(1)}, u32[]{:S(2)}, u32[]{:S(2)}) async-start(f32[32,40,128]{2,1,0:T(8,128)} %bitcast.33), calls=%async_computation | async-start | bytes 1310720 | tf_op jit(solution)/shard_map/all_to_all | solution.py:273
  46.1 4.8 %collective-permute-start.5 = (f32[128,128]{1,0:T(8,128)}, f32[128,128]{1,0:T(8,128)S(1)}, u32[]{:S(2)}, u32[]{:S(2)}) collective-permute-start(f32[128,128]{1,0:T(8,128)} %get-tuple-element.19), channel_id=1, source_target_pairs={{0,1},{1,0},{2,3},{3,2},{4,5},{5,4},{6,7},{7,6},{8,9},{9,8},{10,11... | collective-permute-start | bytes 196616 | tf_op jit(solution)/shard_map/ppermute | solution.py:13
  50.9 0.0 copy-done.1
  50.9 5.7 %collective-permute-done.5 = f32[128,128]{1,0:T(8,128)S(1)} collective-permute-done((f32[128,128]{1,0:T(8,128)}, f32[128,128]{1,0:T(8,128)S(1)}, u32[]{:S(2)}, u32[]{:S(2)}) %collective-permute-start.5) | collective-permute-done | bytes 65568 | tf_op jit(solution)/shard_map/ppermute | solution.py:13
  56.6 0.8 add_bitcast_fusion
  57.5 1.7 %all-to-all-done = f32[32,40,128]{2,1,0:T(8,128)S(1)} async-done(((f32[32,40,128]{2,1,0:T(8,128)}), f32[32,40,128]{2,1,0:T(8,128)S(1)}, u32[]{:S(2)}, u32[]{:S(2)}) %all-to-all-start) | async-done | bytes 655392 | tf_op jit(solution)/shard_map/all_to_all | solution.py:273
  59.2 0.1 reduce_sum.27
  59.2 0.1 fusion.19
  59.3 0.1 fusion.3
  59.6 0.7 pad_maximum_fusion
  60.3 9.4 %all-to-all-start.1 = ((f32[16,18,128]{2,1,0:T(8,128)}), f32[16,18,128]{2,1,0:T(8,128)S(1)}, u32[]{:S(2)}, u32[]{:S(2)}) async-start(f32[16,18,128]{2,1,0:T(8,128)} %pad_maximum_fusion), calls=%async_computation.1 | async-start | bytes 393216 | tf_op jit(solution)/shard_map/all_to_all | solution.py:273
  69.7 20.4 %all_gather.6 = f32[256,128]{1,0:T(8,128)S(1)} all-gather(f32[16,128]{1,0:T(8,128)S(1)} %get-tuple-element.20), channel_id=1, replica_groups=mesh['gx'=16,'gy'=16,'gz'=2] {'gx'}, dimensions={0}, use_global_device_ids=true | all-gather | bytes 139264 | tf_op jit(solution)/shard_map/all_gather | solution.py:310
  90.1 0.0 all-to-all-done.1
  90.1 0.7 broadcast_in_dim.5
  90.8 13.2 %all-to-all-start.2 = ((f32[32,8,128]{2,1,0:T(8,128)}), f32[32,8,128]{2,1,0:T(8,128)S(1)}, u32[]{:S(2)}, u32[]{:S(2)}) async-start(f32[32,8,128]{2,1,0:T(8,128)} %broadcast_in_dim.5), calls=%async_computation.2 | async-start | bytes 262144 | tf_op jit(solution)/shard_map/all_to_all | solution.py:273
  104.1 0.1 copy.18
  104.2 0.6 copy.26
  104.8 16.2 %all-gather = f32[16,2,128]{2,1,0:T(2,128)S(1)} all-gather(f32[1,2,128]{2,1,0:T(2,128)S(1)} %slice_bitcast_fusion), channel_id=1, replica_groups=mesh['gx'=16,'gy'=16,'gz'=2] {'gx'}, dimensions={0}, use_global_device_ids=true | all-gather | bytes 17408 | tf_op jit(solution)/shard_map/all_gather | solution.py:314
  121.1 0.6 copy.27
  121.7 0.6 mul.71
  122.3 0.0 all-to-all-done.2
  122.3 0.7 broadcast_multiply_fusion
  (13 shorter events, 0.2 us)
Async XLA Ops:
  3.9 25.4 %collective-permute-start = (f32[3,2,96,128]{3,2,1,0:T(8,128)}, f32[3,2,96,128]{3,2,1,0:T(8,128)S(1)}, u32[]{:S(2)}, u32[]{:S(2)}) collective-permute-start(f32[3,2,96,128]{3,2,1,0:T(8,128)} %get-tuple-element.12), channel_id=1, source_target_pairs={{0,1},{1,0},{2,3},{3,2},{4,5},{5,4},{6,7},{7,6},{8,9},{9,8},{10,11... | collective-permute-start | bytes 884744 | tf_op jit(solution)/shard_map/ppermute | solution.py:13
  9.6 18.3 %collective-permute-start.1 = (f32[96,128]{1,0:T(8,128)}, f32[96,128]{1,0:T(8,128)S(1)}, u32[]{:S(2)}, u32[]{:S(2)}) collective-permute-start(f32[96,128]{1,0:T(8,128)} %get-tuple-element.13), channel_id=1, source_target_pairs={{0,32},{32,64},{64,96},{96,128},{128,160},{160,192},{192,224},{224... | collective-permute-start | bytes 147464 | tf_op jit(solution)/shard_map/ppermute | solution.py:13
  12.7 15.2 %collective-permute-start.2 = (f32[96,128]{1,0:T(8,128)}, f32[96,128]{1,0:T(8,128)S(1)}, u32[]{:S(2)}, u32[]{:S(2)}) collective-permute-start(f32[96,128]{1,0:T(8,128)} %get-tuple-element.14), channel_id=1, source_target_pairs={{0,480},{32,0},{64,32},{96,64},{128,96},{160,128},{192,160},{224,1... | collective-permute-start | bytes 147464 | tf_op jit(solution)/shard_map/ppermute | solution.py:13
  16.5 11.3 %collective-permute-start.3 = (f32[3,32,128]{2,1,0:T(8,128)}, f32[3,32,128]{2,1,0:T(8,128)S(1)}, u32[]{:S(2)}, u32[]{:S(2)}) collective-permute-start(f32[3,32,128]{2,1,0:T(8,128)} %get-tuple-element.15), channel_id=1, source_target_pairs={{0,2},{2,4},{4,6},{6,8},{8,10},{10,12},{12,14},{14,16},{16,18},{18... | collective-permute-start | bytes 147464 | tf_op jit(solution)/shard_map/ppermute | solution.py:13
  18.5 32.4 %copy-start.1 = (s32[512,96]{0,1:T(8,128)S(1)}, s32[512,96]{0,1:T(8,128)}, u32[]{:S(2)}) copy-start(s32[512,96]{0,1:T(8,128)} %param.16) | copy-start | bytes 589828
  18.5 10.8 %collective-permute-start.4 = (f32[3,32,128]{2,1,0:T(8,128)}, f32[3,32,128]{2,1,0:T(8,128)S(1)}, u32[]{:S(2)}, u32[]{:S(2)}) collective-permute-start(f32[3,32,128]{2,1,0:T(8,128)} %get-tuple-element.16), channel_id=1, source_target_pairs={{0,30},{2,0},{4,2},{6,4},{8,6},{10,8},{12,10},{14,12},{16,14},{18,... | collective-permute-start | bytes 147464 | tf_op jit(solution)/shard_map/ppermute | solution.py:13
  27.8 1.5 %copy-start.2 = (f32[96,128]{1,0:T(8,128)}, f32[96,128]{1,0:T(8,128)S(1)}, u32[]{:S(2)}) copy-start(f32[96,128]{1,0:T(8,128)S(1)} %collective-permute-done.1.x_left) | copy-start | bytes 147460
  27.9 1.5 %copy-start.3 = (f32[96,128]{1,0:T(8,128)}, f32[96,128]{1,0:T(8,128)S(1)}, u32[]{:S(2)}) copy-start(f32[96,128]{1,0:T(8,128)S(1)} %collective-permute-done.2.x_right) | copy-start | bytes 147460
  27.9 1.4 %copy-start.4 = (f32[3,32,128]{2,1,0:T(8,128)}, f32[3,32,128]{2,1,0:T(8,128)S(1)}, u32[]{:S(2)}) copy-start(f32[3,32,128]{2,1,0:T(8,128)S(1)} %collective-permute-done.3.y_before) | copy-start | bytes 147460
  29.3 0.6 copy-start.5
  29.9 0.7 copy-start
  38.1 21.1 %all-to-all-start = ((f32[32,40,128]{2,1,0:T(8,128)}), f32[32,40,128]{2,1,0:T(8,128)S(1)}, u32[]{:S(2)}, u32[]{:S(2)}) async-start(f32[32,40,128]{2,1,0:T(8,128)} %bitcast.33), calls=%async_computation | async-start | bytes 1310720 | tf_op jit(solution)/shard_map/all_to_all | solution.py:273
  46.1 10.5 %collective-permute-start.5 = (f32[128,128]{1,0:T(8,128)}, f32[128,128]{1,0:T(8,128)S(1)}, u32[]{:S(2)}, u32[]{:S(2)}) collective-permute-start(f32[128,128]{1,0:T(8,128)} %get-tuple-element.19), channel_id=1, source_target_pairs={{0,1},{1,0},{2,3},{3,2},{4,5},{5,4},{6,7},{7,6},{8,9},{9,8},{10,11... | collective-permute-start | bytes 196616 | tf_op jit(solution)/shard_map/ppermute | solution.py:13
  60.3 29.8 %all-to-all-start.1 = ((f32[16,18,128]{2,1,0:T(8,128)}), f32[16,18,128]{2,1,0:T(8,128)S(1)}, u32[]{:S(2)}, u32[]{:S(2)}) async-start(f32[16,18,128]{2,1,0:T(8,128)} %pad_maximum_fusion), calls=%async_computation.1 | async-start | bytes 393216 | tf_op jit(solution)/shard_map/all_to_all | solution.py:273
  90.8 31.5 %all-to-all-start.2 = ((f32[32,8,128]{2,1,0:T(8,128)}), f32[32,8,128]{2,1,0:T(8,128)S(1)}, u32[]{:S(2)}, u32[]{:S(2)}) async-start(f32[32,8,128]{2,1,0:T(8,128)} %broadcast_in_dim.5), calls=%async_computation.2 | async-start | bytes 262144 | tf_op jit(solution)/shard_map/all_to_all | solution.py:273

commit v4 on v3

--- a/solution.py
+++ b/solution.py
@@ -65,10 +65,10 @@
 
 
 def field_kernel(
-    phi_z, vel, far, below, above, x_left, x_right, y_before, y_after, omega_x, omega_y, omega_z, phi_x,
+    vel, far, below, above, x_left, x_right, y_before, y_after, omega_x, omega_y, omega_z, phi_x, phi_z,
     send, mine, theirs,
     padded, sides, x_held, y_held, wx_held, wy_held, wz_held, px_held,
-    q_terms, flat, flat_terms, wx, wyz, phx, part_y, part_z, lead, sems,
+    q_terms, flat, flat_terms, wx, wyz, phx, part_y, part_z, lead, pz_held, sems,
 ):
     gz = lax.axis_index("gz")
     middle = pl.ds(8, 96)
@@ -93,7 +93,8 @@
         pltpu.make_async_copy(omega_z, wz_held, sems.at[11]),
         pltpu.make_async_copy(phi_x, px_held, sems.at[12]),
     ]
-    for copy in x_copies + cells_copies + y_copies:
+    z_copy = pltpu.make_async_copy(phi_z, pz_held, sems.at[13])
+    for copy in x_copies + cells_copies + y_copies + [z_copy]:
         copy.start()
 
     @pl.when(gz == 0)
@@ -122,7 +123,7 @@
 
     lax.fori_loop(0, 16, place, 0, unroll=2)
 
-    for copy in y_copies + cells_copies:
+    for copy in y_copies + cells_copies + [z_copy]:
         copy.wait()
     for c in range(3):
         for k in range(16):
@@ -143,7 +144,7 @@
     lane = lax.broadcasted_iota(jnp.int32, (16, 128), 1)
 
     def plane(k, carry):
-        weight = [phi_z[c, k].astype(jnp.float32) for c in range(2)]
+        weight = [pz_held[c, k].astype(jnp.float32) for c in range(2)]
         for block in range(6):
             row = 16 * block
             at = row + 8
@@ -176,7 +177,7 @@
                 flat[96 * c + row : 96 * c + row + 16, :] += weight[c] * field
         return carry
 
-    lax.fori_loop(0, 16, plane, 0, unroll=2)
+    lax.fori_loop(0, 16, plane, 0, unroll=4)
 
     for copy in weight_copies:
         copy.wait()
@@ -206,9 +207,10 @@
     part_y[...] = total_y
 
     lane8 = lax.broadcasted_iota(jnp.int32, (8, 128), 1)
+    shares = [part_z[pl.ds(pl.multiple_of(8 * jnp.abs(z - gz), 8), 8), :] for z in range(2)]
     for g in range(16):
         for z in range(2):
-            base = 40 * (2 * g + z)
+            base = 52 * (2 * g + z)
             near = 32 * g + z
             send[base : base + 16, :] = lead[0, pl.ds(near, 16, stride=2), :]
             send[base + 16 : base + 24, :] = jnp.where(
@@ -218,9 +220,8 @@
             )
             for half in range(2):
                 lanes = slice(128 * half, 128 * half + 128)
-                send[base + 24 + 6 * half : base + 30 + 6 * half, :] = part_y[6 * g : 6 * g + 6, lanes]
-                send[base + 36 + half : base + 37 + half, :] = part_z[g : g + 1, lanes]
-            send[base + 38 : base + 40, :] = jnp.zeros((2, 128), jnp.float32)
+                send[base + 24 + 8 * half : base + 32 + 8 * half, :] = shares[z][:, lanes]
+                send[base + 40 + 6 * half : base + 46 + 6 * half, :] = part_y[6 * g : 6 * g + 6, lanes]
 
     turned = lax.dot_general(
         q_terms[...], wyz[...], (((0,), (0,)), ((), ())), preferred_element_type=jnp.float32
@@ -230,15 +231,15 @@
     theirs[...] = jnp.where(gz == 0, turned[:, 128:256], turned[:, 0:128])
 
 
-def field(phi_z, velocity, far, below, above, sides, omega_x, omega_y, omega_z, phi_x):
+def field(velocity, far, below, above, sides, omega_x, omega_y, omega_z, phi_x, phi_z):
     whole = pl.BlockSpec(memory_space=pltpu.VMEM)
     outside = pl.BlockSpec(memory_space=pl.ANY)
     half = jax.ShapeDtypeStruct((128, 128), jnp.float32)
     return pl.pallas_call(
         field_kernel,
-        in_specs=[pl.BlockSpec(memory_space=pltpu.SMEM)] + [outside] * 12,
+        in_specs=[outside] * 13,
         out_specs=[whole] * 3,
-        out_shape=[jax.ShapeDtypeStruct((1280, 128), jnp.float32), half, half],
+        out_shape=[jax.ShapeDtypeStruct((1664, 128), jnp.float32), half, half],
         scratch_shapes=[
             pltpu.VMEM((3, 20, 112, 128), jnp.float32),
             pltpu.VMEM((3, 16, 96, 128), jnp.float32),
@@ -257,11 +258,12 @@
             pltpu.VMEM((96, 256), jnp.float32),
             pltpu.VMEM((16, 256), jnp.float32),
             pltpu.VMEM((2, 512, 128), jnp.float32),
-            pltpu.SemaphoreType.DMA((13,)),
+            pltpu.SMEM((2, 16), jnp.int32),
+            pltpu.SemaphoreType.DMA((14,)),
         ],
         compiler_params=pltpu.CompilerParams(vmem_limit_bytes=60 * 1024 * 1024),
         name="field_products",
-    )(phi_z, velocity, far, below, above, *sides, omega_x, omega_y, omega_z, phi_x)
+    )(velocity, far, below, above, *sides, omega_x, omega_y, omega_z, phi_x, phi_z)
 
 
 def split(values):
@@ -286,12 +288,17 @@
         shift_permute(y_high, "gy", 1),
         shift_permute(y_low, "gy", -1),
     ]
-    send, mine, theirs = field(phi_z, velocity, far, below, above, sides, omega_x, omega_y, omega_z, phi_x)
-    got = exchange(send, ("gx", "gz")).reshape(16, 2, 40, 128)
+    send, mine, theirs = field(velocity, far, below, above, sides, omega_x, omega_y, omega_z, phi_x, phi_z)
+    got = exchange(send, ("gx", "gz")).reshape(16, 2, 52, 128)
     part_x = mine + shift_permute(theirs, "gz", 1)
 
-    summed = jnp.sum(got, axis=(0, 1))
-    summed_z = jnp.sum(lax.dynamic_index_in_dim(got, gz, 1, keepdims=False)[:, 36:38], axis=0)
+    by_z = jnp.sum(got, axis=0)
+    summed = by_z[0] + by_z[1]
+    same = jnp.where(gz == 0, by_z[0, 24:40], by_z[1, 24:40])
+    cross = jnp.where(gz == 0, by_z[1, 24:40], by_z[0, 24:40])
+    rows_z = jnp.concatenate(
+        [same.reshape(2, 8, 128).transpose(1, 0, 2), cross.reshape(2, 8, 128).transpose(1, 0, 2)], axis=0
+    )
     rest = jnp.concatenate([summed[16:24, :64], summed[16:24, 64:]], axis=0)
     lead_high, lead_low = split(jnp.concatenate([summed[:16], rest], axis=1))
     wide = phi_y.T.astype(jnp.bfloat16)
@@ -301,22 +308,22 @@
     )
     core = jnp.dot(jnp.concatenate([lead_high, lead_low], axis=0), wide, preferred_element_type=jnp.float32)
     core = (core[:16] + core[16:]).reshape(16, 8, 128)
-    send = jnp.concatenate(
-        [core, part_x.reshape(16, 8, 128), jnp.broadcast_to(summed_z[None], (16, 2, 128))], axis=1
-    )
+    send = jnp.concatenate([core, part_x.reshape(16, 8, 128), rows_z], axis=1)
     got = jnp.sum(exchange(send.reshape(288, 128), "gy").reshape(16, 18, 128), axis=0)
     core_sketch = got[:8].reshape(1, 2, 512) * (1.0 / math.sqrt(total_x * total_y * total_z))
 
-    got_y = lax.all_gather(summed[24:40], "gx", axis=0, tiled=True).reshape(16, 16, 128)
-    factor_y = got_y[:, :12].reshape(16, 2, 6, 128).transpose(0, 2, 1, 3).reshape(96, 256)
+    got_y = lax.all_gather(summed[40:52], "gx", axis=0, tiled=True).reshape(16, 2, 6, 128)
+    factor_y = got_y.transpose(0, 2, 1, 3).reshape(96, 256)
     factor_y = factor_y * (1.0 / math.sqrt(total_x * total_z))
 
-    got_z = lax.all_gather(got[16:18], "gx", axis=0, tiled=True)
-    factor_z = got_z.reshape(16, 256) * (1.0 / math.sqrt(total_x * total_y))
-
-    got_x = exchange(jnp.broadcast_to(got[None, 8:16], (32, 8, 128)).reshape(256, 128), ("gy", "gz"))
-    factor_x = got_x.reshape(16, 2, 8, 128).transpose(0, 2, 1, 3).reshape(128, 256)
+    got_x = exchange(jnp.broadcast_to(got[None, 8:18], (32, 10, 128)).reshape(320, 128), ("gy", "gz"))
+    got_x = got_x.reshape(16, 2, 10, 128)
+    factor_x = got_x[:, :, :8].transpose(0, 2, 1, 3).reshape(128, 256)
     factor_x = factor_x * (1.0 / math.sqrt(total_y * total_z))
+    first, second = got_x[:, 0, 8:], got_x[:, 1, 8:]
+    same = jnp.where(gz == 0, first[:8], second[:8])
+    cross = jnp.where(gz == 0, second[8:], first[8:])
+    factor_z = jnp.concatenate([same, cross], axis=0).reshape(16, 256) * (1.0 / math.sqrt(total_x * total_y))
     return (factor_x, factor_y, factor_z, core_sketch)
 
 

time: 124 us -> 120 us (0.968)
  starting transfers between devices: 59.3 us -> 46.6 us
  waiting for transfers between devices: 8.8 us -> 13.4 us
  blocking collectives: 36.6 us -> 40.2 us
  local copies, waits for them, and re-layouts: 4.05 us -> 6.46 us
  other arithmetic: 2.43 us -> 1.16 us
    all_to_all x0 -> x1, blocking collectives: none -> 21.6 us  [exchange(): return lax.all_to_all(rows, axes, 0, 0, tiled=True)]
    all_gather x2 -> x1, blocking collectives: 36.6 us -> 18.6 us  [shards(): lax.all_gather(summed[40:52], 'gx', axis=0, tiled=True)]
    all_to_all x3 -> x2, starting transfers between devices: 30.6 us -> 18.1 us  [exchange(): return lax.all_to_all(rows, axes, 0, 0, tiled=True)]
    ppermute x6, waiting for transfers between devices: 7.1 us -> 9.75 us  [shift_permute(): lax.ppermute(cells, axis, [(i, (i + step) % count) for i in range(count)])]
    all_to_all x0 -> x2, local copies, waits for them, and re-layouts: none -> 2.24 us  [exchange(): return lax.all_to_all(rows, axes, 0, 0, tiled=True)]
    all_to_all x3 -> x2, waiting for transfers between devices: 1.71 us -> 3.69 us  [exchange(): return lax.all_to_all(rows, axes, 0, 0, tiled=True)]
    unnamed x16 -> x18, local copies, waits for them, and re-layouts: 2.59 us -> 1.99 us
  transfers between devices with their start and end apart: 9 -> 8, of which waited for: 3 -> 4; matrix products, arithmetic and copies ran while one was open for 2% -> 1% of each run, Pallas kernels for 0% -> 0%
where the time goes in v4:
time: 120 us; the launch traced here: 119 us
  starting transfers between devices  46.6 us (39%)
  blocking collectives  40.2 us (34%)
  waiting for transfers between devices  13.4 us (11%)
  Pallas kernels  9.86 us (8%)
  local copies, waits for them, and re-layouts  6.46 us (5%)
    ppermute x6, starting transfers between devices, shift_permute(): lax.ppermute(cells, axis, [(i, (i + step) % count) for i in range(count)])  28.6 us
    all_to_all x1, blocking collectives, exchange(): return lax.all_to_all(rows, axes, 0, 0, tiled=True)  21.6 us
    all_gather x1, blocking collectives, shards(): lax.all_gather(summed[40:52], 'gx', axis=0, tiled=True)  18.6 us
    all_to_all x2, starting transfers between devices, exchange(): return lax.all_to_all(rows, axes, 0, 0, tiled=True)  18.1 us
    ppermute x6, waiting for transfers between devices, shift_permute(): lax.ppermute(cells, axis, [(i, (i + step) % count) for i in range(count)])  9.75 us
    pallas_call x1, Pallas kernels, field(): pl.pallas_call(field_kernel, in_specs=[outside] * 13, out_specs=[whole] *...  6.6 us
    all_to_all x2, waiting for transfers between devices, exchange(): return lax.all_to_all(rows, axes, 0, 0, tiled=True)  3.69 us
    pallas_call x1, Pallas kernels, pack(): pl.pallas_call(pack_kernel, in_specs=[outside], out_specs=[outside] + [wh...  3.26 us
  transfers between devices with their start and end apart: 8, of which 4 were waited for; matrix products, arithmetic and copies ran while one was open for 1% of the time, Pallas kernels for 0%

profile of v4, /device:TPU:1, one launch (start us, length us, event | category | flops | bytes accessed | tf_op | source)
XLA Modules:
  0.0 118.8 jit_solution(1489404197281257666)
XLA Ops:
  0.6 3.3 %pack_halos.1 = (f32[3,2,96,128]{3,2,1,0:T(8,128)}, f32[96,128]{1,0:T(8,128)}, f32[96,128]{1,0:T(8,128)}, f32[3,32,128]{2,1,0:T(8,128)}, f32[3,32,128]{2,1,0:T(8,128)}) custom-call(f32[3,16,96,128]{3,2,1,0:T(8,128)} %vel.3), custom_call_target="tpu_custom_call" | custom-call | tf_op jit(solution)/shard_map/pack_halos/pallas_call | solution.py:56
  3.9 5.7 %collective-permute-start = (f32[3,2,96,128]{3,2,1,0:T(8,128)}, f32[3,2,96,128]{3,2,1,0:T(8,128)S(1)}, u32[]{:S(2)}, u32[]{:S(2)}) collective-permute-start(f32[3,2,96,128]{3,2,1,0:T(8,128)} %get-tuple-element.12), channel_id=1, source_target_pairs={{0,1},{1,0},{2,3},{3,2},{4,5},{5,4},{6,7},{7,6},{8,9},{9,8},{10,11... | collective-permute-start | bytes 884744 | tf_op jit(solution)/shard_map/ppermute | solution.py:13
  9.6 3.1 %collective-permute-start.1 = (f32[96,128]{1,0:T(8,128)}, f32[96,128]{1,0:T(8,128)S(1)}, u32[]{:S(2)}, u32[]{:S(2)}) collective-permute-start(f32[96,128]{1,0:T(8,128)} %get-tuple-element.13), channel_id=1, source_target_pairs={{0,32},{32,64},{64,96},{96,128},{128,160},{160,192},{192,224},{224... | collective-permute-start | bytes 147464 | tf_op jit(solution)/shard_map/ppermute | solution.py:13
  12.7 3.8 %collective-permute-start.2 = (f32[96,128]{1,0:T(8,128)}, f32[96,128]{1,0:T(8,128)S(1)}, u32[]{:S(2)}, u32[]{:S(2)}) collective-permute-start(f32[96,128]{1,0:T(8,128)} %get-tuple-element.14), channel_id=1, source_target_pairs={{0,480},{32,0},{64,32},{96,64},{128,96},{160,128},{192,160},{224,1... | collective-permute-start | bytes 147464 | tf_op jit(solution)/shard_map/ppermute | solution.py:13
  16.5 1.9 %collective-permute-start.3 = (f32[3,32,128]{2,1,0:T(8,128)}, f32[3,32,128]{2,1,0:T(8,128)S(1)}, u32[]{:S(2)}, u32[]{:S(2)}) collective-permute-start(f32[3,32,128]{2,1,0:T(8,128)} %get-tuple-element.15), channel_id=1, source_target_pairs={{0,2},{2,4},{4,6},{6,8},{8,10},{10,12},{12,14},{14,16},{16,18},{18... | collective-permute-start | bytes 147464 | tf_op jit(solution)/shard_map/ppermute | solution.py:13
  18.5 9.2 %collective-permute-start.4 = (f32[3,32,128]{2,1,0:T(8,128)}, f32[3,32,128]{2,1,0:T(8,128)S(1)}, u32[]{:S(2)}, u32[]{:S(2)}) collective-permute-start(f32[3,32,128]{2,1,0:T(8,128)} %get-tuple-element.16), channel_id=1, source_target_pairs={{0,30},{2,0},{4,2},{6,4},{8,6},{10,8},{12,10},{14,12},{16,14},{18,... | collective-permute-start | bytes 147464 | tf_op jit(solution)/shard_map/ppermute | solution.py:13
  27.7 0.0 collective-permute-done.1.x_left
  27.7 0.0 copy-start.3
  27.7 0.0 collective-permute-done.2.x_right
  27.7 0.0 copy-start.4
  27.7 0.0 collective-permute-done.3.y_before
  27.7 0.0 copy-start.5
  27.8 1.4 %collective-permute-done.4.y_after = f32[3,32,128]{2,1,0:T(8,128)S(1)} collective-permute-done((f32[3,32,128]{2,1,0:T(8,128)}, f32[3,32,128]{2,1,0:T(8,128)S(1)}, u32[]{:S(2)}, u32[]{:S(2)}) %collective-permute-start.4) | collective-permute-done | bytes 49184 | tf_op jit(solution)/shard_map/ppermute | solution.py:13
  29.2 0.0 copy-start.6
  29.2 0.0 collective-permute-done.far
  29.2 0.0 copy-done.3
  29.2 0.0 copy-done.4
  29.2 0.0 copy-done.5
  29.2 0.6 copy-done.6
  29.8 0.7 copy-done
  30.5 6.6 %field_products.1 = (f32[1664,128]{1,0:T(8,128)}, f32[128,128]{1,0:T(8,128)}, f32[128,128]{1,0:T(8,128)}) custom-call(f32[3,16,96,128]{3,2,1,0:T(8,128)} %vel.3, f32[3,2,96,128]{3,2,1,0:T(8,128)} %copy-done, f32[3,2,96,128]{3,2,1,0:T(8,128)} %below.1, f32[3,2,96,128]{3,2,1,0:T(8,128)} %above.1, f32[96,128]{1,0:T(8,128)} %copy-done.3, f32[96,128]{1,0:T(8,128)} %copy-done.4, ...), custom_call_target="tpu_custom_call" | custom-call | tf_op jit(solution)/shard_map/field_products/pallas_call | solution.py:238
  37.1 0.0 copy-start.7
  37.1 0.0 copy-start.1
  37.1 0.0 copy-start.2
  37.1 2.2 %all_to_all.14 = f32[32,52,128]{2,1,0:T(8,128)} reshape(f32[1664,128]{1,0:T(8,128)} %get-tuple-element.17) | data formatting | bytes 1703936 | tf_op jit(solution)/shard_map/all_to_all | solution.py:275
  39.3 8.0 %all-to-all-start = ((f32[32,52,128]{2,1,0:T(8,128)}), f32[32,52,128]{2,1,0:T(8,128)S(1)}, u32[]{:S(2)}, u32[]{:S(2)}) async-start(f32[32,52,128]{2,1,0:T(8,128)} %all_to_all.14), calls=%async_computation | async-start | bytes 1835008 | tf_op jit(solution)/shard_map/all_to_all | solution.py:275
  47.3 0.0 copy-done.7
  47.3 4.8 %collective-permute-start.5 = (f32[128,128]{1,0:T(8,128)S(1)}, f32[128,128]{1,0:T(8,128)S(1)}, u32[]{:S(2)}, u32[]{:S(2)}) collective-permute-start(f32[128,128]{1,0:T(8,128)S(1)} %copy-done.7), channel_id=1, source_target_pairs={{0,1},{1,0},{2,3},{3,2},{4,5},{5,4},{6,7},{7,6},{8,9},{9,8},{10,11... | collective-permute-start | bytes 196616 | tf_op jit(solution)/shard_map/ppermute | solution.py:13
  52.1 0.0 copy-done.1
  52.2 8.3 %collective-permute-done.5 = f32[128,128]{1,0:T(8,128)S(1)} collective-permute-done((f32[128,128]{1,0:T(8,128)S(1)}, f32[128,128]{1,0:T(8,128)S(1)}, u32[]{:S(2)}, u32[]{:S(2)}) %collective-permute-start.5) | collective-permute-done | bytes 65568 | tf_op jit(solution)/shard_map/ppermute | solution.py:13
  60.5 0.0 copy-done.2
  60.5 3.2 %all-to-all-done = f32[32,52,128]{2,1,0:T(8,128)S(1)} async-done(((f32[32,52,128]{2,1,0:T(8,128)}), f32[32,52,128]{2,1,0:T(8,128)S(1)}, u32[]{:S(2)}, u32[]{:S(2)}) %all-to-all-start) | async-done | bytes 852000 | tf_op jit(solution)/shard_map/all_to_all | solution.py:275
  63.7 0.1 reduce_sum.18
  63.8 0.1 fusion.19
  63.9 0.1 fusion.3
  64.1 21.6 %all_to_all.21 = f32[16,18,128]{2,1,0:T(8,128)S(1)} all-to-all(f32[16,18,128]{2,1,0:T(8,128)S(1)} %pad_maximum_fusion), channel_id=1, replica_groups=mesh['gx'=16,'gy'=16,'gz'=2] {'gy'}, dimensions={0} | all-to-all | bytes 294912 | tf_op jit(solution)/shard_map/all_to_all | solution.py:275
  85.8 0.7 broadcast_in_dim.2
  86.5 10.1 %all-to-all-start.2 = ((f32[32,10,128]{2,1,0:T(8,128)}), f32[32,10,128]{2,1,0:T(8,128)S(1)}, u32[]{:S(2)}, u32[]{:S(2)}) async-start(f32[32,10,128]{2,1,0:T(8,128)} %broadcast_in_dim.2), calls=%async_computation.2 | async-start | bytes 524288 | tf_op jit(solution)/shard_map/all_to_all | solution.py:275
  96.6 18.6 %all-gather = f32[1,192,128]{2,0,1:T(1,128)S(1)} all-gather(f32[1,12,128]{2,0,1:T(1,128)S(1)} %copy.21), channel_id=2, replica_groups=mesh['gx'=16,'gy'=16,'gz'=2] {'gx'}, dimensions={1}, use_global_device_ids=true | all-gather | bytes 104448 | tf_op jit(solution)/shard_map/all_gather | solution.py:315
  115.2 0.3 multiply_reduce_fusion
  115.5 0.1 copy.22
  115.6 0.6 copy.31
  116.2 0.6 mul.63
  116.8 0.5 all-to-all-done.2
  117.3 0.1 copy.19
  117.4 0.1 fusion.10
  117.5 0.7 copy.30
  118.2 0.6 maximum_multiply_fusion
  (20 shorter events, 0.2 us)
Async XLA Ops:
  3.9 25.3 %collective-permute-start = (f32[3,2,96,128]{3,2,1,0:T(8,128)}, f32[3,2,96,128]{3,2,1,0:T(8,128)S(1)}, u32[]{:S(2)}, u32[]{:S(2)}) collective-permute-start(f32[3,2,96,128]{3,2,1,0:T(8,128)} %get-tuple-element.12), channel_id=1, source_target_pairs={{0,1},{1,0},{2,3},{3,2},{4,5},{5,4},{6,7},{7,6},{8,9},{9,8},{10,11... | collective-permute-start | bytes 884744 | tf_op jit(solution)/shard_map/ppermute | solution.py:13
  9.6 18.1 %collective-permute-start.1 = (f32[96,128]{1,0:T(8,128)}, f32[96,128]{1,0:T(8,128)S(1)}, u32[]{:S(2)}, u32[]{:S(2)}) collective-permute-start(f32[96,128]{1,0:T(8,128)} %get-tuple-element.13), channel_id=1, source_target_pairs={{0,32},{32,64},{64,96},{96,128},{128,160},{160,192},{192,224},{224... | collective-permute-start | bytes 147464 | tf_op jit(solution)/shard_map/ppermute | solution.py:13
  12.7 15.0 %collective-permute-start.2 = (f32[96,128]{1,0:T(8,128)}, f32[96,128]{1,0:T(8,128)S(1)}, u32[]{:S(2)}, u32[]{:S(2)}) collective-permute-start(f32[96,128]{1,0:T(8,128)} %get-tuple-element.14), channel_id=1, source_target_pairs={{0,480},{32,0},{64,32},{96,64},{128,96},{160,128},{192,160},{224,1... | collective-permute-start | bytes 147464 | tf_op jit(solution)/shard_map/ppermute | solution.py:13
  16.5 11.2 %collective-permute-start.3 = (f32[3,32,128]{2,1,0:T(8,128)}, f32[3,32,128]{2,1,0:T(8,128)S(1)}, u32[]{:S(2)}, u32[]{:S(2)}) collective-permute-start(f32[3,32,128]{2,1,0:T(8,128)} %get-tuple-element.15), channel_id=1, source_target_pairs={{0,2},{2,4},{4,6},{6,8},{8,10},{10,12},{12,14},{14,16},{16,18},{18... | collective-permute-start | bytes 147464 | tf_op jit(solution)/shard_map/ppermute | solution.py:13
  18.5 10.7 %collective-permute-start.4 = (f32[3,32,128]{2,1,0:T(8,128)}, f32[3,32,128]{2,1,0:T(8,128)S(1)}, u32[]{:S(2)}, u32[]{:S(2)}) collective-permute-start(f32[3,32,128]{2,1,0:T(8,128)} %get-tuple-element.16), channel_id=1, source_target_pairs={{0,30},{2,0},{4,2},{6,4},{8,6},{10,8},{12,10},{14,12},{16,14},{18,... | collective-permute-start | bytes 147464 | tf_op jit(solution)/shard_map/ppermute | solution.py:13
  27.7 1.5 %copy-start.3 = (f32[96,128]{1,0:T(8,128)}, f32[96,128]{1,0:T(8,128)S(1)}, u32[]{:S(2)}) copy-start(f32[96,128]{1,0:T(8,128)S(1)} %collective-permute-done.1.x_left) | copy-start | bytes 147460
  27.7 1.5 %copy-start.4 = (f32[96,128]{1,0:T(8,128)}, f32[96,128]{1,0:T(8,128)S(1)}, u32[]{:S(2)}) copy-start(f32[96,128]{1,0:T(8,128)S(1)} %collective-permute-done.2.x_right) | copy-start | bytes 147460
  27.7 1.4 %copy-start.5 = (f32[3,32,128]{2,1,0:T(8,128)}, f32[3,32,128]{2,1,0:T(8,128)S(1)}, u32[]{:S(2)}) copy-start(f32[3,32,128]{2,1,0:T(8,128)S(1)} %collective-permute-done.3.y_before) | copy-start | bytes 147460
  29.2 0.6 copy-start.6
  29.8 0.7 copy-start
  37.1 10.2 %copy-start.7 = (f32[128,128]{1,0:T(8,128)S(1)}, f32[128,128]{1,0:T(8,128)}, u32[]{:S(2)}) copy-start(f32[128,128]{1,0:T(8,128)} %get-tuple-element.19) | copy-start | bytes 196612
  37.1 15.0 %copy-start.1 = (s32[512,96]{0,1:T(8,128)S(1)}, s32[512,96]{0,1:T(8,128)}, u32[]{:S(2)}) copy-start(s32[512,96]{0,1:T(8,128)} %param.16) | copy-start | bytes 589828
  37.1 23.4 %copy-start.2 = (f32[128,128]{1,0:T(8,128)S(1)}, f32[128,128]{1,0:T(8,128)}, u32[]{:S(2)}) copy-start(f32[128,128]{1,0:T(8,128)} %get-tuple-element.18) | copy-start | bytes 196612
  39.3 24.4 %all-to-all-start = ((f32[32,52,128]{2,1,0:T(8,128)}), f32[32,52,128]{2,1,0:T(8,128)S(1)}, u32[]{:S(2)}, u32[]{:S(2)}) async-start(f32[32,52,128]{2,1,0:T(8,128)} %all_to_all.14), calls=%async_computation | async-start | bytes 1835008 | tf_op jit(solution)/shard_map/all_to_all | solution.py:275
  47.3 13.2 %collective-permute-start.5 = (f32[128,128]{1,0:T(8,128)S(1)}, f32[128,128]{1,0:T(8,128)S(1)}, u32[]{:S(2)}, u32[]{:S(2)}) collective-permute-start(f32[128,128]{1,0:T(8,128)S(1)} %copy-done.7), channel_id=1, source_target_pairs={{0,1},{1,0},{2,3},{3,2},{4,5},{5,4},{6,7},{7,6},{8,9},{9,8},{10,11... | collective-permute-start | bytes 196616 | tf_op jit(solution)/shard_map/ppermute | solution.py:13
  86.5 30.9 %all-to-all-start.2 = ((f32[32,10,128]{2,1,0:T(8,128)}), f32[32,10,128]{2,1,0:T(8,128)S(1)}, u32[]{:S(2)}, u32[]{:S(2)}) async-start(f32[32,10,128]{2,1,0:T(8,128)} %broadcast_in_dim.2), calls=%async_computation.2 | async-start | bytes 524288 | tf_op jit(solution)/shard_map/all_to_all | solution.py:275

commit v5 on v4

--- a/solution.py
+++ b/solution.py
@@ -13,8 +13,18 @@
     return lax.ppermute(cells, axis, [(i, (i + step) % count) for i in range(count)])
 
 
-def pack_kernel(vel, near, x_high, x_low, y_high, y_low, held, sems):
+def edge_swap(cells, axis, odd):
+    count = lax.axis_size(axis)
+    pairs = []
+    for i in range(odd, count + odd, 2):
+        pairs += [(i % count, (i + 1) % count), ((i + 1) % count, i % count)]
+    return lax.ppermute(cells, axis, pairs)
+
+
+def pack_kernel(vel, near, x_even, x_odd, y_even, y_odd, held, sems):
     gz = lax.axis_index("gz")
+    odd_x = lax.rem(lax.axis_index("gx"), 2) == 1
+    odd_y = lax.rem(lax.axis_index("gy"), 2) == 1
     copies = [
         pltpu.make_async_copy(
             vel.at[part // 2, pl.ds(8 * (part % 2), 8)], held.at[part // 2, pl.ds(8 * (part % 2), 8)], sems.at[part]
@@ -40,10 +50,12 @@
             turned = pltpu.roll(held[c, k], spot + 2, 1)
             high = jnp.where((lane >= spot) & (lane < spot + 2), turned, high)
             low = jnp.where((lane >= spot + 2) & (lane < spot + 4), turned, low)
-            y_low[c, 2 * k : 2 * k + 2, :] = held[c, k, 0:2, :]
-            y_high[c, 2 * k : 2 * k + 2, :] = held[c, k, 94:96, :]
-    x_high[...] = high
-    x_low[...] = low
+            first = held[c, k, 0:2, :]
+            last = held[c, k, 94:96, :]
+            y_even[c, 2 * k : 2 * k + 2, :] = jnp.where(odd_y, first, last)
+            y_odd[c, 2 * k : 2 * k + 2, :] = jnp.where(odd_y, last, first)
+    x_even[...] = jnp.where(odd_x, low, high)
+    x_odd[...] = jnp.where(odd_x, high, low)
     for rim in rims:
         rim.wait()
 
@@ -65,20 +77,22 @@
 
 
 def field_kernel(
-    vel, far, below, above, x_left, x_right, y_before, y_after, omega_x, omega_y, omega_z, phi_x, phi_z,
+    vel, far, below, above, x_even, x_odd, y_even, y_odd, omega_x, omega_y, omega_z, phi_x, phi_z,
     send, mine, theirs,
     padded, sides, x_held, y_held, wx_held, wy_held, wz_held, px_held,
     q_terms, flat, flat_terms, wx, wyz, phx, part_y, part_z, lead, pz_held, sems,
 ):
     gz = lax.axis_index("gz")
+    odd_x = lax.rem(lax.axis_index("gx"), 2)
+    odd_y = lax.rem(lax.axis_index("gy"), 2)
     middle = pl.ds(8, 96)
     x_copies = [
-        pltpu.make_async_copy(x_left, x_held.at[0], sems.at[0]),
-        pltpu.make_async_copy(x_right, x_held.at[1], sems.at[1]),
+        pltpu.make_async_copy(x_even, x_held.at[1 - odd_x], sems.at[0]),
+        pltpu.make_async_copy(x_odd, x_held.at[odd_x], sems.at[1]),
     ]
     y_copies = [
-        pltpu.make_async_copy(y_before, y_held.at[0], sems.at[2]),
-        pltpu.make_async_copy(y_after, y_held.at[1], sems.at[3]),
+        pltpu.make_async_copy(y_even, y_held.at[1 - odd_y], sems.at[2]),
+        pltpu.make_async_copy(y_odd, y_held.at[odd_y], sems.at[3]),
     ]
     cells_copies = [
         pltpu.make_async_copy(vel.at[c], padded.at[c, pl.ds(2, 16), middle, :], sems.at[4 + c]) for c in range(3)
@@ -210,7 +224,8 @@
     shares = [part_z[pl.ds(pl.multiple_of(8 * jnp.abs(z - gz), 8), 8), :] for z in range(2)]
     for g in range(16):
         for z in range(2):
-            base = 52 * (2 * g + z)
+            chunk = 2 * g + z
+            base = 48 * chunk
             near = 32 * g + z
             send[base : base + 16, :] = lead[0, pl.ds(near, 16, stride=2), :]
             send[base + 16 : base + 24, :] = jnp.where(
@@ -221,7 +236,8 @@
             for half in range(2):
                 lanes = slice(128 * half, 128 * half + 128)
                 send[base + 24 + 8 * half : base + 32 + 8 * half, :] = shares[z][:, lanes]
-                send[base + 40 + 6 * half : base + 46 + 6 * half, :] = part_y[6 * g : 6 * g + 6, lanes]
+                send[base + 40 + 3 * half : base + 43 + 3 * half, :] = part_y[3 * chunk : 3 * chunk + 3, lanes]
+            send[base + 46 : base + 48, :] = jnp.zeros((2, 128), jnp.float32)
 
     turned = lax.dot_general(
         q_terms[...], wyz[...], (((0,), (0,)), ((), ())), preferred_element_type=jnp.float32
@@ -239,7 +255,7 @@
         field_kernel,
         in_specs=[outside] * 13,
         out_specs=[whole] * 3,
-        out_shape=[jax.ShapeDtypeStruct((1664, 128), jnp.float32), half, half],
+        out_shape=[jax.ShapeDtypeStruct((1536, 128), jnp.float32), half, half],
         scratch_shapes=[
             pltpu.VMEM((3, 20, 112, 128), jnp.float32),
             pltpu.VMEM((3, 16, 96, 128), jnp.float32),
@@ -280,16 +296,16 @@
     total_y = 1536
     total_z = 32
     gz = lax.axis_index("gz")
-    near, x_high, x_low, y_high, y_low = pack(velocity)
+    near, x_even, x_odd, y_even, y_odd = pack(velocity)
     far = shift_permute(near, "gz", 1)
     sides = [
-        shift_permute(x_high, "gx", 1),
-        shift_permute(x_low, "gx", -1),
-        shift_permute(y_high, "gy", 1),
-        shift_permute(y_low, "gy", -1),
+        edge_swap(x_even, "gx", 0),
+        edge_swap(x_odd, "gx", 1),
+        edge_swap(y_even, "gy", 0),
+        edge_swap(y_odd, "gy", 1),
     ]
     send, mine, theirs = field(velocity, far, below, above, sides, omega_x, omega_y, omega_z, phi_x, phi_z)
-    got = exchange(send, ("gx", "gz")).reshape(16, 2, 52, 128)
+    got = exchange(send, ("gx", "gz")).reshape(16, 2, 48, 128)
     part_x = mine + shift_permute(theirs, "gz", 1)
 
     by_z = jnp.sum(got, axis=0)
@@ -309,14 +325,16 @@
     core = jnp.dot(jnp.concatenate([lead_high, lead_low], axis=0), wide, preferred_element_type=jnp.float32)
     core = (core[:16] + core[16:]).reshape(16, 8, 128)
     send = jnp.concatenate([core, part_x.reshape(16, 8, 128), rows_z], axis=1)
-    got = jnp.sum(exchange(send.reshape(288, 128), "gy").reshape(16, 18, 128), axis=0)
+    got = jnp.sum(exchange(send.reshape(16, 9, 2, 128), "gy"), axis=0).reshape(18, 128)
     core_sketch = got[:8].reshape(1, 2, 512) * (1.0 / math.sqrt(total_x * total_y * total_z))
 
-    got_y = lax.all_gather(summed[40:52], "gx", axis=0, tiled=True).reshape(16, 2, 6, 128)
-    factor_y = got_y.transpose(0, 2, 1, 3).reshape(96, 256)
-    factor_y = factor_y * (1.0 / math.sqrt(total_x * total_z))
-
-    got_x = exchange(jnp.broadcast_to(got[None, 8:18], (32, 10, 128)).reshape(320, 128), ("gy", "gz"))
+    got_y = lax.all_gather(summed[40:46], "gx", axis=0, tiled=True)
+    rows, got_y = lax.optimization_barrier((got[8:18], got_y))
+    other_y = shift_permute(got_y, "gz", 1)
+    halves = [jnp.where(gz == z, got_y, other_y).reshape(16, 2, 3, 128).transpose(0, 2, 1, 3) for z in range(2)]
+    factor_y = jnp.stack(halves, axis=1).reshape(96, 256) * (1.0 / math.sqrt(total_x * total_z))
+
+    got_x = exchange(jnp.broadcast_to(rows.reshape(1, 5, 2, 128), (32, 5, 2, 128)), ("gy", "gz"))
     got_x = got_x.reshape(16, 2, 10, 128)
     factor_x = got_x[:, :, :8].transpose(0, 2, 1, 3).reshape(128, 256)
     factor_x = factor_x * (1.0 / math.sqrt(total_y * total_z))

time: 120 us -> 123 us (1.025)
  blocking collectives: 40.2 us -> 19.9 us
  starting transfers between devices: 46.6 us -> 63.4 us
  waiting for transfers between devices: 13.4 us -> 21.7 us
  local copies, waits for them, and re-layouts: 6.46 us -> 5 us
    all_to_all x1 -> x0, blocking collectives: 21.6 us -> none  [exchange(): return lax.all_to_all(rows, axes, 0, 0, tiled=True)]
    ppermute x0 -> x4, starting transfers between devices: none -> 19 us  [edge_swap(): return lax.ppermute(cells, axis, pairs)]
    ppermute x6 -> x3, starting transfers between devices: 28.6 us -> 15.1 us  [shift_permute(): lax.ppermute(cells, axis, [(i, (i + step) % count) for i in range(count)])]
    all_to_all x2 -> x3, starting transfers between devices: 18.1 us -> 29.3 us  [exchange(): return lax.all_to_all(rows, axes, 0, 0, tiled=True)]
    all_to_all x2 -> x3, waiting for transfers between devices: 3.69 us -> 11.5 us  [exchange(): return lax.all_to_all(rows, axes, 0, 0, tiled=True)]
    all_to_all x2 -> x1, local copies, waits for them, and re-layouts: 2.24 us -> 0.01 us  [exchange(): return lax.all_to_all(rows, axes, 0, 0, tiled=True)]
    ppermute x0 -> x4, waiting for transfers between devices: none -> 1.62 us  [edge_swap(): return lax.ppermute(cells, axis, pairs)]
    all_gather x1, blocking collectives: 18.6 us -> 19.9 us  [shards(): got_y = lax.all_gather(summed[40:46], 'gx', axis=0, tiled=True)]
  transfers between devices with their start and end apart: 8 -> 10, of which waited for: 4 -> 5; matrix products, arithmetic and copies ran while one was open for 1% -> 2% of each run, Pallas kernels for 0% -> 0%
where the time goes in v5:
time: 123 us
  starting transfers between devices  63.4 us (52%)
  waiting for transfers between devices  21.7 us (18%)
  blocking collectives  19.9 us (16%)
  Pallas kernels  9.79 us (8%)
  local copies, waits for them, and re-layouts  5 us (4%)
  other arithmetic  1.77 us (1%)
    all_to_all x3, starting transfers between devices, exchange(): return lax.all_to_all(rows, axes, 0, 0, tiled=True)  29.3 us
    all_gather x1, blocking collectives, shards(): got_y = lax.all_gather(summed[40:46], 'gx', axis=0, tiled=True)  19.9 us
    ppermute x4, starting transfers between devices, edge_swap(): return lax.ppermute(cells, axis, pairs)  19 us
    ppermute x3, starting transfers between devices, shift_permute(): lax.ppermute(cells, axis, [(i, (i + step) % count) for i in range(count)])  15.1 us
    all_to_all x3, waiting for transfers between devices, exchange(): return lax.all_to_all(rows, axes, 0, 0, tiled=True)  11.5 us
    ppermute x3, waiting for transfers between devices, shift_permute(): lax.ppermute(cells, axis, [(i, (i + step) % count) for i in range(count)])  8.59 us
    pallas_call x1, Pallas kernels, field(): pl.pallas_call(field_kernel, in_specs=[outside] * 13, out_specs=[whole] *...  6.54 us
    pallas_call x1, Pallas kernels, pack(): pl.pallas_call(pack_kernel, in_specs=[outside], out_specs=[outside] + [wh...  3.25 us
  transfers between devices with their start and end apart: 10, of which 5 were waited for; matrix products, arithmetic and copies ran while one was open for 2% of the time, Pallas kernels for 0%

profile of v5, /device:TPU:1, one launch (start us, length us, event | category | flops | bytes accessed | tf_op | source)
XLA Modules:
  0.0 122.6 jit_solution(3017828396514439586)
XLA Ops:
  0.6 3.2 %pack_halos.1 = (f32[3,2,96,128]{3,2,1,0:T(8,128)}, f32[96,128]{1,0:T(8,128)}, f32[96,128]{1,0:T(8,128)}, f32[3,32,128]{2,1,0:T(8,128)}, f32[3,32,128]{2,1,0:T(8,128)}) custom-call(f32[3,16,96,128]{3,2,1,0:T(8,128)} %vel.3), custom_call_target="tpu_custom_call" | custom-call | tf_op jit(solution)/shard_map/pack_halos/pallas_call | solution.py:68
  3.9 5.7 %collective-permute-start = (f32[3,2,96,128]{3,2,1,0:T(8,128)}, f32[3,2,96,128]{3,2,1,0:T(8,128)S(1)}, u32[]{:S(2)}, u32[]{:S(2)}) collective-permute-start(f32[3,2,96,128]{3,2,1,0:T(8,128)} %get-tuple-element.14), channel_id=1, source_target_pairs={{0,1},{1,0},{2,3},{3,2},{4,5},{5,4},{6,7},{7,6},{8,9},{9,8},{10,11... | collective-permute-start | bytes 884744 | tf_op jit(solution)/shard_map/ppermute | solution.py:13
  9.5 5.1 %collective-permute-start.1 = (f32[96,128]{1,0:T(8,128)}, f32[96,128]{1,0:T(8,128)S(1)}, u32[]{:S(2)}, u32[]{:S(2)}) collective-permute-start(f32[96,128]{1,0:T(8,128)} %get-tuple-element.15), channel_id=1, source_target_pairs={{0,32},{32,0},{64,96},{96,64},{128,160},{160,128},{192,224},{224,1... | collective-permute-start | bytes 147464 | tf_op jit(solution)/shard_map/ppermute | solution.py:21
  14.6 1.9 %collective-permute-start.2 = (f32[96,128]{1,0:T(8,128)}, f32[96,128]{1,0:T(8,128)S(1)}, u32[]{:S(2)}, u32[]{:S(2)}) collective-permute-start(f32[96,128]{1,0:T(8,128)} %get-tuple-element.16), channel_id=1, source_target_pairs={{32,64},{64,32},{96,128},{128,96},{160,192},{192,160},{224,256},{2... | collective-permute-start | bytes 147464 | tf_op jit(solution)/shard_map/ppermute | solution.py:21
  16.5 1.9 %collective-permute-start.3 = (f32[3,32,128]{2,1,0:T(8,128)}, f32[3,32,128]{2,1,0:T(8,128)S(1)}, u32[]{:S(2)}, u32[]{:S(2)}) collective-permute-start(f32[3,32,128]{2,1,0:T(8,128)} %get-tuple-element.17), channel_id=1, source_target_pairs={{0,2},{2,0},{4,6},{6,4},{8,10},{10,8},{12,14},{14,12},{16,18},{18,... | collective-permute-start | bytes 147464 | tf_op jit(solution)/shard_map/ppermute | solution.py:21
  18.5 0.0 copy-start.1
  18.5 10.1 %collective-permute-start.4 = (f32[3,32,128]{2,1,0:T(8,128)}, f32[3,32,128]{2,1,0:T(8,128)S(1)}, u32[]{:S(2)}, u32[]{:S(2)}) collective-permute-start(f32[3,32,128]{2,1,0:T(8,128)} %get-tuple-element.18), channel_id=1, source_target_pairs={{2,4},{4,2},{6,8},{8,6},{10,12},{12,10},{14,16},{16,14},{18,20},{2... | collective-permute-start | bytes 147464 | tf_op jit(solution)/shard_map/ppermute | solution.py:21
  28.5 0.0 collective-permute-done.1.x_even
  28.6 0.0 copy-start.2
  28.6 0.0 collective-permute-done.2.x_odd
  28.6 0.0 copy-start.3
  28.6 0.0 collective-permute-done.3.y_even
  28.6 0.0 copy-start.4
  28.6 1.6 %collective-permute-done.4.y_odd = f32[3,32,128]{2,1,0:T(8,128)S(1)} collective-permute-done((f32[3,32,128]{2,1,0:T(8,128)}, f32[3,32,128]{2,1,0:T(8,128)S(1)}, u32[]{:S(2)}, u32[]{:S(2)}) %collective-permute-start.4) | collective-permute-done | bytes 49184 | tf_op jit(solution)/shard_map/ppermute | solution.py:21
  30.2 0.0 copy-start.5
  30.2 0.0 collective-permute-done.far
  30.2 0.0 copy-done.2
  30.2 0.0 copy-done.3
  30.2 0.0 copy-done.4
  30.3 0.6 copy-done.5
  30.8 0.0 copy-start
  30.8 0.7 copy-done
  31.5 6.5 %field_products.1 = (f32[1536,128]{1,0:T(8,128)}, f32[128,128]{1,0:T(8,128)}, f32[128,128]{1,0:T(8,128)}) custom-call(f32[3,16,96,128]{3,2,1,0:T(8,128)} %vel.3, f32[3,2,96,128]{3,2,1,0:T(8,128)} %copy-done, f32[3,2,96,128]{3,2,1,0:T(8,128)} %below.1, f32[3,2,96,128]{3,2,1,0:T(8,128)} %above.1, f32[96,128]{1,0:T(8,128)} %copy-done.2, f32[96,128]{1,0:T(8,128)} %copy-done.3, ...), custom_call_target="tpu_custom_call" | custom-call | tf_op jit(solution)/shard_map/field_products/pallas_call | solution.py:254
  38.1 7.4 %all-to-all-start = ((f32[32,48,128]{2,1,0:T(8,128)}), f32[32,48,128]{2,1,0:T(8,128)S(1)}, u32[]{:S(2)}, u32[]{:S(2)}) async-start(f32[32,48,128]{2,1,0:T(8,128)} %bitcast.47), calls=%async_computation | async-start | bytes 1572864 | tf_op jit(solution)/shard_map/all_to_all | solution.py:291
  45.5 4.8 %collective-permute-start.5 = (f32[128,128]{1,0:T(8,128)}, f32[128,128]{1,0:T(8,128)S(1)}, u32[]{:S(2)}, u32[]{:S(2)}) collective-permute-start(f32[128,128]{1,0:T(8,128)} %get-tuple-element.21), channel_id=1, source_target_pairs={{0,1},{1,0},{2,3},{3,2},{4,5},{5,4},{6,7},{7,6},{8,9},{9,8},{10,11... | collective-permute-start | bytes 196616 | tf_op jit(solution)/shard_map/ppermute | solution.py:13
  50.3 0.0 copy-done.1
  50.4 7.1 %collective-permute-done.5 = f32[128,128]{1,0:T(8,128)S(1)} collective-permute-done((f32[128,128]{1,0:T(8,128)}, f32[128,128]{1,0:T(8,128)S(1)}, u32[]{:S(2)}, u32[]{:S(2)}) %collective-permute-start.5) | collective-permute-done | bytes 65568 | tf_op jit(solution)/shard_map/ppermute | solution.py:13
  57.5 0.8 add_bitcast_fusion
  58.3 1.9 %all-to-all-done = f32[32,48,128]{2,1,0:T(8,128)S(1)} async-done(((f32[32,48,128]{2,1,0:T(8,128)}), f32[32,48,128]{2,1,0:T(8,128)S(1)}, u32[]{:S(2)}, u32[]{:S(2)}) %all-to-all-start) | async-done | bytes 786464 | tf_op jit(solution)/shard_map/all_to_all | solution.py:291
  60.3 0.1 fusion.19
  60.4 0.1 fusion.3
  60.6 0.7 copy.29
  61.4 8.7 %all-to-all-start.1 = ((f32[16,9,2,128]{3,2,1,0:T(2,128)}), f32[16,9,2,128]{3,2,1,0:T(2,128)S(1)}, u32[]{:S(2)}, u32[]{:S(2)}) async-start(f32[16,9,2,128]{3,2,1,0:T(2,128)} %copy.29), calls=%async_computation.1 | async-start | bytes 294912 | tf_op jit(solution)/shard_map/all_to_all | solution.py:291
  70.0 19.9 %all-gather = f32[1,96,128]{2,0,1:T(1,128)S(1)} all-gather(f32[1,6,128]{2,0,1:T(1,128)S(1)} %copy.30), channel_id=2, replica_groups=mesh['gx'=16,'gy'=16,'gz'=2] {'gx'}, dimensions={1}, use_global_device_ids=true | all-gather | bytes 52224 | tf_op jit(solution)/shard_map/all_gather | solution.py:331
  89.9 0.0 all-to-all-done.1
  89.9 0.1 reduce_sum.19
  90.0 0.7 broadcast_in_dim.9
  90.7 13.3 %all-to-all-start.2 = ((f32[32,5,2,128]{3,2,1,0:T(2,128)}), f32[32,5,2,128]{3,2,1,0:T(2,128)S(1)}, u32[]{:S(2)}, u32[]{:S(2)}) async-start(f32[32,5,2,128]{3,2,1,0:T(2,128)} %broadcast_in_dim.9), calls=%async_computation.2 | async-start | bytes 327680 | tf_op jit(solution)/shard_map/all_to_all | solution.py:291
  104.0 4.6 %collective-permute-start.6 = (f32[96,128]{1,0:T(8,128)S(1)}, f32[96,128]{1,0:T(8,128)S(1)}, u32[]{:S(2)}, u32[]{:S(2)}) collective-permute-start(f32[96,128]{1,0:T(8,128)S(1)} %bitcast.52), channel_id=1, source_target_pairs={{0,1},{1,0},{2,3},{3,2},{4,5},{5,4},{6,7},{7,6},{8,9},{9,8},{10,11... | collective-permute-start | bytes 147464 | tf_op jit(solution)/shard_map/ppermute | solution.py:13
  108.7 0.6 mul.55
  109.3 1.5 %collective-permute-done.6 = f32[96,128]{1,0:T(8,128)S(1)} collective-permute-done((f32[96,128]{1,0:T(8,128)S(1)}, f32[96,128]{1,0:T(8,128)S(1)}, u32[]{:S(2)}, u32[]{:S(2)}) %collective-permute-start.6) | collective-permute-done | bytes 49184 | tf_op jit(solution)/shard_map/ppermute | solution.py:13
  110.9 0.1 copy.35
  110.9 0.6 copy.44
  111.6 9.6 %all-to-all-done.2 = f32[32,5,2,128]{3,2,1,0:T(2,128)S(1)} async-done(((f32[32,5,2,128]{3,2,1,0:T(2,128)}), f32[32,5,2,128]{3,2,1,0:T(2,128)S(1)}, u32[]{:S(2)}, u32[]{:S(2)}) %all-to-all-start.2) | async-done | bytes 163872 | tf_op jit(solution)/shard_map/all_to_all | solution.py:291
  121.2 0.1 fusion.10
  121.3 0.7 copy.43
  122.0 0.6 maximum_multiply_fusion.1
  (23 shorter events, 0.3 us)
Async XLA Ops:
  3.9 26.3 %collective-permute-start = (f32[3,2,96,128]{3,2,1,0:T(8,128)}, f32[3,2,96,128]{3,2,1,0:T(8,128)S(1)}, u32[]{:S(2)}, u32[]{:S(2)}) collective-permute-start(f32[3,2,96,128]{3,2,1,0:T(8,128)} %get-tuple-element.14), channel_id=1, source_target_pairs={{0,1},{1,0},{2,3},{3,2},{4,5},{5,4},{6,7},{7,6},{8,9},{9,8},{10,11... | collective-permute-start | bytes 884744 | tf_op jit(solution)/shard_map/ppermute | solution.py:13
  9.5 19.0 %collective-permute-start.1 = (f32[96,128]{1,0:T(8,128)}, f32[96,128]{1,0:T(8,128)S(1)}, u32[]{:S(2)}, u32[]{:S(2)}) collective-permute-start(f32[96,128]{1,0:T(8,128)} %get-tuple-element.15), channel_id=1, source_target_pairs={{0,32},{32,0},{64,96},{96,64},{128,160},{160,128},{192,224},{224,1... | collective-permute-start | bytes 147464 | tf_op jit(solution)/shard_map/ppermute | solution.py:21
  14.6 14.0 %collective-permute-start.2 = (f32[96,128]{1,0:T(8,128)}, f32[96,128]{1,0:T(8,128)S(1)}, u32[]{:S(2)}, u32[]{:S(2)}) collective-permute-start(f32[96,128]{1,0:T(8,128)} %get-tuple-element.16), channel_id=1, source_target_pairs={{32,64},{64,32},{96,128},{128,96},{160,192},{192,160},{224,256},{2... | collective-permute-start | bytes 147464 | tf_op jit(solution)/shard_map/ppermute | solution.py:21
  16.5 12.1 %collective-permute-start.3 = (f32[3,32,128]{2,1,0:T(8,128)}, f32[3,32,128]{2,1,0:T(8,128)S(1)}, u32[]{:S(2)}, u32[]{:S(2)}) collective-permute-start(f32[3,32,128]{2,1,0:T(8,128)} %get-tuple-element.17), channel_id=1, source_target_pairs={{0,2},{2,0},{4,6},{6,4},{8,10},{10,8},{12,14},{14,12},{16,18},{18,... | collective-permute-start | bytes 147464 | tf_op jit(solution)/shard_map/ppermute | solution.py:21
  18.5 31.9 %copy-start.1 = (s32[512,96]{0,1:T(8,128)S(1)}, s32[512,96]{0,1:T(8,128)}, u32[]{:S(2)}) copy-start(s32[512,96]{0,1:T(8,128)} %param.16) | copy-start | bytes 589828
  18.5 11.7 %collective-permute-start.4 = (f32[3,32,128]{2,1,0:T(8,128)}, f32[3,32,128]{2,1,0:T(8,128)S(1)}, u32[]{:S(2)}, u32[]{:S(2)}) collective-permute-start(f32[3,32,128]{2,1,0:T(8,128)} %get-tuple-element.18), channel_id=1, source_target_pairs={{2,4},{4,2},{6,8},{8,6},{10,12},{12,10},{14,16},{16,14},{18,20},{2... | collective-permute-start | bytes 147464 | tf_op jit(solution)/shard_map/ppermute | solution.py:21
  28.6 1.7 %copy-start.2 = (f32[96,128]{1,0:T(8,128)}, f32[96,128]{1,0:T(8,128)S(1)}, u32[]{:S(2)}) copy-start(f32[96,128]{1,0:T(8,128)S(1)} %collective-permute-done.1.x_even) | copy-start | bytes 147460
  28.6 1.7 %copy-start.3 = (f32[96,128]{1,0:T(8,128)}, f32[96,128]{1,0:T(8,128)S(1)}, u32[]{:S(2)}) copy-start(f32[96,128]{1,0:T(8,128)S(1)} %collective-permute-done.2.x_odd) | copy-start | bytes 147460
  28.6 1.6 %copy-start.4 = (f32[3,32,128]{2,1,0:T(8,128)}, f32[3,32,128]{2,1,0:T(8,128)S(1)}, u32[]{:S(2)}) copy-start(f32[3,32,128]{2,1,0:T(8,128)S(1)} %collective-permute-done.3.y_even) | copy-start | bytes 147460
  30.2 0.6 copy-start.5
  30.8 0.7 copy-start
  38.1 22.1 %all-to-all-start = ((f32[32,48,128]{2,1,0:T(8,128)}), f32[32,48,128]{2,1,0:T(8,128)S(1)}, u32[]{:S(2)}, u32[]{:S(2)}) async-start(f32[32,48,128]{2,1,0:T(8,128)} %bitcast.47), calls=%async_computation | async-start | bytes 1572864 | tf_op jit(solution)/shard_map/all_to_all | solution.py:291
  45.5 12.0 %collective-permute-start.5 = (f32[128,128]{1,0:T(8,128)}, f32[128,128]{1,0:T(8,128)S(1)}, u32[]{:S(2)}, u32[]{:S(2)}) collective-permute-start(f32[128,128]{1,0:T(8,128)} %get-tuple-element.21), channel_id=1, source_target_pairs={{0,1},{1,0},{2,3},{3,2},{4,5},{5,4},{6,7},{7,6},{8,9},{9,8},{10,11... | collective-permute-start | bytes 196616 | tf_op jit(solution)/shard_map/ppermute | solution.py:13
  61.4 28.6 %all-to-all-start.1 = ((f32[16,9,2,128]{3,2,1,0:T(2,128)}), f32[16,9,2,128]{3,2,1,0:T(2,128)S(1)}, u32[]{:S(2)}, u32[]{:S(2)}) async-start(f32[16,9,2,128]{3,2,1,0:T(2,128)} %copy.29), calls=%async_computation.1 | async-start | bytes 294912 | tf_op jit(solution)/shard_map/all_to_all | solution.py:291
  90.7 30.4 %all-to-all-start.2 = ((f32[32,5,2,128]{3,2,1,0:T(2,128)}), f32[32,5,2,128]{3,2,1,0:T(2,128)S(1)}, u32[]{:S(2)}, u32[]{:S(2)}) async-start(f32[32,5,2,128]{3,2,1,0:T(2,128)} %broadcast_in_dim.9), calls=%async_computation.2 | async-start | bytes 327680 | tf_op jit(solution)/shard_map/all_to_all | solution.py:291
  104.0 6.7 %collective-permute-start.6 = (f32[96,128]{1,0:T(8,128)S(1)}, f32[96,128]{1,0:T(8,128)S(1)}, u32[]{:S(2)}, u32[]{:S(2)}) collective-permute-start(f32[96,128]{1,0:T(8,128)S(1)} %bitcast.52), channel_id=1, source_target_pairs={{0,1},{1,0},{2,3},{3,2},{4,5},{5,4},{6,7},{7,6},{8,9},{9,8},{10,11... | collective-permute-start | bytes 147464 | tf_op jit(solution)/shard_map/ppermute | solution.py:13

commit v6 on v5

--- a/solution.py
+++ b/solution.py
@@ -21,63 +21,44 @@
     return lax.ppermute(cells, axis, pairs)
 
 
-def pack_kernel(vel, near, x_even, x_odd, y_even, y_odd, held, sems):
+def pack_kernel(vel, near, x_even, x_odd, y_even, y_odd):
     gz = lax.axis_index("gz")
     odd_x = lax.rem(lax.axis_index("gx"), 2) == 1
     odd_y = lax.rem(lax.axis_index("gy"), 2) == 1
-    copies = [
-        pltpu.make_async_copy(
-            vel.at[part // 2, pl.ds(8 * (part % 2), 8)], held.at[part // 2, pl.ds(8 * (part % 2), 8)], sems.at[part]
-        )
-        for part in range(6)
-    ]
-    for copy in copies:
-        copy.start()
     lane = lax.broadcasted_iota(jnp.int32, (96, 128), 1)
     high = jnp.zeros((96, 128), jnp.float32)
     low = jnp.zeros((96, 128), jnp.float32)
-    rims = []
-    for part in range(6):
-        copies[part].wait()
-        c = part // 2
-        if part % 2 == 1:
-            rims.append(
-                pltpu.make_async_copy(held.at[c, pl.ds(14 * (1 - gz), 2)], near.at[c], sems.at[6 + c])
-            )
-            rims[-1].start()
-        for k in range(8 * (part % 2), 8 * (part % 2) + 8):
+    for c in range(3):
+        near[c] = vel[c, pl.ds(14 * (1 - gz), 2)]
+        for k in range(16):
             spot = 2 * (16 * c + k)
-            turned = pltpu.roll(held[c, k], spot + 2, 1)
+            turned = pltpu.roll(vel[c, k], spot + 2, 1)
             high = jnp.where((lane >= spot) & (lane < spot + 2), turned, high)
             low = jnp.where((lane >= spot + 2) & (lane < spot + 4), turned, low)
-            first = held[c, k, 0:2, :]
-            last = held[c, k, 94:96, :]
+            first = vel[c, k, 0:2, :]
+            last = vel[c, k, 94:96, :]
             y_even[c, 2 * k : 2 * k + 2, :] = jnp.where(odd_y, first, last)
             y_odd[c, 2 * k : 2 * k + 2, :] = jnp.where(odd_y, last, first)
     x_even[...] = jnp.where(odd_x, low, high)
     x_odd[...] = jnp.where(odd_x, high, low)
-    for rim in rims:
-        rim.wait()
 
 
 def pack(velocity):
     rims = jax.ShapeDtypeStruct((96, 128), jnp.float32)
     rows = jax.ShapeDtypeStruct((3, 32, 128), jnp.float32)
     whole = pl.BlockSpec(memory_space=pltpu.VMEM)
-    outside = pl.BlockSpec(memory_space=pl.ANY)
     return pl.pallas_call(
         pack_kernel,
-        in_specs=[outside],
-        out_specs=[outside] + [whole] * 4,
+        in_specs=[whole],
+        out_specs=[whole] * 5,
         out_shape=[jax.ShapeDtypeStruct((3, 2, 96, 128), jnp.float32), rims, rims, rows, rows],
-        scratch_shapes=[pltpu.VMEM((3, 16, 96, 128), jnp.float32), pltpu.SemaphoreType.DMA((9,))],
-        compiler_params=pltpu.CompilerParams(vmem_limit_bytes=60 * 1024 * 1024),
+        compiler_params=pltpu.CompilerParams(vmem_limit_bytes=32 * 1024 * 1024),
         name="pack_halos",
     )(velocity)
 
 
 def field_kernel(
-    vel, far, below, above, x_even, x_odd, y_even, y_odd, omega_x, omega_y, omega_z, phi_x, phi_z,
+    vel, far, below, above, y_even, y_odd, x_odd, x_even, omega_x, omega_y, omega_z, phi_x, phi_z,
     send, mine, theirs,
     padded, sides, x_held, y_held, wx_held, wy_held, wz_held, px_held,
     q_terms, flat, flat_terms, wx, wyz, phx, part_y, part_z, lead, pz_held, sems,
@@ -221,11 +202,10 @@
     part_y[...] = total_y
 
     lane8 = lax.broadcasted_iota(jnp.int32, (8, 128), 1)
-    shares = [part_z[pl.ds(pl.multiple_of(8 * jnp.abs(z - gz), 8), 8), :] for z in range(2)]
     for g in range(16):
         for z in range(2):
             chunk = 2 * g + z
-            base = 48 * chunk
+            base = 32 * chunk
             near = 32 * g + z
             send[base : base + 16, :] = lead[0, pl.ds(near, 16, stride=2), :]
             send[base + 16 : base + 24, :] = jnp.where(
@@ -235,9 +215,8 @@
             )
             for half in range(2):
                 lanes = slice(128 * half, 128 * half + 128)
-                send[base + 24 + 8 * half : base + 32 + 8 * half, :] = shares[z][:, lanes]
-                send[base + 40 + 3 * half : base + 43 + 3 * half, :] = part_y[3 * chunk : 3 * chunk + 3, lanes]
-            send[base + 46 : base + 48, :] = jnp.zeros((2, 128), jnp.float32)
+                send[base + 24 + 3 * half : base + 27 + 3 * half, :] = part_y[3 * chunk : 3 * chunk + 3, lanes]
+                send[base + 30 + half : base + 31 + half, :] = part_z[g : g + 1, lanes]
 
     turned = lax.dot_general(
         q_terms[...], wyz[...], (((0,), (0,)), ((), ())), preferred_element_type=jnp.float32
@@ -255,7 +234,7 @@
         field_kernel,
         in_specs=[outside] * 13,
         out_specs=[whole] * 3,
-        out_shape=[jax.ShapeDtypeStruct((1536, 128), jnp.float32), half, half],
+        out_shape=[jax.ShapeDtypeStruct((1024, 128), jnp.float32), half, half],
         scratch_shapes=[
             pltpu.VMEM((3, 20, 112, 128), jnp.float32),
             pltpu.VMEM((3, 16, 96, 128), jnp.float32),
@@ -277,7 +256,7 @@
             pltpu.SMEM((2, 16), jnp.int32),
             pltpu.SemaphoreType.DMA((14,)),
         ],
-        compiler_params=pltpu.CompilerParams(vmem_limit_bytes=60 * 1024 * 1024),
+        compiler_params=pltpu.CompilerParams(vmem_limit_bytes=32 * 1024 * 1024),
         name="field_products",
     )(velocity, far, below, above, *sides, omega_x, omega_y, omega_z, phi_x, phi_z)
 
@@ -285,6 +264,43 @@
 def split(values):
     high = lax.reduce_precision(values, 8, 7)
     return high.astype(jnp.bfloat16), (values - high).astype(jnp.bfloat16)
+
+
+FAR = [[4 * x + r for x in range(4)] for r in range(4)]
+NEAR = [[4 * x + r for r in range(4)] for x in range(4)]
+FAR_Z = [[8 * x + r for x in range(4)] for r in range(8)]
+NEAR_Z = [[8 * x + r for r in range(8)] for x in range(4)]
+
+
+def gather(rows, axes, groups):
+    return lax.all_gather(rows, axes, axis=0, tiled=True, axis_index_groups=groups)
+
+
+def unfold_kernel(wide_y, wide_z, factor_y, factor_z):
+    scale_y = 1.0 / math.sqrt(2048 * 32)
+    scale_z = 1.0 / math.sqrt(2048 * 1536)
+    for g in range(16):
+        x, near = g // 4, g % 4
+        for half in range(2):
+            lanes = slice(128 * half, 128 * half + 128)
+            for z in range(2):
+                spot = 24 * (2 * near + z) + 6 * x + 3 * half
+                factor_y[6 * g + 3 * z : 6 * g + 3 * z + 3, lanes] = wide_y[spot : spot + 3, :] * scale_y
+            spot = 8 * near + 2 * x + half
+            factor_z[g : g + 1, lanes] = wide_z[spot : spot + 1, :] * scale_z
+
+
+def unfold(wide_y, wide_z):
+    whole = pl.BlockSpec(memory_space=pltpu.VMEM)
+    return pl.pallas_call(
+        unfold_kernel,
+        in_specs=[whole] * 2,
+        out_specs=[whole] * 2,
+        out_shape=[jax.ShapeDtypeStruct((96, 256), jnp.float32), jax.ShapeDtypeStruct((16, 256), jnp.float32)],
+        compiler_params=pltpu.CompilerParams(vmem_limit_bytes=4 * 1024 * 1024),
+        cost_estimate=pl.CostEstimate(flops=0, bytes_accessed=0, transcendentals=0),
+        name="unfold_factors",
+    )(wide_y, wide_z)
 
 
 def exchange(rows, axes):
@@ -298,23 +314,18 @@
     gz = lax.axis_index("gz")
     near, x_even, x_odd, y_even, y_odd = pack(velocity)
     far = shift_permute(near, "gz", 1)
-    sides = [
-        edge_swap(x_even, "gx", 0),
-        edge_swap(x_odd, "gx", 1),
-        edge_swap(y_even, "gy", 0),
-        edge_swap(y_odd, "gy", 1),
-    ]
+    y_even = edge_swap(y_even, "gy", 0)
+    y_odd = edge_swap(y_odd, "gy", 1)
+    x_odd = edge_swap(x_odd, "gx", 1)
+    x_even = edge_swap(x_even, "gx", 0)
+    sides = [y_even, y_odd, x_odd, x_even]
     send, mine, theirs = field(velocity, far, below, above, sides, omega_x, omega_y, omega_z, phi_x, phi_z)
-    got = exchange(send, ("gx", "gz")).reshape(16, 2, 48, 128)
+    got = exchange(send, ("gx", "gz")).reshape(16, 2, 32, 128)
     part_x = mine + shift_permute(theirs, "gz", 1)
 
     by_z = jnp.sum(got, axis=0)
     summed = by_z[0] + by_z[1]
-    same = jnp.where(gz == 0, by_z[0, 24:40], by_z[1, 24:40])
-    cross = jnp.where(gz == 0, by_z[1, 24:40], by_z[0, 24:40])
-    rows_z = jnp.concatenate(
-        [same.reshape(2, 8, 128).transpose(1, 0, 2), cross.reshape(2, 8, 128).transpose(1, 0, 2)], axis=0
-    )
+    summed_z = jnp.where(gz == 0, by_z[0, 30:32], by_z[1, 30:32])
     rest = jnp.concatenate([summed[16:24, :64], summed[16:24, 64:]], axis=0)
     lead_high, lead_low = split(jnp.concatenate([summed[:16], rest], axis=1))
     wide = phi_y.T.astype(jnp.bfloat16)
@@ -324,24 +335,19 @@
     )
     core = jnp.dot(jnp.concatenate([lead_high, lead_low], axis=0), wide, preferred_element_type=jnp.float32)
     core = (core[:16] + core[16:]).reshape(16, 8, 128)
+    rows_z = jnp.broadcast_to(summed_z[None], (16, 2, 128))
     send = jnp.concatenate([core, part_x.reshape(16, 8, 128), rows_z], axis=1)
-    got = jnp.sum(exchange(send.reshape(16, 9, 2, 128), "gy"), axis=0).reshape(18, 128)
+    got = jnp.sum(exchange(send.reshape(288, 128), "gy").reshape(16, 18, 128), axis=0)
     core_sketch = got[:8].reshape(1, 2, 512) * (1.0 / math.sqrt(total_x * total_y * total_z))
 
-    got_y = lax.all_gather(summed[40:46], "gx", axis=0, tiled=True)
-    rows, got_y = lax.optimization_barrier((got[8:18], got_y))
-    other_y = shift_permute(got_y, "gz", 1)
-    halves = [jnp.where(gz == z, got_y, other_y).reshape(16, 2, 3, 128).transpose(0, 2, 1, 3) for z in range(2)]
-    factor_y = jnp.stack(halves, axis=1).reshape(96, 256) * (1.0 / math.sqrt(total_x * total_z))
-
-    got_x = exchange(jnp.broadcast_to(rows.reshape(1, 5, 2, 128), (32, 5, 2, 128)), ("gy", "gz"))
-    got_x = got_x.reshape(16, 2, 10, 128)
-    factor_x = got_x[:, :, :8].transpose(0, 2, 1, 3).reshape(128, 256)
+    part_y = gather(gather(summed[24:30], ("gx", "gz"), FAR_Z), ("gx", "gz"), NEAR_Z)
+    rows, part_y = lax.optimization_barrier((got[8:18], part_y))
+    got_x = exchange(jnp.broadcast_to(rows[None, :8], (32, 8, 128)).reshape(256, 128), ("gy", "gz"))
+    part_z = gather(gather(rows[8:], "gx", FAR), "gx", NEAR)
+    factor_y, factor_z = unfold(part_y, part_z)
+
+    factor_x = got_x.reshape(16, 2, 8, 128).transpose(0, 2, 1, 3).reshape(128, 256)
     factor_x = factor_x * (1.0 / math.sqrt(total_y * total_z))
-    first, second = got_x[:, 0, 8:], got_x[:, 1, 8:]
-    same = jnp.where(gz == 0, first[:8], second[:8])
-    cross = jnp.where(gz == 0, second[8:], first[8:])
-    factor_z = jnp.concatenate([same, cross], axis=0).reshape(16, 256) * (1.0 / math.sqrt(total_x * total_y))
     return (factor_x, factor_y, factor_z, core_sketch)
 
 

time: 123 us -> 130 us (1.057)
  blocking collectives: 19.9 us -> 52.8 us
  waiting for transfers between devices: 21.7 us -> 7.68 us
  starting transfers between devices: 63.4 us -> 54.7 us
  Pallas kernels: 9.79 us -> 7.83 us
  local copies, waits for them, and re-layouts: 5 us -> 3.07 us
    all_gather x1 -> x4, blocking collectives: 19.9 us -> 52.8 us  [gather(): lax.all_gather(rows, axes, axis=0, tiled=True, axis_index_groups=groups)]
    all_to_all x3, waiting for transfers between devices: 11.5 us -> 2.54 us  [exchange(): return lax.all_to_all(rows, axes, 0, 0, tiled=True)]
    all_to_all x3, starting transfers between devices: 29.3 us -> 23.5 us  [exchange(): return lax.all_to_all(rows, axes, 0, 0, tiled=True)]
    ppermute x3 -> x2, starting transfers between devices: 15.1 us -> 10.4 us  [shift_permute(): lax.ppermute(cells, axis, [(i, (i + step) % count) for i in range(count)])]
    ppermute x3 -> x2, waiting for transfers between devices: 8.59 us -> 4.3 us  [shift_permute(): lax.ppermute(cells, axis, [(i, (i + step) % count) for i in range(count)])]
    pallas_call x1 -> x2, Pallas kernels: 3.25 us -> 1.4 us  [the longest x1 0.7 us: pack(): pl.pallas_call(pack_kernel, in_specs=[whole], out_specs=[whole] * 5, out_...]
    ppermute x4, starting transfers between devices: 19 us -> 20.7 us  [edge_swap(): return lax.ppermute(cells, axis, pairs)]
  transfers between devices with their start and end apart: 10 -> 9, of which waited for: 5 -> 3; matrix products, arithmetic and copies ran while one was open for 2% -> 0% of each run, Pallas kernels for 0% -> 1%
where the time goes in v6:
time: 130 us; the launch traced here: 129 us
  starting transfers between devices  54.7 us (42%)
  blocking collectives  52.8 us (41%)
  Pallas kernels  7.83 us (6%)
  waiting for transfers between devices  7.68 us (6%)
  local copies, waits for them, and re-layouts  3.07 us (2%)
  other arithmetic  1.5 us (1%)
    all_gather x4, blocking collectives, gather(): lax.all_gather(rows, axes, axis=0, tiled=True, axis_index_groups=groups)  52.8 us
    all_to_all x3, starting transfers between devices, exchange(): return lax.all_to_all(rows, axes, 0, 0, tiled=True)  23.5 us
    ppermute x4, starting transfers between devices, edge_swap(): return lax.ppermute(cells, axis, pairs)  20.7 us
    ppermute x2, starting transfers between devices, shift_permute(): lax.ppermute(cells, axis, [(i, (i + step) % count) for i in range(count)])  10.4 us
    pallas_call x1, Pallas kernels, field(): pl.pallas_call(field_kernel, in_specs=[outside] * 13, out_specs=[whole] *...  6.43 us
    ppermute x2, waiting for transfers between devices, shift_permute(): lax.ppermute(cells, axis, [(i, (i + step) % count) for i in range(count)])  4.3 us
  transfers between devices with their start and end apart: 9, of which 3 were waited for; matrix products, arithmetic and copies ran while one was open for 0% of the time, Pallas kernels for 1%

profile of v6, /device:TPU:1, one launch (start us, length us, event | category | flops | bytes accessed | tf_op | source)
XLA Modules:
  0.0 128.6 jit_solution(12652703088238796096)
XLA Ops:
  0.6 0.0 copy-start
  0.6 1.7 %copy-done = f32[3,16,96,128]{3,2,1,0:T(8,128)S(1)} copy-done((f32[3,16,96,128]{3,2,1,0:T(8,128)S(1)}, f32[3,16,96,128]{3,2,1,0:T(8,128)}, u32[]{:S(2)}) %copy-start) | copy-done | bytes 2359320
  2.3 0.0 copy-start.1
  2.3 0.0 copy-start.2
  2.3 0.0 copy-start.3
  2.3 0.0 copy-start.5
  2.3 0.0 copy-start.6
  2.3 0.0 copy-start.7
  2.3 0.7 pack_halos.1
  3.1 5.7 %collective-permute-start = (f32[3,2,96,128]{3,2,1,0:T(8,128)S(1)}, f32[3,2,96,128]{3,2,1,0:T(8,128)S(1)}, u32[]{:S(2)}, u32[]{:S(2)}) collective-permute-start(f32[3,2,96,128]{3,2,1,0:T(8,128)S(1)} %get-tuple-element.16), channel_id=1, source_target_pairs={{0,1},{1,0},{2,3},{3,2},{4,5},{5,4},{6,7},{7,6},{8,9},{9,8},{10,11... | collective-permute-start | bytes 884744 | tf_op jit(solution)/shard_map/ppermute | solution.py:13
  8.7 3.5 %collective-permute-start.1 = (f32[3,32,128]{2,1,0:T(8,128)S(1)}, f32[3,32,128]{2,1,0:T(8,128)S(1)}, u32[]{:S(2)}, u32[]{:S(2)}) collective-permute-start(f32[3,32,128]{2,1,0:T(8,128)S(1)} %get-tuple-element.17), channel_id=1, source_target_pairs={{0,2},{2,0},{4,6},{6,4},{8,10},{10,8},{12,14},{14,12},{16,18},{18,... | collective-permute-start | bytes 147464 | tf_op jit(solution)/shard_map/ppermute | solution.py:21
  12.3 10.2 %collective-permute-start.2 = (f32[3,32,128]{2,1,0:T(8,128)S(1)}, f32[3,32,128]{2,1,0:T(8,128)S(1)}, u32[]{:S(2)}, u32[]{:S(2)}) collective-permute-start(f32[3,32,128]{2,1,0:T(8,128)S(1)} %get-tuple-element.18), channel_id=1, source_target_pairs={{2,4},{4,2},{6,8},{8,6},{10,12},{12,10},{14,16},{16,14},{18,20},{2... | collective-permute-start | bytes 147464 | tf_op jit(solution)/shard_map/ppermute | solution.py:21
  22.5 3.7 %collective-permute-start.3 = (f32[96,128]{1,0:T(8,128)S(1)}, f32[96,128]{1,0:T(8,128)S(1)}, u32[]{:S(2)}, u32[]{:S(2)}) collective-permute-start(f32[96,128]{1,0:T(8,128)S(1)} %get-tuple-element.19), channel_id=1, source_target_pairs={{32,64},{64,32},{96,128},{128,96},{160,192},{192,160},{224,256},{2... | collective-permute-start | bytes 147464 | tf_op jit(solution)/shard_map/ppermute | solution.py:21
  26.2 0.0 copy-start.8
  26.2 3.2 %collective-permute-start.4 = (f32[96,128]{1,0:T(8,128)S(1)}, f32[96,128]{1,0:T(8,128)S(1)}, u32[]{:S(2)}, u32[]{:S(2)}) collective-permute-start(f32[96,128]{1,0:T(8,128)S(1)} %get-tuple-element.20), channel_id=1, source_target_pairs={{0,32},{32,0},{64,96},{96,64},{128,160},{160,128},{192,224},{224,1... | collective-permute-start | bytes 147464 | tf_op jit(solution)/shard_map/ppermute | solution.py:21
  29.5 0.0 collective-permute-done.1.y_even
  29.5 0.0 collective-permute-done.2.y_odd
  29.5 0.0 collective-permute-done.3.x_odd
  29.5 0.8 collective-permute-done.4.x_even
  30.3 0.0 collective-permute-done.far
  30.3 0.0 copy-done.1
  30.3 0.0 copy-done.2
  30.3 0.0 copy-done.3
  30.3 0.0 copy-done.4
  30.3 0.0 copy-done.5
  30.3 0.0 copy-done.6
  30.4 0.0 copy-done.7
  30.4 6.4 %field_products.1 = (f32[1024,128]{1,0:T(8,128)}, f32[128,128]{1,0:T(8,128)S(1)}, f32[128,128]{1,0:T(8,128)S(1)}) custom-call(f32[3,16,96,128]{3,2,1,0:T(8,128)S(1)} %copy-done, f32[3,2,96,128]{3,2,1,0:T(8,128)S(1)} %collective-permute-done.far, f32[3,2,96,128]{3,2,1,0:T(8,128)S(1)} %copy-done.1, f32[3,2,96,128]{3,2,1,0:T(8,128)S(1)} %copy-done.2, ...), custom_call_target="tpu_custom_call" | custom-call | tf_op jit(solution)/shard_map/field_products/pallas_call | solution.py:233
  36.8 5.2 %all-to-all-start = ((f32[32,32,128]{2,1,0:T(8,128)}), f32[32,32,128]{2,1,0:T(8,128)S(1)}, u32[]{:S(2)}, u32[]{:S(2)}) async-start(f32[32,32,128]{2,1,0:T(8,128)} %bitcast), calls=%async_computation | async-start | bytes 1048576 | tf_op jit(solution)/shard_map/all_to_all | solution.py:307
  42.0 4.8 %collective-permute-start.5 = (f32[128,128]{1,0:T(8,128)S(1)}, f32[128,128]{1,0:T(8,128)S(1)}, u32[]{:S(2)}, u32[]{:S(2)}) collective-permute-start(f32[128,128]{1,0:T(8,128)S(1)} %get-tuple-element.23), channel_id=1, source_target_pairs={{0,1},{1,0},{2,3},{3,2},{4,5},{5,4},{6,7},{7,6},{8,9},{9,8},{10,11... | collective-permute-start | bytes 196616 | tf_op jit(solution)/shard_map/ppermute | solution.py:13
  46.8 0.0 copy-done.8
  46.9 4.3 %collective-permute-done.5 = f32[128,128]{1,0:T(8,128)S(1)} collective-permute-done((f32[128,128]{1,0:T(8,128)S(1)}, f32[128,128]{1,0:T(8,128)S(1)}, u32[]{:S(2)}, u32[]{:S(2)}) %collective-permute-start.5) | collective-permute-done | bytes 65568 | tf_op jit(solution)/shard_map/ppermute | solution.py:13
  51.2 2.5 %all-to-all-done = f32[32,32,128]{2,1,0:T(8,128)S(1)} async-done(((f32[32,32,128]{2,1,0:T(8,128)}), f32[32,32,128]{2,1,0:T(8,128)S(1)}, u32[]{:S(2)}, u32[]{:S(2)}) %all-to-all-start) | async-done | bytes 524320 | tf_op jit(solution)/shard_map/all_to_all | solution.py:307
  53.8 0.1 fusion.19
  53.9 0.1 fusion.3
  54.1 0.7 pad_maximum_fusion
  54.8 6.0 %all-to-all-start.1 = ((f32[16,18,128]{2,1,0:T(8,128)}), f32[16,18,128]{2,1,0:T(8,128)S(1)}, u32[]{:S(2)}, u32[]{:S(2)}) async-start(f32[16,18,128]{2,1,0:T(8,128)} %pad_maximum_fusion), calls=%async_computation.1 | async-start | bytes 393216 | tf_op jit(solution)/shard_map/all_to_all | solution.py:307
  60.8 9.4 %all-gather = f32[1,24,128]{2,0,1:T(1,128)S(1)} all-gather(f32[1,6,128]{2,0,1:T(1,128)S(1)} %copy.14), channel_id=2, replica_groups={{0,128,256,384},{1,129,257,385},{32,160,288,416},{33,161,289,417},{64,1..., dimensions={1}, use_global_device_ids=true | all-gather | bytes 15360 | tf_op jit(solution)/shard_map/all_gather | solution.py:276
  70.2 29.0 %all-gather.1 = f32[1,192,128]{2,1,0:T(8,128)S(1)} all-gather(f32[1,24,128]{2,1,0:T(8,128)S(1)} %bitcast.29), channel_id=3, replica_groups={{0,1,32,33,64,65,96,97},{128,129,160,161,192,193,224,225},{256,257,288,..., dimensions={1}, use_global_device_ids=true | all-gather | bytes 110592 | tf_op jit(solution)/shard_map/all_gather | solution.py:276
  99.3 0.0 all-to-all-done.1
  99.3 0.7 broadcast_in_dim.8
  100.0 12.3 %all-to-all-start.2 = ((f32[32,8,128]{2,1,0:T(8,128)}), f32[32,8,128]{2,1,0:T(8,128)S(1)}, u32[]{:S(2)}, u32[]{:S(2)}) async-start(f32[32,8,128]{2,1,0:T(8,128)} %broadcast_in_dim.8), calls=%async_computation.2 | async-start | bytes 262144 | tf_op jit(solution)/shard_map/all_to_all | solution.py:307
  112.3 0.6 mul.39
  112.9 7.2 %all-gather.2 = f32[4,2,128]{2,1,0:T(2,128)S(1)} all-gather(f32[1,2,128]{2,1,0:T(2,128)S(1)} %slice_bitcast_fusion.1), channel_id=1, replica_groups={{0,128,256,384},{32,160,288,416},{64,192,320,448},{96,224,352,480},{1,1..., dimensions={0}, use_global_device_ids=true | all-gather | bytes 5120 | tf_op jit(solution)/shard_map/all_gather | solution.py:276
  120.1 7.2 %all_gather.15.wide_z = f32[32,128]{1,0:T(8,128)S(1)} all-gather(f32[8,128]{1,0:T(8,128)S(1)} %bitcast.30), channel_id=1, replica_groups={{0,32,64,96},{128,160,192,224},{256,288,320,352},{384,416,448,480},{1,3..., dimensions={0}, use_global_device_ids=true | all-gather | bytes 20480 | tf_op jit(solution)/shard_map/all_gather | solution.py:276
  127.3 0.7 unfold_factors.1
  128.0 0.0 all-to-all-done.2
  128.0 0.7 broadcast_multiply_fusion
  (19 shorter events, 0.2 us)
Async XLA Ops:
  0.6 1.7 %copy-start = (f32[3,16,96,128]{3,2,1,0:T(8,128)S(1)}, f32[3,16,96,128]{3,2,1,0:T(8,128)}, u32[]{:S(2)}) copy-start(f32[3,16,96,128]{3,2,1,0:T(8,128)} %vel.3) | copy-start | bytes 7077892
  2.3 28.0 %copy-start.1 = (f32[3,2,96,128]{3,2,1,0:T(8,128)S(1)}, f32[3,2,96,128]{3,2,1,0:T(8,128)}, u32[]{:S(2)}) copy-start(f32[3,2,96,128]{3,2,1,0:T(8,128)} %below.1) | copy-start | bytes 884740
  2.3 28.0 %copy-start.2 = (f32[3,2,96,128]{3,2,1,0:T(8,128)S(1)}, f32[3,2,96,128]{3,2,1,0:T(8,128)}, u32[]{:S(2)}) copy-start(f32[3,2,96,128]{3,2,1,0:T(8,128)} %above.1) | copy-start | bytes 884740
  2.3 28.0 %copy-start.3 = (s32[512,128]{1,0:T(8,128)S(1)}, s32[512,128]{1,0:T(8,128)}, u32[]{:S(2)}) copy-start(s32[512,128]{1,0:T(8,128)} %phi_x.1) | copy-start | bytes 786436
  2.3 28.0 %copy-start.4 = (s32[128,256]{1,0:T(8,128)S(1)}, s32[128,256]{1,0:T(8,128)}, u32[]{:S(2)}) copy-start(s32[128,256]{1,0:T(8,128)} %omega_x.1) | copy-start | bytes 393220
  2.3 28.0 %copy-start.5 = (s32[96,256]{1,0:T(8,128)S(1)}, s32[96,256]{1,0:T(8,128)}, u32[]{:S(2)}) copy-start(s32[96,256]{1,0:T(8,128)} %omega_y.1) | copy-start | bytes 294916
  2.3 28.0 %copy-start.6 = (s32[16,256]{1,0:T(8,128)S(1)}, s32[16,256]{1,0:T(8,128)}, u32[]{:S(2)}) copy-start(s32[16,256]{1,0:T(8,128)} %omega_z.1) | copy-start | bytes 49156
  2.3 28.0 %copy-start.7 = (s32[2,16]{1,0:T(2,128)S(1)}, s32[2,16]{1,0:T(2,128)}, u32[]{:S(2)}) copy-start(s32[2,16]{1,0:T(2,128)} %phi_z.1) | copy-start | bytes 388
  3.1 27.3 %collective-permute-start = (f32[3,2,96,128]{3,2,1,0:T(8,128)S(1)}, f32[3,2,96,128]{3,2,1,0:T(8,128)S(1)}, u32[]{:S(2)}, u32[]{:S(2)}) collective-permute-start(f32[3,2,96,128]{3,2,1,0:T(8,128)S(1)} %get-tuple-element.16), channel_id=1, source_target_pairs={{0,1},{1,0},{2,3},{3,2},{4,5},{5,4},{6,7},{7,6},{8,9},{9,8},{10,11... | collective-permute-start | bytes 884744 | tf_op jit(solution)/shard_map/ppermute | solution.py:13
  8.7 20.7 %collective-permute-start.1 = (f32[3,32,128]{2,1,0:T(8,128)S(1)}, f32[3,32,128]{2,1,0:T(8,128)S(1)}, u32[]{:S(2)}, u32[]{:S(2)}) collective-permute-start(f32[3,32,128]{2,1,0:T(8,128)S(1)} %get-tuple-element.17), channel_id=1, source_target_pairs={{0,2},{2,0},{4,6},{6,4},{8,10},{10,8},{12,14},{14,12},{16,18},{18,... | collective-permute-start | bytes 147464 | tf_op jit(solution)/shard_map/ppermute | solution.py:21
  12.3 17.2 %collective-permute-start.2 = (f32[3,32,128]{2,1,0:T(8,128)S(1)}, f32[3,32,128]{2,1,0:T(8,128)S(1)}, u32[]{:S(2)}, u32[]{:S(2)}) collective-permute-start(f32[3,32,128]{2,1,0:T(8,128)S(1)} %get-tuple-element.18), channel_id=1, source_target_pairs={{2,4},{4,2},{6,8},{8,6},{10,12},{12,10},{14,16},{16,14},{18,20},{2... | collective-permute-start | bytes 147464 | tf_op jit(solution)/shard_map/ppermute | solution.py:21
  22.5 7.0 %collective-permute-start.3 = (f32[96,128]{1,0:T(8,128)S(1)}, f32[96,128]{1,0:T(8,128)S(1)}, u32[]{:S(2)}, u32[]{:S(2)}) collective-permute-start(f32[96,128]{1,0:T(8,128)S(1)} %get-tuple-element.19), channel_id=1, source_target_pairs={{32,64},{64,32},{96,128},{128,96},{160,192},{192,160},{224,256},{2... | collective-permute-start | bytes 147464 | tf_op jit(solution)/shard_map/ppermute | solution.py:21
  26.2 20.6 %copy-start.8 = (s32[512,96]{0,1:T(8,128)S(1)}, s32[512,96]{0,1:T(8,128)}, u32[]{:S(2)}) copy-start(s32[512,96]{0,1:T(8,128)} %param.16) | copy-start | bytes 589828
  26.2 4.1 %collective-permute-start.4 = (f32[96,128]{1,0:T(8,128)S(1)}, f32[96,128]{1,0:T(8,128)S(1)}, u32[]{:S(2)}, u32[]{:S(2)}) collective-permute-start(f32[96,128]{1,0:T(8,128)S(1)} %get-tuple-element.20), channel_id=1, source_target_pairs={{0,32},{32,0},{64,96},{96,64},{128,160},{160,128},{192,224},{224,1... | collective-permute-start | bytes 147464 | tf_op jit(solution)/shard_map/ppermute | solution.py:21
  36.8 16.9 %all-to-all-start = ((f32[32,32,128]{2,1,0:T(8,128)}), f32[32,32,128]{2,1,0:T(8,128)S(1)}, u32[]{:S(2)}, u32[]{:S(2)}) async-start(f32[32,32,128]{2,1,0:T(8,128)} %bitcast), calls=%async_computation | async-start | bytes 1048576 | tf_op jit(solution)/shard_map/all_to_all | solution.py:307
  42.0 9.1 %collective-permute-start.5 = (f32[128,128]{1,0:T(8,128)S(1)}, f32[128,128]{1,0:T(8,128)S(1)}, u32[]{:S(2)}, u32[]{:S(2)}) collective-permute-start(f32[128,128]{1,0:T(8,128)S(1)} %get-tuple-element.23), channel_id=1, source_target_pairs={{0,1},{1,0},{2,3},{3,2},{4,5},{5,4},{6,7},{7,6},{8,9},{9,8},{10,11... | collective-permute-start | bytes 196616 | tf_op jit(solution)/shard_map/ppermute | solution.py:13
  54.8 44.5 %all-to-all-start.1 = ((f32[16,18,128]{2,1,0:T(8,128)}), f32[16,18,128]{2,1,0:T(8,128)S(1)}, u32[]{:S(2)}, u32[]{:S(2)}) async-start(f32[16,18,128]{2,1,0:T(8,128)} %pad_maximum_fusion), calls=%async_computation.1 | async-start | bytes 393216 | tf_op jit(solution)/shard_map/all_to_all | solution.py:307
  100.0 28.0 %all-to-all-start.2 = ((f32[32,8,128]{2,1,0:T(8,128)}), f32[32,8,128]{2,1,0:T(8,128)S(1)}, u32[]{:S(2)}, u32[]{:S(2)}) async-start(f32[32,8,128]{2,1,0:T(8,128)} %broadcast_in_dim.8), calls=%async_computation.2 | async-start | bytes 262144 | tf_op jit(solution)/shard_map/all_to_all | solution.py:307

commit v7 on v6

--- a/solution.py
+++ b/solution.py
@@ -205,7 +205,7 @@
     for g in range(16):
         for z in range(2):
             chunk = 2 * g + z
-            base = 32 * chunk
+            base = 40 * chunk
             near = 32 * g + z
             send[base : base + 16, :] = lead[0, pl.ds(near, 16, stride=2), :]
             send[base + 16 : base + 24, :] = jnp.where(
@@ -213,10 +213,12 @@
                 lead[1, pl.ds(near, 8, stride=2), :],
                 pltpu.roll(lead[1, pl.ds(near + 16, 8, stride=2), :], 64, 1),
             )
+            rank = 4 * ((g // 4) % 2) + g % 4
+            spot = 6 * (2 * rank + z)
             for half in range(2):
                 lanes = slice(128 * half, 128 * half + 128)
-                send[base + 24 + 3 * half : base + 27 + 3 * half, :] = part_y[3 * chunk : 3 * chunk + 3, lanes]
-                send[base + 30 + half : base + 31 + half, :] = part_z[g : g + 1, lanes]
+                send[base + 24 + 6 * half : base + 30 + 6 * half, :] = part_y[spot : spot + 6, lanes]
+                send[base + 36 + 2 * half : base + 38 + 2 * half, :] = part_z[2 * rank : 2 * rank + 2, lanes]
 
     turned = lax.dot_general(
         q_terms[...], wyz[...], (((0,), (0,)), ((), ())), preferred_element_type=jnp.float32
@@ -234,7 +236,7 @@
         field_kernel,
         in_specs=[outside] * 13,
         out_specs=[whole] * 3,
-        out_shape=[jax.ShapeDtypeStruct((1024, 128), jnp.float32), half, half],
+        out_shape=[jax.ShapeDtypeStruct((1280, 128), jnp.float32), half, half],
         scratch_shapes=[
             pltpu.VMEM((3, 20, 112, 128), jnp.float32),
             pltpu.VMEM((3, 16, 96, 128), jnp.float32),
@@ -266,41 +268,54 @@
     return high.astype(jnp.bfloat16), (values - high).astype(jnp.bfloat16)
 
 
-FAR = [[4 * x + r for x in range(4)] for r in range(4)]
 NEAR = [[4 * x + r for r in range(4)] for x in range(4)]
-FAR_Z = [[8 * x + r for x in range(4)] for r in range(8)]
-NEAR_Z = [[8 * x + r for r in range(8)] for x in range(4)]
-
-
-def gather(rows, axes, groups):
-    return lax.all_gather(rows, axes, axis=0, tiled=True, axis_index_groups=groups)
-
-
-def unfold_kernel(wide_y, wide_z, factor_y, factor_z):
+
+
+def gather(rows):
+    return lax.all_gather(rows, "gx", axis=0, tiled=True, axis_index_groups=NEAR)
+
+
+def pair_swap(rows):
+    return lax.ppermute(rows, "gx", [(i, i ^ 4) for i in range(16)])
+
+
+def cross_swap(rows):
+    return lax.ppermute(rows, ("gx", "gz"), [(i, i ^ 9) for i in range(32)])
+
+
+def unfold_kernel(own_y, beside_y, above_y, cross_y, own_z, beside_z, factor_y, factor_z):
     scale_y = 1.0 / math.sqrt(2048 * 32)
     scale_z = 1.0 / math.sqrt(2048 * 1536)
-    for g in range(16):
-        x, near = g // 4, g % 4
-        for half in range(2):
-            lanes = slice(128 * half, 128 * half + 128)
-            for z in range(2):
-                spot = 24 * (2 * near + z) + 6 * x + 3 * half
-                factor_y[6 * g + 3 * z : 6 * g + 3 * z + 3, lanes] = wide_y[spot : spot + 3, :] * scale_y
-            spot = 8 * near + 2 * x + half
-            factor_z[g : g + 1, lanes] = wide_z[spot : spot + 1, :] * scale_z
-
-
-def unfold(wide_y, wide_z):
+    gz = lax.axis_index("gz")
+    pair = lax.rem(lax.axis_index("gx") // 4, 2)
+    for x in range(2):
+        rows_z = jnp.where(pair == x, own_z[...], beside_z[...]) * scale_z
+        for z in range(2):
+            near = jnp.where(gz == z, own_y[...], above_y[...])
+            away = jnp.where(gz == z, beside_y[...], cross_y[...])
+            rows_y = jnp.where(pair == x, near, away) * scale_y
+            for r in range(4):
+                rank = 4 * x + r
+                spot = 6 * (2 * rank + z)
+                factor_y[spot : spot + 6, 0:128] = rows_y[12 * r : 12 * r + 6, :]
+                factor_y[spot : spot + 6, 128:256] = rows_y[12 * r + 6 : 12 * r + 12, :]
+        for r in range(4):
+            rank = 4 * x + r
+            factor_z[2 * rank : 2 * rank + 2, 0:128] = rows_z[4 * r : 4 * r + 2, :]
+            factor_z[2 * rank : 2 * rank + 2, 128:256] = rows_z[4 * r + 2 : 4 * r + 4, :]
+
+
+def unfold(*pieces):
     whole = pl.BlockSpec(memory_space=pltpu.VMEM)
     return pl.pallas_call(
         unfold_kernel,
-        in_specs=[whole] * 2,
+        in_specs=[whole] * 6,
         out_specs=[whole] * 2,
         out_shape=[jax.ShapeDtypeStruct((96, 256), jnp.float32), jax.ShapeDtypeStruct((16, 256), jnp.float32)],
         compiler_params=pltpu.CompilerParams(vmem_limit_bytes=4 * 1024 * 1024),
         cost_estimate=pl.CostEstimate(flops=0, bytes_accessed=0, transcendentals=0),
         name="unfold_factors",
-    )(wide_y, wide_z)
+    )(*pieces)
 
 
 def exchange(rows, axes):
@@ -320,12 +335,12 @@
     x_even = edge_swap(x_even, "gx", 0)
     sides = [y_even, y_odd, x_odd, x_even]
     send, mine, theirs = field(velocity, far, below, above, sides, omega_x, omega_y, omega_z, phi_x, phi_z)
-    got = exchange(send, ("gx", "gz")).reshape(16, 2, 32, 128)
+    got = exchange(send, ("gx", "gz")).reshape(16, 2, 40, 128)
     part_x = mine + shift_permute(theirs, "gz", 1)
 
     by_z = jnp.sum(got, axis=0)
     summed = by_z[0] + by_z[1]
-    summed_z = jnp.where(gz == 0, by_z[0, 30:32], by_z[1, 30:32])
+    summed_z = jnp.where(gz == 0, by_z[0, 36:40], by_z[1, 36:40])
     rest = jnp.concatenate([summed[16:24, :64], summed[16:24, 64:]], axis=0)
     lead_high, lead_low = split(jnp.concatenate([summed[:16], rest], axis=1))
     wide = phi_y.T.astype(jnp.bfloat16)
@@ -335,16 +350,17 @@
     )
     core = jnp.dot(jnp.concatenate([lead_high, lead_low], axis=0), wide, preferred_element_type=jnp.float32)
     core = (core[:16] + core[16:]).reshape(16, 8, 128)
-    rows_z = jnp.broadcast_to(summed_z[None], (16, 2, 128))
+    rows_z = jnp.broadcast_to(summed_z[None], (16, 4, 128))
     send = jnp.concatenate([core, part_x.reshape(16, 8, 128), rows_z], axis=1)
-    got = jnp.sum(exchange(send.reshape(288, 128), "gy").reshape(16, 18, 128), axis=0)
+    got = jnp.sum(exchange(send.reshape(320, 128), "gy").reshape(16, 20, 128), axis=0)
     core_sketch = got[:8].reshape(1, 2, 512) * (1.0 / math.sqrt(total_x * total_y * total_z))
 
-    part_y = gather(gather(summed[24:30], ("gx", "gz"), FAR_Z), ("gx", "gz"), NEAR_Z)
-    rows, part_y = lax.optimization_barrier((got[8:18], part_y))
+    own_y = gather(summed[24:36])
+    pieces = (own_y, pair_swap(own_y), shift_permute(own_y, "gz", 1), cross_swap(own_y))
+    rows, pieces = lax.optimization_barrier((got[8:20], pieces))
     got_x = exchange(jnp.broadcast_to(rows[None, :8], (32, 8, 128)).reshape(256, 128), ("gy", "gz"))
-    part_z = gather(gather(rows[8:], "gx", FAR), "gx", NEAR)
-    factor_y, factor_z = unfold(part_y, part_z)
+    own_z = gather(rows[8:])
+    factor_y, factor_z = unfold(*pieces, own_z, pair_swap(own_z))
 
     factor_x = got_x.reshape(16, 2, 8, 128).transpose(0, 2, 1, 3).reshape(128, 256)
     factor_x = factor_x * (1.0 / math.sqrt(total_y * total_z))

time: 130 us -> 113 us (0.87)
  the two profiles are of different devices: /device:TPU:1 before, /device:TPU:4 now
where the time goes in v7:
time: 113 us
  starting transfers between devices  68.7 us (61%)
  waiting for transfers between devices  19.8 us (18%)
  blocking collectives  10.4 us (9%)
  Pallas kernels  7.86 us (7%)
  local copies, waits for them, and re-layouts  3.07 us (3%)
  other arithmetic  1.52 us (1%)
    all_to_all x3, starting transfers between devices, exchange(): return lax.all_to_all(rows, axes, 0, 0, tiled=True)  26.3 us
    ppermute x4, starting transfers between devices, edge_swap(): return lax.ppermute(cells, axis, pairs)  19.1 us
    ppermute x3, starting transfers between devices, shift_permute(): lax.ppermute(cells, axis, [(i, (i + step) % count) for i in range(count)])  12.8 us
    all_gather x2, blocking collectives, gather(): lax.all_gather(rows, 'gx', axis=0, tiled=True, axis_index_groups=NEAR)  10.4 us
    ppermute x3, waiting for transfers between devices, shift_permute(): lax.ppermute(cells, axis, [(i, (i + step) % count) for i in range(count)])  7.9 us
    pallas_call x1, Pallas kernels, field(): pl.pallas_call(field_kernel, in_specs=[outside] * 13, out_specs=[whole] *...  6.49 us
    ppermute x2, starting transfers between devices, pair_swap(): return lax.ppermute(rows, 'gx', [(i, i ^ 4) for i in range(16)])  5.82 us
    all_to_all x3, waiting for transfers between devices, exchange(): return lax.all_to_all(rows, axes, 0, 0, tiled=True)  5.06 us
  transfers between devices with their start and end apart: 13, of which 6 were waited for; matrix products, arithmetic and copies ran while one was open for 1% of the time, Pallas kernels for 1%

profile of v7, /device:TPU:4, one launch (start us, length us, event | category | flops | bytes accessed | tf_op | source)
XLA Modules:
  0.0 112.5 jit_solution(15090210899875092969)
XLA Ops:
  0.6 0.0 copy-start
  0.6 1.7 %copy-done = f32[3,16,96,128]{3,2,1,0:T(8,128)S(1)} copy-done((f32[3,16,96,128]{3,2,1,0:T(8,128)S(1)}, f32[3,16,96,128]{3,2,1,0:T(8,128)}, u32[]{:S(2)}) %copy-start) | copy-done | bytes 2359320
  2.3 0.0 copy-start.5
  2.3 0.0 copy-start.6
  2.3 0.0 copy-start.7
  2.3 0.7 pack_halos.1
  3.1 5.1 %collective-permute-start = (f32[3,2,96,128]{3,2,1,0:T(8,128)S(1)}, f32[3,2,96,128]{3,2,1,0:T(8,128)S(1)}, u32[]{:S(2)}, u32[]{:S(2)}) collective-permute-start(f32[3,2,96,128]{3,2,1,0:T(8,128)S(1)} %get-tuple-element.19), channel_id=1, source_target_pairs={{0,1},{1,0},{2,3},{3,2},{4,5},{5,4},{6,7},{7,6},{8,9},{9,8},{10,11... | collective-permute-start | bytes 884744 | tf_op jit(solution)/shard_map/ppermute | solution.py:13
  8.2 3.8 %collective-permute-start.1 = (f32[3,32,128]{2,1,0:T(8,128)S(1)}, f32[3,32,128]{2,1,0:T(8,128)S(1)}, u32[]{:S(2)}, u32[]{:S(2)}) collective-permute-start(f32[3,32,128]{2,1,0:T(8,128)S(1)} %get-tuple-element.20), channel_id=1, source_target_pairs={{0,2},{2,0},{4,6},{6,4},{8,10},{10,8},{12,14},{14,12},{16,18},{18,... | collective-permute-start | bytes 147464 | tf_op jit(solution)/shard_map/ppermute | solution.py:21
  12.0 10.5 %collective-permute-start.2 = (f32[3,32,128]{2,1,0:T(8,128)S(1)}, f32[3,32,128]{2,1,0:T(8,128)S(1)}, u32[]{:S(2)}, u32[]{:S(2)}) collective-permute-start(f32[3,32,128]{2,1,0:T(8,128)S(1)} %get-tuple-element.21), channel_id=1, source_target_pairs={{2,4},{4,2},{6,8},{8,6},{10,12},{12,10},{14,16},{16,14},{18,20},{2... | collective-permute-start | bytes 147464 | tf_op jit(solution)/shard_map/ppermute | solution.py:21
  22.5 1.9 %collective-permute-start.3 = (f32[96,128]{1,0:T(8,128)S(1)}, f32[96,128]{1,0:T(8,128)S(1)}, u32[]{:S(2)}, u32[]{:S(2)}) collective-permute-start(f32[96,128]{1,0:T(8,128)S(1)} %get-tuple-element.22), channel_id=1, source_target_pairs={{32,64},{64,32},{96,128},{128,96},{160,192},{192,160},{224,256},{2... | collective-permute-start | bytes 147464 | tf_op jit(solution)/shard_map/ppermute | solution.py:21
  24.4 0.0 copy-start.8
  24.4 2.8 %collective-permute-start.4 = (f32[96,128]{1,0:T(8,128)S(1)}, f32[96,128]{1,0:T(8,128)S(1)}, u32[]{:S(2)}, u32[]{:S(2)}) collective-permute-start(f32[96,128]{1,0:T(8,128)S(1)} %get-tuple-element.23), channel_id=1, source_target_pairs={{0,32},{32,0},{64,96},{96,64},{128,160},{160,128},{192,224},{224,1... | collective-permute-start | bytes 147464 | tf_op jit(solution)/shard_map/ppermute | solution.py:21
  27.3 0.0 collective-permute-done.1.y_even
  27.3 0.0 collective-permute-done.2.y_odd
  27.3 1.5 %collective-permute-done.3.x_odd = f32[96,128]{1,0:T(8,128)S(1)} collective-permute-done((f32[96,128]{1,0:T(8,128)S(1)}, f32[96,128]{1,0:T(8,128)S(1)}, u32[]{:S(2)}, u32[]{:S(2)}) %collective-permute-start.3) | collective-permute-done | bytes 49184 | tf_op jit(solution)/shard_map/ppermute | solution.py:21
  28.8 0.0 collective-permute-done.4.x_even
  28.8 0.0 collective-permute-done.far
  28.8 0.0 copy-done.1
  28.8 0.0 copy-done.2
  28.8 0.0 copy-done.3
  28.8 0.0 copy-done.4
  28.8 0.0 copy-done.5
  28.9 6.5 %field_products.1 = (f32[1280,128]{1,0:T(8,128)}, f32[128,128]{1,0:T(8,128)S(1)}, f32[128,128]{1,0:T(8,128)S(1)}) custom-call(f32[3,16,96,128]{3,2,1,0:T(8,128)S(1)} %copy-done, f32[3,2,96,128]{3,2,1,0:T(8,128)S(1)} %collective-permute-done.far, f32[3,2,96,128]{3,2,1,0:T(8,128)S(1)} %copy-done.1, f32[3,2,96,128]{3,2,1,0:T(8,128)S(1)} %copy-done.2, ...), custom_call_target="tpu_custom_call" | custom-call | tf_op jit(solution)/shard_map/field_products/pallas_call | solution.py:235
  35.4 5.7 %all-to-all-start = ((f32[32,40,128]{2,1,0:T(8,128)}), f32[32,40,128]{2,1,0:T(8,128)S(1)}, u32[]{:S(2)}, u32[]{:S(2)}) async-start(f32[32,40,128]{2,1,0:T(8,128)} %bitcast), calls=%async_computation | async-start | bytes 1310720 | tf_op jit(solution)/shard_map/all_to_all | solution.py:322
  41.1 4.9 %collective-permute-start.5 = (f32[128,128]{1,0:T(8,128)S(1)}, f32[128,128]{1,0:T(8,128)S(1)}, u32[]{:S(2)}, u32[]{:S(2)}) collective-permute-start(f32[128,128]{1,0:T(8,128)S(1)} %get-tuple-element.26), channel_id=1, source_target_pairs={{0,1},{1,0},{2,3},{3,2},{4,5},{5,4},{6,7},{7,6},{8,9},{9,8},{10,11... | collective-permute-start | bytes 196616 | tf_op jit(solution)/shard_map/ppermute | solution.py:13
  46.0 7.9 %collective-permute-done.5 = f32[128,128]{1,0:T(8,128)S(1)} collective-permute-done((f32[128,128]{1,0:T(8,128)S(1)}, f32[128,128]{1,0:T(8,128)S(1)}, u32[]{:S(2)}, u32[]{:S(2)}) %collective-permute-start.5) | collective-permute-done | bytes 65568 | tf_op jit(solution)/shard_map/ppermute | solution.py:13
  53.9 0.0 all-to-all-done
  54.0 0.1 fusion.19
  54.1 0.1 fusion.3
  54.3 0.7 pad_maximum_fusion
  55.0 6.3 %all-to-all-start.1 = ((f32[16,20,128]{2,1,0:T(8,128)}), f32[16,20,128]{2,1,0:T(8,128)S(1)}, u32[]{:S(2)}, u32[]{:S(2)}) async-start(f32[16,20,128]{2,1,0:T(8,128)} %pad_maximum_fusion), calls=%async_computation.1 | async-start | bytes 393216 | tf_op jit(solution)/shard_map/all_to_all | solution.py:322
  61.4 5.2 %all-gather = f32[1,48,128]{2,0,1:T(1,128)S(1)} all-gather(f32[1,12,128]{2,0,1:T(1,128)S(1)} %copy.13), channel_id=2, replica_groups={{0,32,64,96},{128,160,192,224},{256,288,320,352},{384,416,448,480},{1,3..., dimensions={1}, use_global_device_ids=true | all-gather | bytes 30720 | tf_op jit(solution)/shard_map/all_gather | solution.py:275
  66.5 3.2 %collective-permute-start.6 = (f32[48,128]{1,0:T(8,128)S(1)}, f32[48,128]{1,0:T(8,128)S(1)}, u32[]{:S(2)}, u32[]{:S(2)}) collective-permute-start(f32[48,128]{1,0:T(8,128)S(1)} %bitcast.24), channel_id=1, source_target_pairs={{0,128},{32,160},{64,192},{96,224},{128,0},{160,32},{192,64},{224,... | collective-permute-start | bytes 73736 | tf_op jit(solution)/shard_map/ppermute | solution.py:279
  69.7 2.9 %collective-permute-start.7 = (f32[48,128]{1,0:T(8,128)S(1)}, f32[48,128]{1,0:T(8,128)S(1)}, u32[]{:S(2)}, u32[]{:S(2)}) collective-permute-start(f32[48,128]{1,0:T(8,128)S(1)} %bitcast.25), channel_id=1, source_target_pairs={{0,1},{1,0},{2,3},{3,2},{4,5},{5,4},{6,7},{7,6},{8,9},{9,8},{10,11... | collective-permute-start | bytes 73736 | tf_op jit(solution)/shard_map/ppermute | solution.py:13
  72.6 4.7 %collective-permute-start.8 = (f32[48,128]{1,0:T(8,128)S(1)}, f32[48,128]{1,0:T(8,128)S(1)}, u32[]{:S(2)}, u32[]{:S(2)}) collective-permute-start(f32[48,128]{1,0:T(8,128)S(1)} %bitcast.26), channel_id=1, source_target_pairs={{0,129},{1,128},{32,161},{33,160},{64,193},{65,192},{96,225},{97,2... | collective-permute-start | bytes 73736 | tf_op jit(solution)/shard_map/ppermute | solution.py:283
  77.3 0.3 all-to-all-done.1
  77.6 0.0 collective-permute-done.6.beside_y
  77.6 0.0 collective-permute-done.7.above_y
  77.6 3.1 %collective-permute-done.8.cross_y = f32[48,128]{1,0:T(8,128)S(1)} collective-permute-done((f32[48,128]{1,0:T(8,128)S(1)}, f32[48,128]{1,0:T(8,128)S(1)}, u32[]{:S(2)}, u32[]{:S(2)}) %collective-permute-start.8) | collective-permute-done | bytes 24608 | tf_op jit(solution)/shard_map/ppermute | solution.py:283
  80.7 0.7 broadcast_in_dim.8
  81.4 14.3 %all-to-all-start.2 = ((f32[32,8,128]{2,1,0:T(8,128)}), f32[32,8,128]{2,1,0:T(8,128)S(1)}, u32[]{:S(2)}, u32[]{:S(2)}) async-start(f32[32,8,128]{2,1,0:T(8,128)} %broadcast_in_dim.8), calls=%async_computation.2 | async-start | bytes 262144 | tf_op jit(solution)/shard_map/all_to_all | solution.py:322
  95.7 5.2 %all-gather.1 = f32[4,4,128]{2,1,0:T(4,128)S(1)} all-gather(f32[1,4,128]{2,1,0:T(4,128)S(1)} %slice_bitcast_fusion.1), channel_id=1, replica_groups={{0,32,64,96},{128,160,192,224},{256,288,320,352},{384,416,448,480},{1,3..., dimensions={0}, use_global_device_ids=true | all-gather | bytes 10240 | tf_op jit(solution)/shard_map/all_gather | solution.py:275
  100.9 2.7 %collective-permute-start.9 = (f32[16,128]{1,0:T(8,128)S(1)}, f32[16,128]{1,0:T(8,128)S(1)}, u32[]{:S(2)}, u32[]{:S(2)}) collective-permute-start(f32[16,128]{1,0:T(8,128)S(1)} %bitcast.28), channel_id=1, source_target_pairs={{0,128},{32,160},{64,192},{96,224},{128,0},{160,32},{192,64},{224,... | collective-permute-start | bytes 24584 | tf_op jit(solution)/shard_map/ppermute | solution.py:279
  103.6 0.6 mul.39
  104.2 2.3 %collective-permute-done.9.beside_z = f32[16,128]{1,0:T(8,128)S(1)} collective-permute-done((f32[16,128]{1,0:T(8,128)S(1)}, f32[16,128]{1,0:T(8,128)S(1)}, u32[]{:S(2)}, u32[]{:S(2)}) %collective-permute-start.9) | collective-permute-done | bytes 8224 | tf_op jit(solution)/shard_map/ppermute | solution.py:279
  106.4 0.7 unfold_factors.1
  107.1 4.8 %all-to-all-done.2 = f32[32,8,128]{2,1,0:T(8,128)S(1)} async-done(((f32[32,8,128]{2,1,0:T(8,128)}), f32[32,8,128]{2,1,0:T(8,128)S(1)}, u32[]{:S(2)}, u32[]{:S(2)}) %all-to-all-start.2) | async-done | bytes 131104 | tf_op jit(solution)/shard_map/all_to_all | solution.py:322
  111.8 0.7 broadcast_multiply_fusion
  (25 shorter events, 0.2 us)
Async XLA Ops:
  0.6 1.7 %copy-start = (f32[3,16,96,128]{3,2,1,0:T(8,128)S(1)}, f32[3,16,96,128]{3,2,1,0:T(8,128)}, u32[]{:S(2)}) copy-start(f32[3,16,96,128]{3,2,1,0:T(8,128)} %vel.3) | copy-start | bytes 7077892
  2.3 26.5 %copy-start.1 = (f32[3,2,96,128]{3,2,1,0:T(8,128)S(1)}, f32[3,2,96,128]{3,2,1,0:T(8,128)}, u32[]{:S(2)}) copy-start(f32[3,2,96,128]{3,2,1,0:T(8,128)} %below.1) | copy-start | bytes 884740
  2.3 26.5 %copy-start.2 = (f32[3,2,96,128]{3,2,1,0:T(8,128)S(1)}, f32[3,2,96,128]{3,2,1,0:T(8,128)}, u32[]{:S(2)}) copy-start(f32[3,2,96,128]{3,2,1,0:T(8,128)} %above.1) | copy-start | bytes 884740
  2.3 26.5 %copy-start.3 = (s32[512,128]{1,0:T(8,128)S(1)}, s32[512,128]{1,0:T(8,128)}, u32[]{:S(2)}) copy-start(s32[512,128]{1,0:T(8,128)} %phi_x.1) | copy-start | bytes 786436
  2.3 26.5 %copy-start.4 = (s32[128,256]{1,0:T(8,128)S(1)}, s32[128,256]{1,0:T(8,128)}, u32[]{:S(2)}) copy-start(s32[128,256]{1,0:T(8,128)} %omega_x.1) | copy-start | bytes 393220
  2.3 26.5 %copy-start.5 = (s32[96,256]{1,0:T(8,128)S(1)}, s32[96,256]{1,0:T(8,128)}, u32[]{:S(2)}) copy-start(s32[96,256]{1,0:T(8,128)} %omega_y.1) | copy-start | bytes 294916
  2.3 26.5 %copy-start.6 = (s32[16,256]{1,0:T(8,128)S(1)}, s32[16,256]{1,0:T(8,128)}, u32[]{:S(2)}) copy-start(s32[16,256]{1,0:T(8,128)} %omega_z.1) | copy-start | bytes 49156
  2.3 26.5 %copy-start.7 = (s32[2,16]{1,0:T(2,128)S(1)}, s32[2,16]{1,0:T(2,128)}, u32[]{:S(2)}) copy-start(s32[2,16]{1,0:T(2,128)} %phi_z.1) | copy-start | bytes 388
  3.1 25.8 %collective-permute-start = (f32[3,2,96,128]{3,2,1,0:T(8,128)S(1)}, f32[3,2,96,128]{3,2,1,0:T(8,128)S(1)}, u32[]{:S(2)}, u32[]{:S(2)}) collective-permute-start(f32[3,2,96,128]{3,2,1,0:T(8,128)S(1)} %get-tuple-element.19), channel_id=1, source_target_pairs={{0,1},{1,0},{2,3},{3,2},{4,5},{5,4},{6,7},{7,6},{8,9},{9,8},{10,11... | collective-permute-start | bytes 884744 | tf_op jit(solution)/shard_map/ppermute | solution.py:13
  8.2 19.1 %collective-permute-start.1 = (f32[3,32,128]{2,1,0:T(8,128)S(1)}, f32[3,32,128]{2,1,0:T(8,128)S(1)}, u32[]{:S(2)}, u32[]{:S(2)}) collective-permute-start(f32[3,32,128]{2,1,0:T(8,128)S(1)} %get-tuple-element.20), channel_id=1, source_target_pairs={{0,2},{2,0},{4,6},{6,4},{8,10},{10,8},{12,14},{14,12},{16,18},{18,... | collective-permute-start | bytes 147464 | tf_op jit(solution)/shard_map/ppermute | solution.py:21
  12.0 15.3 %collective-permute-start.2 = (f32[3,32,128]{2,1,0:T(8,128)S(1)}, f32[3,32,128]{2,1,0:T(8,128)S(1)}, u32[]{:S(2)}, u32[]{:S(2)}) collective-permute-start(f32[3,32,128]{2,1,0:T(8,128)S(1)} %get-tuple-element.21), channel_id=1, source_target_pairs={{2,4},{4,2},{6,8},{8,6},{10,12},{12,10},{14,16},{16,14},{18,20},{2... | collective-permute-start | bytes 147464 | tf_op jit(solution)/shard_map/ppermute | solution.py:21
  22.5 6.3 %collective-permute-start.3 = (f32[96,128]{1,0:T(8,128)S(1)}, f32[96,128]{1,0:T(8,128)S(1)}, u32[]{:S(2)}, u32[]{:S(2)}) collective-permute-start(f32[96,128]{1,0:T(8,128)S(1)} %get-tuple-element.22), channel_id=1, source_target_pairs={{32,64},{64,32},{96,128},{128,96},{160,192},{192,160},{224,256},{2... | collective-permute-start | bytes 147464 | tf_op jit(solution)/shard_map/ppermute | solution.py:21
  24.4 21.5 %copy-start.8 = (s32[512,96]{0,1:T(8,128)S(1)}, s32[512,96]{0,1:T(8,128)}, u32[]{:S(2)}) copy-start(s32[512,96]{0,1:T(8,128)} %param.16) | copy-start | bytes 589828
  24.4 4.4 %collective-permute-start.4 = (f32[96,128]{1,0:T(8,128)S(1)}, f32[96,128]{1,0:T(8,128)S(1)}, u32[]{:S(2)}, u32[]{:S(2)}) collective-permute-start(f32[96,128]{1,0:T(8,128)S(1)} %get-tuple-element.23), channel_id=1, source_target_pairs={{0,32},{32,0},{64,96},{96,64},{128,160},{160,128},{192,224},{224,1... | collective-permute-start | bytes 147464 | tf_op jit(solution)/shard_map/ppermute | solution.py:21
  35.4 18.6 %all-to-all-start = ((f32[32,40,128]{2,1,0:T(8,128)}), f32[32,40,128]{2,1,0:T(8,128)S(1)}, u32[]{:S(2)}, u32[]{:S(2)}) async-start(f32[32,40,128]{2,1,0:T(8,128)} %bitcast), calls=%async_computation | async-start | bytes 1310720 | tf_op jit(solution)/shard_map/all_to_all | solution.py:322
  41.1 12.8 %collective-permute-start.5 = (f32[128,128]{1,0:T(8,128)S(1)}, f32[128,128]{1,0:T(8,128)S(1)}, u32[]{:S(2)}, u32[]{:S(2)}) collective-permute-start(f32[128,128]{1,0:T(8,128)S(1)} %get-tuple-element.26), channel_id=1, source_target_pairs={{0,1},{1,0},{2,3},{3,2},{4,5},{5,4},{6,7},{7,6},{8,9},{9,8},{10,11... | collective-permute-start | bytes 196616 | tf_op jit(solution)/shard_map/ppermute | solution.py:13
  55.0 22.6 %all-to-all-start.1 = ((f32[16,20,128]{2,1,0:T(8,128)}), f32[16,20,128]{2,1,0:T(8,128)S(1)}, u32[]{:S(2)}, u32[]{:S(2)}) async-start(f32[16,20,128]{2,1,0:T(8,128)} %pad_maximum_fusion), calls=%async_computation.1 | async-start | bytes 393216 | tf_op jit(solution)/shard_map/all_to_all | solution.py:322
  66.5 11.1 %collective-permute-start.6 = (f32[48,128]{1,0:T(8,128)S(1)}, f32[48,128]{1,0:T(8,128)S(1)}, u32[]{:S(2)}, u32[]{:S(2)}) collective-permute-start(f32[48,128]{1,0:T(8,128)S(1)} %bitcast.24), channel_id=1, source_target_pairs={{0,128},{32,160},{64,192},{96,224},{128,0},{160,32},{192,64},{224,... | collective-permute-start | bytes 73736 | tf_op jit(solution)/shard_map/ppermute | solution.py:279
  69.7 7.9 %collective-permute-start.7 = (f32[48,128]{1,0:T(8,128)S(1)}, f32[48,128]{1,0:T(8,128)S(1)}, u32[]{:S(2)}, u32[]{:S(2)}) collective-permute-start(f32[48,128]{1,0:T(8,128)S(1)} %bitcast.25), channel_id=1, source_target_pairs={{0,1},{1,0},{2,3},{3,2},{4,5},{5,4},{6,7},{7,6},{8,9},{9,8},{10,11... | collective-permute-start | bytes 73736 | tf_op jit(solution)/shard_map/ppermute | solution.py:13
  72.6 8.1 %collective-permute-start.8 = (f32[48,128]{1,0:T(8,128)S(1)}, f32[48,128]{1,0:T(8,128)S(1)}, u32[]{:S(2)}, u32[]{:S(2)}) collective-permute-start(f32[48,128]{1,0:T(8,128)S(1)} %bitcast.26), channel_id=1, source_target_pairs={{0,129},{1,128},{32,161},{33,160},{64,193},{65,192},{96,225},{97,2... | collective-permute-start | bytes 73736 | tf_op jit(solution)/shard_map/ppermute | solution.py:283
  81.4 30.5 %all-to-all-start.2 = ((f32[32,8,128]{2,1,0:T(8,128)}), f32[32,8,128]{2,1,0:T(8,128)S(1)}, u32[]{:S(2)}, u32[]{:S(2)}) async-start(f32[32,8,128]{2,1,0:T(8,128)} %broadcast_in_dim.8), calls=%async_computation.2 | async-start | bytes 262144 | tf_op jit(solution)/shard_map/all_to_all | solution.py:322
  100.9 5.5 %collective-permute-start.9 = (f32[16,128]{1,0:T(8,128)S(1)}, f32[16,128]{1,0:T(8,128)S(1)}, u32[]{:S(2)}, u32[]{:S(2)}) collective-permute-start(f32[16,128]{1,0:T(8,128)S(1)} %bitcast.28), channel_id=1, source_target_pairs={{0,128},{32,160},{64,192},{96,224},{128,0},{160,32},{192,64},{224,... | collective-permute-start | bytes 24584 | tf_op jit(solution)/shard_map/ppermute | solution.py:279

commit v8 on v7

--- a/solution.py
+++ b/solution.py
@@ -59,7 +59,7 @@
 
 def field_kernel(
     vel, far, below, above, y_even, y_odd, x_odd, x_even, omega_x, omega_y, omega_z, phi_x, phi_z,
-    send, mine, theirs,
+    send, part_x,
     padded, sides, x_held, y_held, wx_held, wy_held, wz_held, px_held,
     q_terms, flat, flat_terms, wx, wyz, phx, part_y, part_z, lead, pz_held, sems,
 ):
@@ -224,19 +224,19 @@
         q_terms[...], wyz[...], (((0,), (0,)), ((), ())), preferred_element_type=jnp.float32
     )
     turned = turned[0:128, :] + turned[128:256, :]
-    mine[...] = jnp.where(gz == 0, turned[:, 0:128], turned[:, 128:256])
-    theirs[...] = jnp.where(gz == 0, turned[:, 128:256], turned[:, 0:128])
+    for h in range(16):
+        part_x[16 * h : 16 * h + 8, :] = turned[8 * h : 8 * h + 8, 0:128]
+        part_x[16 * h + 8 : 16 * h + 16, :] = turned[8 * h : 8 * h + 8, 128:256]
 
 
 def field(velocity, far, below, above, sides, omega_x, omega_y, omega_z, phi_x, phi_z):
     whole = pl.BlockSpec(memory_space=pltpu.VMEM)
     outside = pl.BlockSpec(memory_space=pl.ANY)
-    half = jax.ShapeDtypeStruct((128, 128), jnp.float32)
     return pl.pallas_call(
         field_kernel,
         in_specs=[outside] * 13,
-        out_specs=[whole] * 3,
-        out_shape=[jax.ShapeDtypeStruct((1280, 128), jnp.float32), half, half],
+        out_specs=[whole] * 2,
+        out_shape=[jax.ShapeDtypeStruct((1280, 128), jnp.float32), jax.ShapeDtypeStruct((256, 128), jnp.float32)],
         scratch_shapes=[
             pltpu.VMEM((3, 20, 112, 128), jnp.float32),
             pltpu.VMEM((3, 16, 96, 128), jnp.float32),
@@ -334,9 +334,9 @@
     x_odd = edge_swap(x_odd, "gx", 1)
     x_even = edge_swap(x_even, "gx", 0)
     sides = [y_even, y_odd, x_odd, x_even]
-    send, mine, theirs = field(velocity, far, below, above, sides, omega_x, omega_y, omega_z, phi_x, phi_z)
+    send, part_x = field(velocity, far, below, above, sides, omega_x, omega_y, omega_z, phi_x, phi_z)
     got = exchange(send, ("gx", "gz")).reshape(16, 2, 40, 128)
-    part_x = mine + shift_permute(theirs, "gz", 1)
+    part_x = part_x + shift_permute(part_x, "gz", 1)
 
     by_z = jnp.sum(got, axis=0)
     summed = by_z[0] + by_z[1]
@@ -351,16 +351,18 @@
     core = jnp.dot(jnp.concatenate([lead_high, lead_low], axis=0), wide, preferred_element_type=jnp.float32)
     core = (core[:16] + core[16:]).reshape(16, 8, 128)
     rows_z = jnp.broadcast_to(summed_z[None], (16, 4, 128))
-    send = jnp.concatenate([core, part_x.reshape(16, 8, 128), rows_z], axis=1)
-    got = jnp.sum(exchange(send.reshape(320, 128), "gy").reshape(16, 20, 128), axis=0)
+    send = jnp.concatenate([core, part_x.reshape(16, 16, 128), rows_z], axis=1)
+    got = jnp.sum(exchange(send.reshape(16, 7, 4, 128), "gy"), axis=0).reshape(28, 128)
     core_sketch = got[:8].reshape(1, 2, 512) * (1.0 / math.sqrt(total_x * total_y * total_z))
 
     own_y = gather(summed[24:36])
-    pieces = (own_y, pair_swap(own_y), shift_permute(own_y, "gz", 1), cross_swap(own_y))
-    rows, pieces = lax.optimization_barrier((got[8:20], pieces))
-    got_x = exchange(jnp.broadcast_to(rows[None, :8], (32, 8, 128)).reshape(256, 128), ("gy", "gz"))
-    own_z = gather(rows[8:])
-    factor_y, factor_z = unfold(*pieces, own_z, pair_swap(own_z))
+    cross_y = cross_swap(own_y)
+    rows, own_y, beside_y, above_y = lax.optimization_barrier(
+        (got[8:28], own_y, pair_swap(own_y), shift_permute(own_y, "gz", 1))
+    )
+    got_x = exchange(jnp.broadcast_to(rows[None, :16], (16, 16, 128)).reshape(256, 128), "gy")
+    own_z = gather(rows[16:])
+    factor_y, factor_z = unfold(own_y, beside_y, above_y, cross_y, own_z, pair_swap(own_z))
 
     factor_x = got_x.reshape(16, 2, 8, 128).transpose(0, 2, 1, 3).reshape(128, 256)
     factor_x = factor_x * (1.0 / math.sqrt(total_y * total_z))

time: 113 us -> 108 us (0.956)
  the two profiles are of different devices: /device:TPU:4 before, /device:TPU:1 now
where the time goes in v8:
time: 108 us
  starting transfers between devices  64.5 us (60%)
  waiting for transfers between devices  15.4 us (14%)
  blocking collectives  13.8 us (13%)
  Pallas kernels  7.87 us (7%)
  local copies, waits for them, and re-layouts  3.9 us (4%)
    all_to_all x3, starting transfers between devices, exchange(): return lax.all_to_all(rows, axes, 0, 0, tiled=True)  22.7 us
    ppermute x4, starting transfers between devices, edge_swap(): return lax.ppermute(cells, axis, pairs)  20.7 us
    all_gather x2, blocking collectives, gather(): lax.all_gather(rows, 'gx', axis=0, tiled=True, axis_index_groups=NEAR)  13.8 us
    ppermute x3, starting transfers between devices, shift_permute(): lax.ppermute(cells, axis, [(i, (i + step) % count) for i in range(count)])  13.1 us
    ppermute x3, waiting for transfers between devices, shift_permute(): lax.ppermute(cells, axis, [(i, (i + step) % count) for i in range(count)])  11.9 us
    pallas_call x1, Pallas kernels, field(): pl.pallas_call(field_kernel, in_specs=[outside] * 13, out_specs=[whole] *...  6.49 us
    ppermute x2, starting transfers between devices, pair_swap(): return lax.ppermute(rows, 'gx', [(i, i ^ 4) for i in range(16)])  4.7 us
    ppermute x1, starting transfers between devices, cross_swap(): return lax.ppermute(rows, ('gx', 'gz'), [(i, i ^ 9) for i in range(32)])  3.39 us
  transfers between devices with their start and end apart: 13, of which 5 were waited for; matrix products, arithmetic and copies ran while one was open for 1% of the time, Pallas kernels for 1%

profile of v8, /device:TPU:1, one launch (start us, length us, event | category | flops | bytes accessed | tf_op | source)
XLA Modules:
  0.0 107.5 jit_solution(637754655654980154)
XLA Ops:
  0.6 0.0 copy-start
  0.6 1.7 %copy-done = f32[3,16,96,128]{3,2,1,0:T(8,128)S(1)} copy-done((f32[3,16,96,128]{3,2,1,0:T(8,128)S(1)}, f32[3,16,96,128]{3,2,1,0:T(8,128)}, u32[]{:S(2)}) %copy-start) | copy-done | bytes 2359320
  2.3 0.0 copy-start.5
  2.3 0.0 copy-start.6
  2.3 0.0 copy-start.7
  2.3 0.7 pack_halos.1
  3.1 5.7 %collective-permute-start = (f32[3,2,96,128]{3,2,1,0:T(8,128)S(1)}, f32[3,2,96,128]{3,2,1,0:T(8,128)S(1)}, u32[]{:S(2)}, u32[]{:S(2)}) collective-permute-start(f32[3,2,96,128]{3,2,1,0:T(8,128)S(1)} %get-tuple-element.17), channel_id=1, source_target_pairs={{0,1},{1,0},{2,3},{3,2},{4,5},{5,4},{6,7},{7,6},{8,9},{9,8},{10,11... | collective-permute-start | bytes 884744 | tf_op jit(solution)/shard_map/ppermute | solution.py:13
  8.7 3.5 %collective-permute-start.1 = (f32[3,32,128]{2,1,0:T(8,128)S(1)}, f32[3,32,128]{2,1,0:T(8,128)S(1)}, u32[]{:S(2)}, u32[]{:S(2)}) collective-permute-start(f32[3,32,128]{2,1,0:T(8,128)S(1)} %get-tuple-element.18), channel_id=1, source_target_pairs={{0,2},{2,0},{4,6},{6,4},{8,10},{10,8},{12,14},{14,12},{16,18},{18,... | collective-permute-start | bytes 147464 | tf_op jit(solution)/shard_map/ppermute | solution.py:21
  12.3 10.2 %collective-permute-start.2 = (f32[3,32,128]{2,1,0:T(8,128)S(1)}, f32[3,32,128]{2,1,0:T(8,128)S(1)}, u32[]{:S(2)}, u32[]{:S(2)}) collective-permute-start(f32[3,32,128]{2,1,0:T(8,128)S(1)} %get-tuple-element.19), channel_id=1, source_target_pairs={{2,4},{4,2},{6,8},{8,6},{10,12},{12,10},{14,16},{16,14},{18,20},{2... | collective-permute-start | bytes 147464 | tf_op jit(solution)/shard_map/ppermute | solution.py:21
  22.5 3.7 %collective-permute-start.3 = (f32[96,128]{1,0:T(8,128)S(1)}, f32[96,128]{1,0:T(8,128)S(1)}, u32[]{:S(2)}, u32[]{:S(2)}) collective-permute-start(f32[96,128]{1,0:T(8,128)S(1)} %get-tuple-element.20), channel_id=1, source_target_pairs={{32,64},{64,32},{96,128},{128,96},{160,192},{192,160},{224,256},{2... | collective-permute-start | bytes 147464 | tf_op jit(solution)/shard_map/ppermute | solution.py:21
  26.2 0.0 copy-start.8
  26.2 3.2 %collective-permute-start.4 = (f32[96,128]{1,0:T(8,128)S(1)}, f32[96,128]{1,0:T(8,128)S(1)}, u32[]{:S(2)}, u32[]{:S(2)}) collective-permute-start(f32[96,128]{1,0:T(8,128)S(1)} %get-tuple-element.21), channel_id=1, source_target_pairs={{0,32},{32,0},{64,96},{96,64},{128,160},{160,128},{192,224},{224,1... | collective-permute-start | bytes 147464 | tf_op jit(solution)/shard_map/ppermute | solution.py:21
  29.5 0.0 collective-permute-done.1.y_even
  29.5 0.0 collective-permute-done.2.y_odd
  29.5 0.0 collective-permute-done.3.x_odd
  29.5 0.8 collective-permute-done.4.x_even
  30.3 0.0 collective-permute-done.far
  30.3 0.0 copy-done.1
  30.3 0.0 copy-done.2
  30.3 0.0 copy-done.3
  30.4 6.5 %field_products.1 = (f32[1280,128]{1,0:T(8,128)}, f32[256,128]{1,0:T(8,128)S(1)}) custom-call(f32[3,16,96,128]{3,2,1,0:T(8,128)S(1)} %copy-done, f32[3,2,96,128]{3,2,1,0:T(8,128)S(1)} %collective-permute-done.far, f32[3,2,96,128]{3,2,1,0:T(8,128)S(1)} %copy-done.1, f32[3,2,96,128]{3,2,1,0:T(8,128)S(1)} %copy-done.2, ...), custom_call_target="tpu_custom_call" | custom-call | tf_op jit(solution)/shard_map/field_products/pallas_call | solution.py:235
  36.9 5.2 %all-to-all-start = ((f32[32,40,128]{2,1,0:T(8,128)}), f32[32,40,128]{2,1,0:T(8,128)S(1)}, u32[]{:S(2)}, u32[]{:S(2)}) async-start(f32[32,40,128]{2,1,0:T(8,128)} %bitcast), calls=%async_computation | async-start | bytes 1310720 | tf_op jit(solution)/shard_map/all_to_all | solution.py:322
  42.1 4.8 %collective-permute-start.5 = (f32[256,128]{1,0:T(8,128)S(1)}, f32[256,128]{1,0:T(8,128)S(1)}, u32[]{:S(2)}, u32[]{:S(2)}) collective-permute-start(f32[256,128]{1,0:T(8,128)S(1)} %get-tuple-element.23), channel_id=1, source_target_pairs={{0,1},{1,0},{2,3},{3,2},{4,5},{5,4},{6,7},{7,6},{8,9},{9,8},{10,11... | collective-permute-start | bytes 393224 | tf_op jit(solution)/shard_map/ppermute | solution.py:13
  46.9 0.0 copy-done.8
  46.9 9.2 %collective-permute-done.5 = f32[256,128]{1,0:T(8,128)S(1)} collective-permute-done((f32[256,128]{1,0:T(8,128)S(1)}, f32[256,128]{1,0:T(8,128)S(1)}, u32[]{:S(2)}, u32[]{:S(2)}) %collective-permute-start.5) | collective-permute-done | bytes 131104 | tf_op jit(solution)/shard_map/ppermute | solution.py:13
  56.2 0.0 all-to-all-done
  56.3 0.1 fusion.19
  56.4 0.1 fusion.3
  56.6 0.8 copy.20
  57.4 6.0 %all-to-all-start.1 = ((f32[16,7,4,128]{3,2,1,0:T(4,128)}), f32[16,7,4,128]{3,2,1,0:T(4,128)S(1)}, u32[]{:S(2)}, u32[]{:S(2)}) async-start(f32[16,7,4,128]{3,2,1,0:T(4,128)} %copy.20), calls=%async_computation.1 | async-start | bytes 458752 | tf_op jit(solution)/shard_map/all_to_all | solution.py:322
  63.4 6.6 %all-gather = f32[1,48,128]{2,0,1:T(1,128)S(1)} all-gather(f32[1,12,128]{2,0,1:T(1,128)S(1)} %copy.21), channel_id=2, replica_groups={{0,32,64,96},{128,160,192,224},{256,288,320,352},{384,416,448,480},{1,3..., dimensions={1}, use_global_device_ids=true | all-gather | bytes 30720 | tf_op jit(solution)/shard_map/all_gather | solution.py:275
  70.0 2.4 %collective-permute-start.6 = (f32[48,128]{1,0:T(8,128)S(1)}, f32[48,128]{1,0:T(8,128)S(1)}, u32[]{:S(2)}, u32[]{:S(2)}) collective-permute-start(f32[48,128]{1,0:T(8,128)S(1)} %bitcast.27), channel_id=1, source_target_pairs={{0,128},{32,160},{64,192},{96,224},{128,0},{160,32},{192,64},{224,... | collective-permute-start | bytes 73736 | tf_op jit(solution)/shard_map/ppermute | solution.py:279
  72.4 2.6 %collective-permute-start.7 = (f32[48,128]{1,0:T(8,128)S(1)}, f32[48,128]{1,0:T(8,128)S(1)}, u32[]{:S(2)}, u32[]{:S(2)}) collective-permute-start(f32[48,128]{1,0:T(8,128)S(1)} %bitcast.28), channel_id=1, source_target_pairs={{0,1},{1,0},{2,3},{3,2},{4,5},{5,4},{6,7},{7,6},{8,9},{9,8},{10,11... | collective-permute-start | bytes 73736 | tf_op jit(solution)/shard_map/ppermute | solution.py:13
  75.1 0.9 all-to-all-done.1
  76.0 0.1 reduce_sum.19
  76.1 0.0 collective-permute-done.6.beside_y
  76.1 2.7 %collective-permute-done.7.above_y = f32[48,128]{1,0:T(8,128)S(1)} collective-permute-done((f32[48,128]{1,0:T(8,128)S(1)}, f32[48,128]{1,0:T(8,128)S(1)}, u32[]{:S(2)}, u32[]{:S(2)}) %collective-permute-start.7) | collective-permute-done | bytes 24608 | tf_op jit(solution)/shard_map/ppermute | solution.py:13
  78.8 0.7 broadcast_in_dim.8
  79.5 11.4 %all-to-all-start.2 = ((f32[16,16,128]{2,1,0:T(8,128)}), f32[16,16,128]{2,1,0:T(8,128)S(1)}, u32[]{:S(2)}, u32[]{:S(2)}) async-start(f32[16,16,128]{2,1,0:T(8,128)} %broadcast_in_dim.8), calls=%async_computation.2 | async-start | bytes 262144 | tf_op jit(solution)/shard_map/all_to_all | solution.py:322
  90.9 3.4 %collective-permute-start.8 = (f32[48,128]{1,0:T(8,128)S(1)}, f32[48,128]{1,0:T(8,128)S(1)}, u32[]{:S(2)}, u32[]{:S(2)}) collective-permute-start(f32[48,128]{1,0:T(8,128)S(1)} %bitcast.29), channel_id=1, source_target_pairs={{0,129},{1,128},{32,161},{33,160},{64,193},{65,192},{96,225},{97,2... | collective-permute-start | bytes 73736 | tf_op jit(solution)/shard_map/ppermute | solution.py:283
  94.3 7.1 %all-gather.1 = f32[4,4,128]{2,1,0:T(4,128)S(1)} all-gather(f32[1,4,128]{2,1,0:T(4,128)S(1)} %slice_bitcast_fusion.1), channel_id=1, replica_groups={{0,32,64,96},{128,160,192,224},{256,288,320,352},{384,416,448,480},{1,3..., dimensions={0}, use_global_device_ids=true | all-gather | bytes 10240 | tf_op jit(solution)/shard_map/all_gather | solution.py:275
  101.5 2.3 %collective-permute-start.9 = (f32[16,128]{1,0:T(8,128)S(1)}, f32[16,128]{1,0:T(8,128)S(1)}, u32[]{:S(2)}, u32[]{:S(2)}) collective-permute-start(f32[16,128]{1,0:T(8,128)S(1)} %bitcast.31), channel_id=1, source_target_pairs={{0,128},{32,160},{64,192},{96,224},{128,0},{160,32},{192,64},{224,... | collective-permute-start | bytes 24584 | tf_op jit(solution)/shard_map/ppermute | solution.py:279
  103.8 0.6 mul.39
  104.4 0.0 collective-permute-done.8.cross_y
  104.4 1.7 %collective-permute-done.9.beside_z = f32[16,128]{1,0:T(8,128)S(1)} collective-permute-done((f32[16,128]{1,0:T(8,128)S(1)}, f32[16,128]{1,0:T(8,128)S(1)}, u32[]{:S(2)}, u32[]{:S(2)}) %collective-permute-start.9) | collective-permute-done | bytes 8224 | tf_op jit(solution)/shard_map/ppermute | solution.py:279
  106.2 0.7 unfold_factors.1
  106.8 0.0 all-to-all-done.2
  106.8 0.7 multiply_bitcast_fusion
  (27 shorter events, 0.3 us)
Async XLA Ops:
  0.6 1.7 %copy-start = (f32[3,16,96,128]{3,2,1,0:T(8,128)S(1)}, f32[3,16,96,128]{3,2,1,0:T(8,128)}, u32[]{:S(2)}) copy-start(f32[3,16,96,128]{3,2,1,0:T(8,128)} %vel.3) | copy-start | bytes 7077892
  2.3 28.0 %copy-start.1 = (f32[3,2,96,128]{3,2,1,0:T(8,128)S(1)}, f32[3,2,96,128]{3,2,1,0:T(8,128)}, u32[]{:S(2)}) copy-start(f32[3,2,96,128]{3,2,1,0:T(8,128)} %below.1) | copy-start | bytes 884740
  2.3 28.0 %copy-start.2 = (f32[3,2,96,128]{3,2,1,0:T(8,128)S(1)}, f32[3,2,96,128]{3,2,1,0:T(8,128)}, u32[]{:S(2)}) copy-start(f32[3,2,96,128]{3,2,1,0:T(8,128)} %above.1) | copy-start | bytes 884740
  2.3 28.0 %copy-start.3 = (s32[512,128]{1,0:T(8,128)S(1)}, s32[512,128]{1,0:T(8,128)}, u32[]{:S(2)}) copy-start(s32[512,128]{1,0:T(8,128)} %phi_x.1) | copy-start | bytes 786436
  2.3 28.0 %copy-start.4 = (s32[128,256]{1,0:T(8,128)S(1)}, s32[128,256]{1,0:T(8,128)}, u32[]{:S(2)}) copy-start(s32[128,256]{1,0:T(8,128)} %omega_x.1) | copy-start | bytes 393220
  2.3 28.0 %copy-start.5 = (s32[96,256]{1,0:T(8,128)S(1)}, s32[96,256]{1,0:T(8,128)}, u32[]{:S(2)}) copy-start(s32[96,256]{1,0:T(8,128)} %omega_y.1) | copy-start | bytes 294916
  2.3 28.0 %copy-start.6 = (s32[16,256]{1,0:T(8,128)S(1)}, s32[16,256]{1,0:T(8,128)}, u32[]{:S(2)}) copy-start(s32[16,256]{1,0:T(8,128)} %omega_z.1) | copy-start | bytes 49156
  2.3 28.0 %copy-start.7 = (s32[2,16]{1,0:T(2,128)S(1)}, s32[2,16]{1,0:T(2,128)}, u32[]{:S(2)}) copy-start(s32[2,16]{1,0:T(2,128)} %phi_z.1) | copy-start | bytes 388
  3.1 27.3 %collective-permute-start = (f32[3,2,96,128]{3,2,1,0:T(8,128)S(1)}, f32[3,2,96,128]{3,2,1,0:T(8,128)S(1)}, u32[]{:S(2)}, u32[]{:S(2)}) collective-permute-start(f32[3,2,96,128]{3,2,1,0:T(8,128)S(1)} %get-tuple-element.17), channel_id=1, source_target_pairs={{0,1},{1,0},{2,3},{3,2},{4,5},{5,4},{6,7},{7,6},{8,9},{9,8},{10,11... | collective-permute-start | bytes 884744 | tf_op jit(solution)/shard_map/ppermute | solution.py:13
  8.7 20.7 %collective-permute-start.1 = (f32[3,32,128]{2,1,0:T(8,128)S(1)}, f32[3,32,128]{2,1,0:T(8,128)S(1)}, u32[]{:S(2)}, u32[]{:S(2)}) collective-permute-start(f32[3,32,128]{2,1,0:T(8,128)S(1)} %get-tuple-element.18), channel_id=1, source_target_pairs={{0,2},{2,0},{4,6},{6,4},{8,10},{10,8},{12,14},{14,12},{16,18},{18,... | collective-permute-start | bytes 147464 | tf_op jit(solution)/shard_map/ppermute | solution.py:21
  12.3 17.2 %collective-permute-start.2 = (f32[3,32,128]{2,1,0:T(8,128)S(1)}, f32[3,32,128]{2,1,0:T(8,128)S(1)}, u32[]{:S(2)}, u32[]{:S(2)}) collective-permute-start(f32[3,32,128]{2,1,0:T(8,128)S(1)} %get-tuple-element.19), channel_id=1, source_target_pairs={{2,4},{4,2},{6,8},{8,6},{10,12},{12,10},{14,16},{16,14},{18,20},{2... | collective-permute-start | bytes 147464 | tf_op jit(solution)/shard_map/ppermute | solution.py:21
  22.5 7.0 %collective-permute-start.3 = (f32[96,128]{1,0:T(8,128)S(1)}, f32[96,128]{1,0:T(8,128)S(1)}, u32[]{:S(2)}, u32[]{:S(2)}) collective-permute-start(f32[96,128]{1,0:T(8,128)S(1)} %get-tuple-element.20), channel_id=1, source_target_pairs={{32,64},{64,32},{96,128},{128,96},{160,192},{192,160},{224,256},{2... | collective-permute-start | bytes 147464 | tf_op jit(solution)/shard_map/ppermute | solution.py:21
  26.2 20.7 %copy-start.8 = (s32[512,96]{0,1:T(8,128)S(1)}, s32[512,96]{0,1:T(8,128)}, u32[]{:S(2)}) copy-start(s32[512,96]{0,1:T(8,128)} %param.16) | copy-start | bytes 589828
  26.2 4.1 %collective-permute-start.4 = (f32[96,128]{1,0:T(8,128)S(1)}, f32[96,128]{1,0:T(8,128)S(1)}, u32[]{:S(2)}, u32[]{:S(2)}) collective-permute-start(f32[96,128]{1,0:T(8,128)S(1)} %get-tuple-element.21), channel_id=1, source_target_pairs={{0,32},{32,0},{64,96},{96,64},{128,160},{160,128},{192,224},{224,1... | collective-permute-start | bytes 147464 | tf_op jit(solution)/shard_map/ppermute | solution.py:21
  36.9 19.3 %all-to-all-start = ((f32[32,40,128]{2,1,0:T(8,128)}), f32[32,40,128]{2,1,0:T(8,128)S(1)}, u32[]{:S(2)}, u32[]{:S(2)}) async-start(f32[32,40,128]{2,1,0:T(8,128)} %bitcast), calls=%async_computation | async-start | bytes 1310720 | tf_op jit(solution)/shard_map/all_to_all | solution.py:322
  42.1 14.0 %collective-permute-start.5 = (f32[256,128]{1,0:T(8,128)S(1)}, f32[256,128]{1,0:T(8,128)S(1)}, u32[]{:S(2)}, u32[]{:S(2)}) collective-permute-start(f32[256,128]{1,0:T(8,128)S(1)} %get-tuple-element.23), channel_id=1, source_target_pairs={{0,1},{1,0},{2,3},{3,2},{4,5},{5,4},{6,7},{7,6},{8,9},{9,8},{10,11... | collective-permute-start | bytes 393224 | tf_op jit(solution)/shard_map/ppermute | solution.py:13
  57.4 18.6 %all-to-all-start.1 = ((f32[16,7,4,128]{3,2,1,0:T(4,128)}), f32[16,7,4,128]{3,2,1,0:T(4,128)S(1)}, u32[]{:S(2)}, u32[]{:S(2)}) async-start(f32[16,7,4,128]{3,2,1,0:T(4,128)} %copy.20), calls=%async_computation.1 | async-start | bytes 458752 | tf_op jit(solution)/shard_map/all_to_all | solution.py:322
  70.0 6.0 %collective-permute-start.6 = (f32[48,128]{1,0:T(8,128)S(1)}, f32[48,128]{1,0:T(8,128)S(1)}, u32[]{:S(2)}, u32[]{:S(2)}) collective-permute-start(f32[48,128]{1,0:T(8,128)S(1)} %bitcast.27), channel_id=1, source_target_pairs={{0,128},{32,160},{64,192},{96,224},{128,0},{160,32},{192,64},{224,... | collective-permute-start | bytes 73736 | tf_op jit(solution)/shard_map/ppermute | solution.py:279
  72.4 6.4 %collective-permute-start.7 = (f32[48,128]{1,0:T(8,128)S(1)}, f32[48,128]{1,0:T(8,128)S(1)}, u32[]{:S(2)}, u32[]{:S(2)}) collective-permute-start(f32[48,128]{1,0:T(8,128)S(1)} %bitcast.28), channel_id=1, source_target_pairs={{0,1},{1,0},{2,3},{3,2},{4,5},{5,4},{6,7},{7,6},{8,9},{9,8},{10,11... | collective-permute-start | bytes 73736 | tf_op jit(solution)/shard_map/ppermute | solution.py:13
  79.5 27.4 %all-to-all-start.2 = ((f32[16,16,128]{2,1,0:T(8,128)}), f32[16,16,128]{2,1,0:T(8,128)S(1)}, u32[]{:S(2)}, u32[]{:S(2)}) async-start(f32[16,16,128]{2,1,0:T(8,128)} %broadcast_in_dim.8), calls=%async_computation.2 | async-start | bytes 262144 | tf_op jit(solution)/shard_map/all_to_all | solution.py:322
  90.9 13.5 %collective-permute-start.8 = (f32[48,128]{1,0:T(8,128)S(1)}, f32[48,128]{1,0:T(8,128)S(1)}, u32[]{:S(2)}, u32[]{:S(2)}) collective-permute-start(f32[48,128]{1,0:T(8,128)S(1)} %bitcast.29), channel_id=1, source_target_pairs={{0,129},{1,128},{32,161},{33,160},{64,193},{65,192},{96,225},{97,2... | collective-permute-start | bytes 73736 | tf_op jit(solution)/shard_map/ppermute | solution.py:283
  101.5 4.7 %collective-permute-start.9 = (f32[16,128]{1,0:T(8,128)S(1)}, f32[16,128]{1,0:T(8,128)S(1)}, u32[]{:S(2)}, u32[]{:S(2)}) collective-permute-start(f32[16,128]{1,0:T(8,128)S(1)} %bitcast.31), channel_id=1, source_target_pairs={{0,128},{32,160},{64,192},{96,224},{128,0},{160,32},{192,64},{224,... | collective-permute-start | bytes 24584 | tf_op jit(solution)/shard_map/ppermute | solution.py:279

commit v9 on v8

--- a/solution.py
+++ b/solution.py
@@ -279,11 +279,7 @@
     return lax.ppermute(rows, "gx", [(i, i ^ 4) for i in range(16)])
 
 
-def cross_swap(rows):
-    return lax.ppermute(rows, ("gx", "gz"), [(i, i ^ 9) for i in range(32)])
-
-
-def unfold_kernel(own_y, beside_y, above_y, cross_y, own_z, beside_z, factor_y, factor_z):
+def unfold_kernel(both_y, beside_y, own_z, beside_z, factor_y, factor_z):
     scale_y = 1.0 / math.sqrt(2048 * 32)
     scale_z = 1.0 / math.sqrt(2048 * 1536)
     gz = lax.axis_index("gz")
@@ -291,8 +287,8 @@
     for x in range(2):
         rows_z = jnp.where(pair == x, own_z[...], beside_z[...]) * scale_z
         for z in range(2):
-            near = jnp.where(gz == z, own_y[...], above_y[...])
-            away = jnp.where(gz == z, beside_y[...], cross_y[...])
+            near = jnp.where(gz == z, both_y[0:48, :], both_y[48:96, :])
+            away = jnp.where(gz == z, beside_y[0:48, :], beside_y[48:96, :])
             rows_y = jnp.where(pair == x, near, away) * scale_y
             for r in range(4):
                 rank = 4 * x + r
@@ -309,7 +305,7 @@
     whole = pl.BlockSpec(memory_space=pltpu.VMEM)
     return pl.pallas_call(
         unfold_kernel,
-        in_specs=[whole] * 6,
+        in_specs=[whole] * 4,
         out_specs=[whole] * 2,
         out_shape=[jax.ShapeDtypeStruct((96, 256), jnp.float32), jax.ShapeDtypeStruct((16, 256), jnp.float32)],
         compiler_params=pltpu.CompilerParams(vmem_limit_bytes=4 * 1024 * 1024),
@@ -356,13 +352,11 @@
     core_sketch = got[:8].reshape(1, 2, 512) * (1.0 / math.sqrt(total_x * total_y * total_z))
 
     own_y = gather(summed[24:36])
-    cross_y = cross_swap(own_y)
-    rows, own_y, beside_y, above_y = lax.optimization_barrier(
-        (got[8:28], own_y, pair_swap(own_y), shift_permute(own_y, "gz", 1))
-    )
+    both_y = jnp.concatenate([own_y, shift_permute(own_y, "gz", 1)], axis=0)
+    rows, both_y, beside_y = lax.optimization_barrier((got[8:28], both_y, pair_swap(both_y)))
     got_x = exchange(jnp.broadcast_to(rows[None, :16], (16, 16, 128)).reshape(256, 128), "gy")
     own_z = gather(rows[16:])
-    factor_y, factor_z = unfold(own_y, beside_y, above_y, cross_y, own_z, pair_swap(own_z))
+    factor_y, factor_z = unfold(both_y, beside_y, own_z, pair_swap(own_z))
 
     factor_x = got_x.reshape(16, 2, 8, 128).transpose(0, 2, 1, 3).reshape(128, 256)
     factor_x = factor_x * (1.0 / math.sqrt(total_y * total_z))

time: 108 us -> 109 us (level); the launches traced: 108 us -> 107 us
  starting transfers between devices: 64.5 us -> 61 us
  waiting for transfers between devices: 15.4 us -> 18 us
    ppermute x1 -> x0, starting transfers between devices: 3.39 us -> none  [cross_swap(): return lax.ppermute(rows, ('gx', 'gz'), [(i, i ^ 9) for i in range(32)])]
    ppermute x2, waiting for transfers between devices: 1.74 us -> 4.29 us  [pair_swap(): return lax.ppermute(rows, 'gx', [(i, i ^ 4) for i in range(16)])]
  transfers between devices with their start and end apart: 13 -> 12, of which waited for: 5 -> 5; matrix products, arithmetic and copies ran while one was open for 1% -> 1% of each run, Pallas kernels for 1% -> 1%
where the time goes in v9:
time: 109 us; the launch traced here: 107 us
  starting transfers between devices  61 us (56%)
  waiting for transfers between devices  18 us (17%)
  blocking collectives  14.4 us (13%)
  Pallas kernels  7.87 us (7%)
  local copies, waits for them, and re-layouts  3.9 us (4%)
    all_to_all x3, starting transfers between devices, exchange(): return lax.all_to_all(rows, axes, 0, 0, tiled=True)  22.4 us
    ppermute x4, starting transfers between devices, edge_swap(): return lax.ppermute(cells, axis, pairs)  20.7 us
    all_gather x2, blocking collectives, gather(): lax.all_gather(rows, 'gx', axis=0, tiled=True, axis_index_groups=NEAR)  14.4 us
    ppermute x3, starting transfers between devices, shift_permute(): lax.ppermute(cells, axis, [(i, (i + step) % count) for i in range(count)])  13.1 us
    ppermute x3, waiting for transfers between devices, shift_permute(): lax.ppermute(cells, axis, [(i, (i + step) % count) for i in range(count)])  12.9 us
    pallas_call x1, Pallas kernels, field(): pl.pallas_call(field_kernel, in_specs=[outside] * 13, out_specs=[whole] *...  6.5 us
    ppermute x2, starting transfers between devices, pair_swap(): return lax.ppermute(rows, 'gx', [(i, i ^ 4) for i in range(16)])  4.77 us
    ppermute x2, waiting for transfers between devices, pair_swap(): return lax.ppermute(rows, 'gx', [(i, i ^ 4) for i in range(16)])  4.29 us
  transfers between devices with their start and end apart: 12, of which 5 were waited for; matrix products, arithmetic and copies ran while one was open for 1% of the time, Pallas kernels for 1%

profile of v9, /device:TPU:1, one launch (start us, length us, event | category | flops | bytes accessed | tf_op | source)
XLA Modules:
  0.0 107.1 jit_solution(16318771024619764513)
XLA Ops:
  0.6 0.0 copy-start
  0.6 1.7 %copy-done = f32[3,16,96,128]{3,2,1,0:T(8,128)S(1)} copy-done((f32[3,16,96,128]{3,2,1,0:T(8,128)S(1)}, f32[3,16,96,128]{3,2,1,0:T(8,128)}, u32[]{:S(2)}) %copy-start) | copy-done | bytes 2359320
  2.3 0.0 copy-start.5
  2.3 0.0 copy-start.6
  2.3 0.0 copy-start.7
  2.3 0.7 pack_halos.1
  3.1 5.7 %collective-permute-start = (f32[3,2,96,128]{3,2,1,0:T(8,128)S(1)}, f32[3,2,96,128]{3,2,1,0:T(8,128)S(1)}, u32[]{:S(2)}, u32[]{:S(2)}) collective-permute-start(f32[3,2,96,128]{3,2,1,0:T(8,128)S(1)} %get-tuple-element.16), channel_id=1, source_target_pairs={{0,1},{1,0},{2,3},{3,2},{4,5},{5,4},{6,7},{7,6},{8,9},{9,8},{10,11... | collective-permute-start | bytes 884744 | tf_op jit(solution)/shard_map/ppermute | solution.py:13
  8.7 3.5 %collective-permute-start.1 = (f32[3,32,128]{2,1,0:T(8,128)S(1)}, f32[3,32,128]{2,1,0:T(8,128)S(1)}, u32[]{:S(2)}, u32[]{:S(2)}) collective-permute-start(f32[3,32,128]{2,1,0:T(8,128)S(1)} %get-tuple-element.17), channel_id=1, source_target_pairs={{0,2},{2,0},{4,6},{6,4},{8,10},{10,8},{12,14},{14,12},{16,18},{18,... | collective-permute-start | bytes 147464 | tf_op jit(solution)/shard_map/ppermute | solution.py:21
  12.3 10.2 %collective-permute-start.2 = (f32[3,32,128]{2,1,0:T(8,128)S(1)}, f32[3,32,128]{2,1,0:T(8,128)S(1)}, u32[]{:S(2)}, u32[]{:S(2)}) collective-permute-start(f32[3,32,128]{2,1,0:T(8,128)S(1)} %get-tuple-element.18), channel_id=1, source_target_pairs={{2,4},{4,2},{6,8},{8,6},{10,12},{12,10},{14,16},{16,14},{18,20},{2... | collective-permute-start | bytes 147464 | tf_op jit(solution)/shard_map/ppermute | solution.py:21
  22.5 3.7 %collective-permute-start.3 = (f32[96,128]{1,0:T(8,128)S(1)}, f32[96,128]{1,0:T(8,128)S(1)}, u32[]{:S(2)}, u32[]{:S(2)}) collective-permute-start(f32[96,128]{1,0:T(8,128)S(1)} %get-tuple-element.19), channel_id=1, source_target_pairs={{32,64},{64,32},{96,128},{128,96},{160,192},{192,160},{224,256},{2... | collective-permute-start | bytes 147464 | tf_op jit(solution)/shard_map/ppermute | solution.py:21
  26.2 0.0 copy-start.8
  26.2 3.2 %collective-permute-start.4 = (f32[96,128]{1,0:T(8,128)S(1)}, f32[96,128]{1,0:T(8,128)S(1)}, u32[]{:S(2)}, u32[]{:S(2)}) collective-permute-start(f32[96,128]{1,0:T(8,128)S(1)} %get-tuple-element.20), channel_id=1, source_target_pairs={{0,32},{32,0},{64,96},{96,64},{128,160},{160,128},{192,224},{224,1... | collective-permute-start | bytes 147464 | tf_op jit(solution)/shard_map/ppermute | solution.py:21
  29.5 0.0 collective-permute-done.1.y_even
  29.5 0.0 collective-permute-done.2.y_odd
  29.5 0.0 collective-permute-done.3.x_odd
  29.5 0.8 collective-permute-done.4.x_even
  30.3 0.0 collective-permute-done.far
  30.3 0.0 copy-done.1
  30.3 0.0 copy-done.2
  30.3 0.0 copy-done.3
  30.3 0.0 copy-done.4
  30.3 0.0 copy-done.5
  30.3 0.0 copy-done.6
  30.4 6.5 %field_products.1 = (f32[1280,128]{1,0:T(8,128)}, f32[256,128]{1,0:T(8,128)S(1)}) custom-call(f32[3,16,96,128]{3,2,1,0:T(8,128)S(1)} %copy-done, f32[3,2,96,128]{3,2,1,0:T(8,128)S(1)} %collective-permute-done.far, f32[3,2,96,128]{3,2,1,0:T(8,128)S(1)} %copy-done.1, f32[3,2,96,128]{3,2,1,0:T(8,128)S(1)} %copy-done.2, ...), custom_call_target="tpu_custom_call" | custom-call | tf_op jit(solution)/shard_map/field_products/pallas_call | solution.py:235
  36.9 5.2 %all-to-all-start = ((f32[32,40,128]{2,1,0:T(8,128)}), f32[32,40,128]{2,1,0:T(8,128)S(1)}, u32[]{:S(2)}, u32[]{:S(2)}) async-start(f32[32,40,128]{2,1,0:T(8,128)} %bitcast), calls=%async_computation | async-start | bytes 1310720 | tf_op jit(solution)/shard_map/all_to_all | solution.py:318
  42.1 4.8 %collective-permute-start.5 = (f32[256,128]{1,0:T(8,128)S(1)}, f32[256,128]{1,0:T(8,128)S(1)}, u32[]{:S(2)}, u32[]{:S(2)}) collective-permute-start(f32[256,128]{1,0:T(8,128)S(1)} %get-tuple-element.22), channel_id=1, source_target_pairs={{0,1},{1,0},{2,3},{3,2},{4,5},{5,4},{6,7},{7,6},{8,9},{9,8},{10,11... | collective-permute-start | bytes 393224 | tf_op jit(solution)/shard_map/ppermute | solution.py:13
  46.9 9.2 %collective-permute-done.5 = f32[256,128]{1,0:T(8,128)S(1)} collective-permute-done((f32[256,128]{1,0:T(8,128)S(1)}, f32[256,128]{1,0:T(8,128)S(1)}, u32[]{:S(2)}, u32[]{:S(2)}) %collective-permute-start.5) | collective-permute-done | bytes 131104 | tf_op jit(solution)/shard_map/ppermute | solution.py:13
  56.2 0.0 all-to-all-done
  56.3 0.1 fusion.19
  56.4 0.1 fusion.3
  56.6 0.8 copy.20
  57.4 6.0 %all-to-all-start.1 = ((f32[16,7,4,128]{3,2,1,0:T(4,128)}), f32[16,7,4,128]{3,2,1,0:T(4,128)S(1)}, u32[]{:S(2)}, u32[]{:S(2)}) async-start(f32[16,7,4,128]{3,2,1,0:T(4,128)} %copy.20), calls=%async_computation.1 | async-start | bytes 458752 | tf_op jit(solution)/shard_map/all_to_all | solution.py:318
  63.4 6.6 %all-gather = f32[1,48,128]{2,0,1:T(1,128)S(1)} all-gather(f32[1,12,128]{2,0,1:T(1,128)S(1)} %copy.21), channel_id=2, replica_groups={{0,32,64,96},{128,160,192,224},{256,288,320,352},{384,416,448,480},{1,3..., dimensions={1}, use_global_device_ids=true | all-gather | bytes 30720 | tf_op jit(solution)/shard_map/all_gather | solution.py:275
  70.0 2.7 %collective-permute-start.6 = (f32[48,128]{1,0:T(8,128)S(1)}, f32[48,128]{1,0:T(8,128)S(1)}, u32[]{:S(2)}, u32[]{:S(2)}) collective-permute-start(f32[48,128]{1,0:T(8,128)S(1)} %bitcast.32), channel_id=1, source_target_pairs={{0,1},{1,0},{2,3},{3,2},{4,5},{5,4},{6,7},{7,6},{8,9},{9,8},{10,11... | collective-permute-start | bytes 73736 | tf_op jit(solution)/shard_map/ppermute | solution.py:13
  72.7 3.7 %collective-permute-done.6 = f32[48,128]{1,0:T(8,128)S(1)} collective-permute-done((f32[48,128]{1,0:T(8,128)S(1)}, f32[48,128]{1,0:T(8,128)S(1)}, u32[]{:S(2)}, u32[]{:S(2)}) %collective-permute-start.6) | collective-permute-done | bytes 24608 | tf_op jit(solution)/shard_map/ppermute | solution.py:13
  76.4 2.4 %collective-permute-start.7 = (f32[96,128]{1,0:T(8,128)S(1)}, f32[96,128]{1,0:T(8,128)S(1)}, u32[]{:S(2)}, u32[]{:S(2)}) collective-permute-start(f32[96,128]{1,0:T(8,128)S(1)} %pad_maximum_fusion.1.both_y), channel_id=1, source_target_pairs={{0,128},{32,160},{64,192},{96,224},{128,0},{160,32},{192,64},{224,... | collective-permute-start | bytes 147464 | tf_op jit(solution)/shard_map/ppermute | solution.py:279
  78.8 0.0 all-to-all-done.1
  78.8 0.1 reduce_sum.19
  78.9 2.6 %collective-permute-done.7.beside_y = f32[96,128]{1,0:T(8,128)S(1)} collective-permute-done((f32[96,128]{1,0:T(8,128)S(1)}, f32[96,128]{1,0:T(8,128)S(1)}, u32[]{:S(2)}, u32[]{:S(2)}) %collective-permute-start.7) | collective-permute-done | bytes 49184 | tf_op jit(solution)/shard_map/ppermute | solution.py:279
  81.5 0.7 broadcast_in_dim.8
  82.2 11.2 %all-to-all-start.2 = ((f32[16,16,128]{2,1,0:T(8,128)}), f32[16,16,128]{2,1,0:T(8,128)S(1)}, u32[]{:S(2)}, u32[]{:S(2)}) async-start(f32[16,16,128]{2,1,0:T(8,128)} %broadcast_in_dim.8), calls=%async_computation.2 | async-start | bytes 262144 | tf_op jit(solution)/shard_map/all_to_all | solution.py:318
  93.4 7.7 %all-gather.1 = f32[4,4,128]{2,1,0:T(4,128)S(1)} all-gather(f32[1,4,128]{2,1,0:T(4,128)S(1)} %slice_bitcast_fusion.1), channel_id=1, replica_groups={{0,32,64,96},{128,160,192,224},{256,288,320,352},{384,416,448,480},{1,3..., dimensions={0}, use_global_device_ids=true | all-gather | bytes 10240 | tf_op jit(solution)/shard_map/all_gather | solution.py:275
  101.1 2.4 %collective-permute-start.8 = (f32[16,128]{1,0:T(8,128)S(1)}, f32[16,128]{1,0:T(8,128)S(1)}, u32[]{:S(2)}, u32[]{:S(2)}) collective-permute-start(f32[16,128]{1,0:T(8,128)S(1)} %bitcast.27), channel_id=1, source_target_pairs={{0,128},{32,160},{64,192},{96,224},{128,0},{160,32},{192,64},{224,... | collective-permute-start | bytes 24584 | tf_op jit(solution)/shard_map/ppermute | solution.py:279
  103.5 0.6 mul.39
  104.1 1.7 %collective-permute-done.8.beside_z = f32[16,128]{1,0:T(8,128)S(1)} collective-permute-done((f32[16,128]{1,0:T(8,128)S(1)}, f32[16,128]{1,0:T(8,128)S(1)}, u32[]{:S(2)}, u32[]{:S(2)}) %collective-permute-start.8) | collective-permute-done | bytes 8224 | tf_op jit(solution)/shard_map/ppermute | solution.py:279
  105.8 0.7 unfold_factors.1
  106.4 0.0 all-to-all-done.2
  106.5 0.7 multiply_bitcast_fusion
  (26 shorter events, 0.3 us)
Async XLA Ops:
  0.6 1.7 %copy-start = (f32[3,16,96,128]{3,2,1,0:T(8,128)S(1)}, f32[3,16,96,128]{3,2,1,0:T(8,128)}, u32[]{:S(2)}) copy-start(f32[3,16,96,128]{3,2,1,0:T(8,128)} %vel.3) | copy-start | bytes 7077892
  2.3 28.0 %copy-start.1 = (f32[3,2,96,128]{3,2,1,0:T(8,128)S(1)}, f32[3,2,96,128]{3,2,1,0:T(8,128)}, u32[]{:S(2)}) copy-start(f32[3,2,96,128]{3,2,1,0:T(8,128)} %below.1) | copy-start | bytes 884740
  2.3 28.0 %copy-start.2 = (f32[3,2,96,128]{3,2,1,0:T(8,128)S(1)}, f32[3,2,96,128]{3,2,1,0:T(8,128)}, u32[]{:S(2)}) copy-start(f32[3,2,96,128]{3,2,1,0:T(8,128)} %above.1) | copy-start | bytes 884740
  2.3 28.0 %copy-start.3 = (s32[512,128]{1,0:T(8,128)S(1)}, s32[512,128]{1,0:T(8,128)}, u32[]{:S(2)}) copy-start(s32[512,128]{1,0:T(8,128)} %phi_x.1) | copy-start | bytes 786436
  2.3 28.0 %copy-start.4 = (s32[128,256]{1,0:T(8,128)S(1)}, s32[128,256]{1,0:T(8,128)}, u32[]{:S(2)}) copy-start(s32[128,256]{1,0:T(8,128)} %omega_x.1) | copy-start | bytes 393220
  2.3 28.0 %copy-start.5 = (s32[96,256]{1,0:T(8,128)S(1)}, s32[96,256]{1,0:T(8,128)}, u32[]{:S(2)}) copy-start(s32[96,256]{1,0:T(8,128)} %omega_y.1) | copy-start | bytes 294916
  2.3 28.0 %copy-start.6 = (s32[16,256]{1,0:T(8,128)S(1)}, s32[16,256]{1,0:T(8,128)}, u32[]{:S(2)}) copy-start(s32[16,256]{1,0:T(8,128)} %omega_z.1) | copy-start | bytes 49156
  2.3 28.0 %copy-start.7 = (s32[2,16]{1,0:T(2,128)S(1)}, s32[2,16]{1,0:T(2,128)}, u32[]{:S(2)}) copy-start(s32[2,16]{1,0:T(2,128)} %phi_z.1) | copy-start | bytes 388
  3.1 27.3 %collective-permute-start = (f32[3,2,96,128]{3,2,1,0:T(8,128)S(1)}, f32[3,2,96,128]{3,2,1,0:T(8,128)S(1)}, u32[]{:S(2)}, u32[]{:S(2)}) collective-permute-start(f32[3,2,96,128]{3,2,1,0:T(8,128)S(1)} %get-tuple-element.16), channel_id=1, source_target_pairs={{0,1},{1,0},{2,3},{3,2},{4,5},{5,4},{6,7},{7,6},{8,9},{9,8},{10,11... | collective-permute-start | bytes 884744 | tf_op jit(solution)/shard_map/ppermute | solution.py:13
  8.7 20.7 %collective-permute-start.1 = (f32[3,32,128]{2,1,0:T(8,128)S(1)}, f32[3,32,128]{2,1,0:T(8,128)S(1)}, u32[]{:S(2)}, u32[]{:S(2)}) collective-permute-start(f32[3,32,128]{2,1,0:T(8,128)S(1)} %get-tuple-element.17), channel_id=1, source_target_pairs={{0,2},{2,0},{4,6},{6,4},{8,10},{10,8},{12,14},{14,12},{16,18},{18,... | collective-permute-start | bytes 147464 | tf_op jit(solution)/shard_map/ppermute | solution.py:21
  12.3 17.2 %collective-permute-start.2 = (f32[3,32,128]{2,1,0:T(8,128)S(1)}, f32[3,32,128]{2,1,0:T(8,128)S(1)}, u32[]{:S(2)}, u32[]{:S(2)}) collective-permute-start(f32[3,32,128]{2,1,0:T(8,128)S(1)} %get-tuple-element.18), channel_id=1, source_target_pairs={{2,4},{4,2},{6,8},{8,6},{10,12},{12,10},{14,16},{16,14},{18,20},{2... | collective-permute-start | bytes 147464 | tf_op jit(solution)/shard_map/ppermute | solution.py:21
  22.5 7.0 %collective-permute-start.3 = (f32[96,128]{1,0:T(8,128)S(1)}, f32[96,128]{1,0:T(8,128)S(1)}, u32[]{:S(2)}, u32[]{:S(2)}) collective-permute-start(f32[96,128]{1,0:T(8,128)S(1)} %get-tuple-element.19), channel_id=1, source_target_pairs={{32,64},{64,32},{96,128},{128,96},{160,192},{192,160},{224,256},{2... | collective-permute-start | bytes 147464 | tf_op jit(solution)/shard_map/ppermute | solution.py:21
  26.2 20.7 %copy-start.8 = (s32[512,96]{0,1:T(8,128)S(1)}, s32[512,96]{0,1:T(8,128)}, u32[]{:S(2)}) copy-start(s32[512,96]{0,1:T(8,128)} %param.16) | copy-start | bytes 589828
  26.2 4.1 %collective-permute-start.4 = (f32[96,128]{1,0:T(8,128)S(1)}, f32[96,128]{1,0:T(8,128)S(1)}, u32[]{:S(2)}, u32[]{:S(2)}) collective-permute-start(f32[96,128]{1,0:T(8,128)S(1)} %get-tuple-element.20), channel_id=1, source_target_pairs={{0,32},{32,0},{64,96},{96,64},{128,160},{160,128},{192,224},{224,1... | collective-permute-start | bytes 147464 | tf_op jit(solution)/shard_map/ppermute | solution.py:21
  36.9 19.3 %all-to-all-start = ((f32[32,40,128]{2,1,0:T(8,128)}), f32[32,40,128]{2,1,0:T(8,128)S(1)}, u32[]{:S(2)}, u32[]{:S(2)}) async-start(f32[32,40,128]{2,1,0:T(8,128)} %bitcast), calls=%async_computation | async-start | bytes 1310720 | tf_op jit(solution)/shard_map/all_to_all | solution.py:318
  42.1 14.0 %collective-permute-start.5 = (f32[256,128]{1,0:T(8,128)S(1)}, f32[256,128]{1,0:T(8,128)S(1)}, u32[]{:S(2)}, u32[]{:S(2)}) collective-permute-start(f32[256,128]{1,0:T(8,128)S(1)} %get-tuple-element.22), channel_id=1, source_target_pairs={{0,1},{1,0},{2,3},{3,2},{4,5},{5,4},{6,7},{7,6},{8,9},{9,8},{10,11... | collective-permute-start | bytes 393224 | tf_op jit(solution)/shard_map/ppermute | solution.py:13
  57.4 21.4 %all-to-all-start.1 = ((f32[16,7,4,128]{3,2,1,0:T(4,128)}), f32[16,7,4,128]{3,2,1,0:T(4,128)S(1)}, u32[]{:S(2)}, u32[]{:S(2)}) async-start(f32[16,7,4,128]{3,2,1,0:T(4,128)} %copy.20), calls=%async_computation.1 | async-start | bytes 458752 | tf_op jit(solution)/shard_map/all_to_all | solution.py:318
  70.0 6.4 %collective-permute-start.6 = (f32[48,128]{1,0:T(8,128)S(1)}, f32[48,128]{1,0:T(8,128)S(1)}, u32[]{:S(2)}, u32[]{:S(2)}) collective-permute-start(f32[48,128]{1,0:T(8,128)S(1)} %bitcast.32), channel_id=1, source_target_pairs={{0,1},{1,0},{2,3},{3,2},{4,5},{5,4},{6,7},{7,6},{8,9},{9,8},{10,11... | collective-permute-start | bytes 73736 | tf_op jit(solution)/shard_map/ppermute | solution.py:13
  76.4 5.1 %collective-permute-start.7 = (f32[96,128]{1,0:T(8,128)S(1)}, f32[96,128]{1,0:T(8,128)S(1)}, u32[]{:S(2)}, u32[]{:S(2)}) collective-permute-start(f32[96,128]{1,0:T(8,128)S(1)} %pad_maximum_fusion.1.both_y), channel_id=1, source_target_pairs={{0,128},{32,160},{64,192},{96,224},{128,0},{160,32},{192,64},{224,... | collective-permute-start | bytes 147464 | tf_op jit(solution)/shard_map/ppermute | solution.py:279
  82.2 24.3 %all-to-all-start.2 = ((f32[16,16,128]{2,1,0:T(8,128)}), f32[16,16,128]{2,1,0:T(8,128)S(1)}, u32[]{:S(2)}, u32[]{:S(2)}) async-start(f32[16,16,128]{2,1,0:T(8,128)} %broadcast_in_dim.8), calls=%async_computation.2 | async-start | bytes 262144 | tf_op jit(solution)/shard_map/all_to_all | solution.py:318
  101.1 4.7 %collective-permute-start.8 = (f32[16,128]{1,0:T(8,128)S(1)}, f32[16,128]{1,0:T(8,128)S(1)}, u32[]{:S(2)}, u32[]{:S(2)}) collective-permute-start(f32[16,128]{1,0:T(8,128)S(1)} %bitcast.27), channel_id=1, source_target_pairs={{0,128},{32,160},{64,192},{96,224},{128,0},{160,32},{192,64},{224,... | collective-permute-start | bytes 24584 | tf_op jit(solution)/shard_map/ppermute | solution.py:279

commit v10 on v9

--- a/solution.py
+++ b/solution.py
@@ -279,16 +279,16 @@
     return lax.ppermute(rows, "gx", [(i, i ^ 4) for i in range(16)])
 
 
-def unfold_kernel(both_y, beside_y, own_z, beside_z, factor_y, factor_z):
+def unfold_kernel(own, beside, factor_y, factor_z):
     scale_y = 1.0 / math.sqrt(2048 * 32)
     scale_z = 1.0 / math.sqrt(2048 * 1536)
     gz = lax.axis_index("gz")
     pair = lax.rem(lax.axis_index("gx") // 4, 2)
     for x in range(2):
-        rows_z = jnp.where(pair == x, own_z[...], beside_z[...]) * scale_z
+        rows_z = jnp.where(pair == x, own[96:112, :], beside[96:112, :]) * scale_z
         for z in range(2):
-            near = jnp.where(gz == z, both_y[0:48, :], both_y[48:96, :])
-            away = jnp.where(gz == z, beside_y[0:48, :], beside_y[48:96, :])
+            near = jnp.where(gz == z, own[0:48, :], own[48:96, :])
+            away = jnp.where(gz == z, beside[0:48, :], beside[48:96, :])
             rows_y = jnp.where(pair == x, near, away) * scale_y
             for r in range(4):
                 rank = 4 * x + r
@@ -305,7 +305,7 @@
     whole = pl.BlockSpec(memory_space=pltpu.VMEM)
     return pl.pallas_call(
         unfold_kernel,
-        in_specs=[whole] * 4,
+        in_specs=[whole] * 2,
         out_specs=[whole] * 2,
         out_shape=[jax.ShapeDtypeStruct((96, 256), jnp.float32), jax.ShapeDtypeStruct((16, 256), jnp.float32)],
         compiler_params=pltpu.CompilerParams(vmem_limit_bytes=4 * 1024 * 1024),
@@ -353,10 +353,10 @@
 
     own_y = gather(summed[24:36])
     both_y = jnp.concatenate([own_y, shift_permute(own_y, "gz", 1)], axis=0)
-    rows, both_y, beside_y = lax.optimization_barrier((got[8:28], both_y, pair_swap(both_y)))
+    rows, both_y = lax.optimization_barrier((got[8:28], both_y))
     got_x = exchange(jnp.broadcast_to(rows[None, :16], (16, 16, 128)).reshape(256, 128), "gy")
-    own_z = gather(rows[16:])
-    factor_y, factor_z = unfold(both_y, beside_y, own_z, pair_swap(own_z))
+    own = jnp.concatenate([both_y, gather(rows[16:])], axis=0)
+    factor_y, factor_z = unfold(own, pair_swap(own))
 
     factor_x = got_x.reshape(16, 2, 8, 128).transpose(0, 2, 1, 3).reshape(128, 256)
     factor_x = factor_x * (1.0 / math.sqrt(total_y * total_z))

time: 109 us -> 104 us (0.954)
  starting transfers between devices: 61 us -> 58.9 us
  waiting for transfers between devices: 18 us -> 15.9 us
  blocking collectives: 14.4 us -> 13.2 us
    ppermute x2 -> x1, starting transfers between devices: 4.77 us -> 2.39 us  [pair_swap(): return lax.ppermute(rows, 'gx', [(i, i ^ 4) for i in range(16)])]
    ppermute x2 -> x1, waiting for transfers between devices: 4.29 us -> 2.19 us  [pair_swap(): return lax.ppermute(rows, 'gx', [(i, i ^ 4) for i in range(16)])]
    all_gather x2, blocking collectives: 14.4 us -> 13.2 us  [gather(): lax.all_gather(rows, 'gx', axis=0, tiled=True, axis_index_groups=NEAR)]
  transfers between devices with their start and end apart: 12 -> 11, of which waited for: 5 -> 4; matrix products, arithmetic and copies ran while one was open for 1% -> 1% of each run, Pallas kernels for 1% -> 1%
where the time goes in v10:
time: 104 us; the launch traced here: 102 us
  starting transfers between devices  58.9 us (57%)
  waiting for transfers between devices  15.9 us (15%)
  blocking collectives  13.2 us (13%)
  Pallas kernels  7.88 us (8%)
  local copies, waits for them, and re-layouts  3.9 us (4%)
    all_to_all x3, starting transfers between devices, exchange(): return lax.all_to_all(rows, axes, 0, 0, tiled=True)  22.7 us
    ppermute x4, starting transfers between devices, edge_swap(): return lax.ppermute(cells, axis, pairs)  20.7 us
    all_gather x2, blocking collectives, gather(): lax.all_gather(rows, 'gx', axis=0, tiled=True, axis_index_groups=NEAR)  13.2 us
    ppermute x3, starting transfers between devices, shift_permute(): lax.ppermute(cells, axis, [(i, (i + step) % count) for i in range(count)])  13.1 us
    ppermute x3, waiting for transfers between devices, shift_permute(): lax.ppermute(cells, axis, [(i, (i + step) % count) for i in range(count)])  12.9 us
    pallas_call x1, Pallas kernels, field(): pl.pallas_call(field_kernel, in_specs=[outside] * 13, out_specs=[whole] *...  6.5 us
    ppermute x1, starting transfers between devices, pair_swap(): return lax.ppermute(rows, 'gx', [(i, i ^ 4) for i in range(16)])  2.39 us
    ppermute x1, waiting for transfers between devices, pair_swap(): return lax.ppermute(rows, 'gx', [(i, i ^ 4) for i in range(16)])  2.19 us
  transfers between devices with their start and end apart: 11, of which 4 were waited for; matrix products, arithmetic and copies ran while one was open for 1% of the time, Pallas kernels for 1%

profile of v10, /device:TPU:1, one launch (start us, length us, event | category | flops | bytes accessed | tf_op | source)
XLA Modules:
  0.0 101.8 jit_solution(18297149653325131452)
XLA Ops:
  0.6 0.0 copy-start
  0.6 1.7 %copy-done = f32[3,16,96,128]{3,2,1,0:T(8,128)S(1)} copy-done((f32[3,16,96,128]{3,2,1,0:T(8,128)S(1)}, f32[3,16,96,128]{3,2,1,0:T(8,128)}, u32[]{:S(2)}) %copy-start) | copy-done | bytes 2359320
  2.3 0.0 copy-start.5
  2.3 0.0 copy-start.6
  2.3 0.0 copy-start.7
  2.3 0.7 pack_halos.1
  3.1 5.7 %collective-permute-start = (f32[3,2,96,128]{3,2,1,0:T(8,128)S(1)}, f32[3,2,96,128]{3,2,1,0:T(8,128)S(1)}, u32[]{:S(2)}, u32[]{:S(2)}) collective-permute-start(f32[3,2,96,128]{3,2,1,0:T(8,128)S(1)} %get-tuple-element.15), channel_id=1, source_target_pairs={{0,1},{1,0},{2,3},{3,2},{4,5},{5,4},{6,7},{7,6},{8,9},{9,8},{10,11... | collective-permute-start | bytes 884744 | tf_op jit(solution)/shard_map/ppermute | solution.py:13
  8.7 3.5 %collective-permute-start.1 = (f32[3,32,128]{2,1,0:T(8,128)S(1)}, f32[3,32,128]{2,1,0:T(8,128)S(1)}, u32[]{:S(2)}, u32[]{:S(2)}) collective-permute-start(f32[3,32,128]{2,1,0:T(8,128)S(1)} %get-tuple-element.16), channel_id=1, source_target_pairs={{0,2},{2,0},{4,6},{6,4},{8,10},{10,8},{12,14},{14,12},{16,18},{18,... | collective-permute-start | bytes 147464 | tf_op jit(solution)/shard_map/ppermute | solution.py:21
  12.3 10.2 %collective-permute-start.2 = (f32[3,32,128]{2,1,0:T(8,128)S(1)}, f32[3,32,128]{2,1,0:T(8,128)S(1)}, u32[]{:S(2)}, u32[]{:S(2)}) collective-permute-start(f32[3,32,128]{2,1,0:T(8,128)S(1)} %get-tuple-element.17), channel_id=1, source_target_pairs={{2,4},{4,2},{6,8},{8,6},{10,12},{12,10},{14,16},{16,14},{18,20},{2... | collective-permute-start | bytes 147464 | tf_op jit(solution)/shard_map/ppermute | solution.py:21
  22.5 3.7 %collective-permute-start.3 = (f32[96,128]{1,0:T(8,128)S(1)}, f32[96,128]{1,0:T(8,128)S(1)}, u32[]{:S(2)}, u32[]{:S(2)}) collective-permute-start(f32[96,128]{1,0:T(8,128)S(1)} %get-tuple-element.18), channel_id=1, source_target_pairs={{32,64},{64,32},{96,128},{128,96},{160,192},{192,160},{224,256},{2... | collective-permute-start | bytes 147464 | tf_op jit(solution)/shard_map/ppermute | solution.py:21
  26.2 0.0 copy-start.8
  26.2 3.2 %collective-permute-start.4 = (f32[96,128]{1,0:T(8,128)S(1)}, f32[96,128]{1,0:T(8,128)S(1)}, u32[]{:S(2)}, u32[]{:S(2)}) collective-permute-start(f32[96,128]{1,0:T(8,128)S(1)} %get-tuple-element.19), channel_id=1, source_target_pairs={{0,32},{32,0},{64,96},{96,64},{128,160},{160,128},{192,224},{224,1... | collective-permute-start | bytes 147464 | tf_op jit(solution)/shard_map/ppermute | solution.py:21
  29.5 0.0 collective-permute-done.1.y_even
  29.5 0.0 collective-permute-done.2.y_odd
  29.5 0.0 collective-permute-done.3.x_odd
  29.5 0.8 collective-permute-done.4.x_even
  30.3 0.0 collective-permute-done.far
  30.3 0.0 copy-done.1
  30.3 0.0 copy-done.2
  30.3 0.0 copy-done.3
  30.3 0.0 copy-done.4
  30.3 0.0 copy-done.5
  30.3 0.0 copy-done.6
  30.4 0.0 copy-done.7
  30.4 6.5 %field_products.1 = (f32[1280,128]{1,0:T(8,128)}, f32[256,128]{1,0:T(8,128)S(1)}) custom-call(f32[3,16,96,128]{3,2,1,0:T(8,128)S(1)} %copy-done, f32[3,2,96,128]{3,2,1,0:T(8,128)S(1)} %collective-permute-done.far, f32[3,2,96,128]{3,2,1,0:T(8,128)S(1)} %copy-done.1, f32[3,2,96,128]{3,2,1,0:T(8,128)S(1)} %copy-done.2, ...), custom_call_target="tpu_custom_call" | custom-call | tf_op jit(solution)/shard_map/field_products/pallas_call | solution.py:235
  36.9 5.2 %all-to-all-start = ((f32[32,40,128]{2,1,0:T(8,128)}), f32[32,40,128]{2,1,0:T(8,128)S(1)}, u32[]{:S(2)}, u32[]{:S(2)}) async-start(f32[32,40,128]{2,1,0:T(8,128)} %bitcast), calls=%async_computation | async-start | bytes 1310720 | tf_op jit(solution)/shard_map/all_to_all | solution.py:318
  42.1 4.8 %collective-permute-start.5 = (f32[256,128]{1,0:T(8,128)S(1)}, f32[256,128]{1,0:T(8,128)S(1)}, u32[]{:S(2)}, u32[]{:S(2)}) collective-permute-start(f32[256,128]{1,0:T(8,128)S(1)} %get-tuple-element.21), channel_id=1, source_target_pairs={{0,1},{1,0},{2,3},{3,2},{4,5},{5,4},{6,7},{7,6},{8,9},{9,8},{10,11... | collective-permute-start | bytes 393224 | tf_op jit(solution)/shard_map/ppermute | solution.py:13
  46.9 0.0 copy-done.8
  46.9 9.2 %collective-permute-done.5 = f32[256,128]{1,0:T(8,128)S(1)} collective-permute-done((f32[256,128]{1,0:T(8,128)S(1)}, f32[256,128]{1,0:T(8,128)S(1)}, u32[]{:S(2)}, u32[]{:S(2)}) %collective-permute-start.5) | collective-permute-done | bytes 131104 | tf_op jit(solution)/shard_map/ppermute | solution.py:13
  56.2 0.0 all-to-all-done
  56.3 0.1 fusion.19
  56.4 0.1 fusion.3
  56.6 0.8 copy.20
  57.4 6.0 %all-to-all-start.1 = ((f32[16,7,4,128]{3,2,1,0:T(4,128)}), f32[16,7,4,128]{3,2,1,0:T(4,128)S(1)}, u32[]{:S(2)}, u32[]{:S(2)}) async-start(f32[16,7,4,128]{3,2,1,0:T(4,128)} %copy.20), calls=%async_computation.1 | async-start | bytes 458752 | tf_op jit(solution)/shard_map/all_to_all | solution.py:318
  63.4 6.6 %all-gather = f32[1,48,128]{2,0,1:T(1,128)S(1)} all-gather(f32[1,12,128]{2,0,1:T(1,128)S(1)} %copy.21), channel_id=2, replica_groups={{0,32,64,96},{128,160,192,224},{256,288,320,352},{384,416,448,480},{1,3..., dimensions={1}, use_global_device_ids=true | all-gather | bytes 30720 | tf_op jit(solution)/shard_map/all_gather | solution.py:275
  70.1 2.7 %collective-permute-start.6 = (f32[48,128]{1,0:T(8,128)S(1)}, f32[48,128]{1,0:T(8,128)S(1)}, u32[]{:S(2)}, u32[]{:S(2)}) collective-permute-start(f32[48,128]{1,0:T(8,128)S(1)} %bitcast.30), channel_id=1, source_target_pairs={{0,1},{1,0},{2,3},{3,2},{4,5},{5,4},{6,7},{7,6},{8,9},{9,8},{10,11... | collective-permute-start | bytes 73736 | tf_op jit(solution)/shard_map/ppermute | solution.py:13
  72.8 3.7 %collective-permute-done.6 = f32[48,128]{1,0:T(8,128)S(1)} collective-permute-done((f32[48,128]{1,0:T(8,128)S(1)}, f32[48,128]{1,0:T(8,128)S(1)}, u32[]{:S(2)}, u32[]{:S(2)}) %collective-permute-start.6) | collective-permute-done | bytes 24608 | tf_op jit(solution)/shard_map/ppermute | solution.py:13
  76.4 0.0 all-to-all-done.1
  76.4 0.1 reduce_sum.19
  76.5 0.7 broadcast_in_dim.8
  77.2 11.4 %all-to-all-start.2 = ((f32[16,16,128]{2,1,0:T(8,128)}), f32[16,16,128]{2,1,0:T(8,128)S(1)}, u32[]{:S(2)}, u32[]{:S(2)}) async-start(f32[16,16,128]{2,1,0:T(8,128)} %broadcast_in_dim.8), calls=%async_computation.2 | async-start | bytes 262144 | tf_op jit(solution)/shard_map/all_to_all | solution.py:318
  88.6 6.6 %all-gather.1 = f32[4,4,128]{2,1,0:T(4,128)S(1)} all-gather(f32[1,4,128]{2,1,0:T(4,128)S(1)} %slice_bitcast_fusion.1), channel_id=1, replica_groups={{0,32,64,96},{128,160,192,224},{256,288,320,352},{384,416,448,480},{1,3..., dimensions={0}, use_global_device_ids=true | all-gather | bytes 10240 | tf_op jit(solution)/shard_map/all_gather | solution.py:275
  95.2 2.4 %collective-permute-start.7 = (f32[112,128]{1,0:T(8,128)S(1)}, f32[112,128]{1,0:T(8,128)S(1)}, u32[]{:S(2)}, u32[]{:S(2)}) collective-permute-start(f32[112,128]{1,0:T(8,128)S(1)} %pad_maximum_fusion.1.own), channel_id=1, source_target_pairs={{0,128},{32,160},{64,192},{96,224},{128,0},{160,32},{192,64},{224,... | collective-permute-start | bytes 172040 | tf_op jit(solution)/shard_map/ppermute | solution.py:279
  97.6 0.6 mul.39
  98.2 2.2 %collective-permute-done.7.beside = f32[112,128]{1,0:T(8,128)S(1)} collective-permute-done((f32[112,128]{1,0:T(8,128)S(1)}, f32[112,128]{1,0:T(8,128)S(1)}, u32[]{:S(2)}, u32[]{:S(2)}) %collective-permute-start.7) | collective-permute-done | bytes 57376 | tf_op jit(solution)/shard_map/ppermute | solution.py:279
  100.4 0.7 unfold_factors.1
  101.1 0.0 all-to-all-done.2
  101.1 0.7 multiply_bitcast_fusion
  (25 shorter events, 0.3 us)
Async XLA Ops:
  0.6 1.7 %copy-start = (f32[3,16,96,128]{3,2,1,0:T(8,128)S(1)}, f32[3,16,96,128]{3,2,1,0:T(8,128)}, u32[]{:S(2)}) copy-start(f32[3,16,96,128]{3,2,1,0:T(8,128)} %vel.3) | copy-start | bytes 7077892
  2.3 28.0 %copy-start.1 = (f32[3,2,96,128]{3,2,1,0:T(8,128)S(1)}, f32[3,2,96,128]{3,2,1,0:T(8,128)}, u32[]{:S(2)}) copy-start(f32[3,2,96,128]{3,2,1,0:T(8,128)} %below.1) | copy-start | bytes 884740
  2.3 28.0 %copy-start.2 = (f32[3,2,96,128]{3,2,1,0:T(8,128)S(1)}, f32[3,2,96,128]{3,2,1,0:T(8,128)}, u32[]{:S(2)}) copy-start(f32[3,2,96,128]{3,2,1,0:T(8,128)} %above.1) | copy-start | bytes 884740
  2.3 28.0 %copy-start.3 = (s32[512,128]{1,0:T(8,128)S(1)}, s32[512,128]{1,0:T(8,128)}, u32[]{:S(2)}) copy-start(s32[512,128]{1,0:T(8,128)} %phi_x.1) | copy-start | bytes 786436
  2.3 28.0 %copy-start.4 = (s32[128,256]{1,0:T(8,128)S(1)}, s32[128,256]{1,0:T(8,128)}, u32[]{:S(2)}) copy-start(s32[128,256]{1,0:T(8,128)} %omega_x.1) | copy-start | bytes 393220
  2.3 28.0 %copy-start.5 = (s32[96,256]{1,0:T(8,128)S(1)}, s32[96,256]{1,0:T(8,128)}, u32[]{:S(2)}) copy-start(s32[96,256]{1,0:T(8,128)} %omega_y.1) | copy-start | bytes 294916
  2.3 28.0 %copy-start.6 = (s32[16,256]{1,0:T(8,128)S(1)}, s32[16,256]{1,0:T(8,128)}, u32[]{:S(2)}) copy-start(s32[16,256]{1,0:T(8,128)} %omega_z.1) | copy-start | bytes 49156
  2.3 28.0 %copy-start.7 = (s32[2,16]{1,0:T(2,128)S(1)}, s32[2,16]{1,0:T(2,128)}, u32[]{:S(2)}) copy-start(s32[2,16]{1,0:T(2,128)} %phi_z.1) | copy-start | bytes 388
  3.1 27.3 %collective-permute-start = (f32[3,2,96,128]{3,2,1,0:T(8,128)S(1)}, f32[3,2,96,128]{3,2,1,0:T(8,128)S(1)}, u32[]{:S(2)}, u32[]{:S(2)}) collective-permute-start(f32[3,2,96,128]{3,2,1,0:T(8,128)S(1)} %get-tuple-element.15), channel_id=1, source_target_pairs={{0,1},{1,0},{2,3},{3,2},{4,5},{5,4},{6,7},{7,6},{8,9},{9,8},{10,11... | collective-permute-start | bytes 884744 | tf_op jit(solution)/shard_map/ppermute | solution.py:13
  8.7 20.7 %collective-permute-start.1 = (f32[3,32,128]{2,1,0:T(8,128)S(1)}, f32[3,32,128]{2,1,0:T(8,128)S(1)}, u32[]{:S(2)}, u32[]{:S(2)}) collective-permute-start(f32[3,32,128]{2,1,0:T(8,128)S(1)} %get-tuple-element.16), channel_id=1, source_target_pairs={{0,2},{2,0},{4,6},{6,4},{8,10},{10,8},{12,14},{14,12},{16,18},{18,... | collective-permute-start | bytes 147464 | tf_op jit(solution)/shard_map/ppermute | solution.py:21
  12.3 17.2 %collective-permute-start.2 = (f32[3,32,128]{2,1,0:T(8,128)S(1)}, f32[3,32,128]{2,1,0:T(8,128)S(1)}, u32[]{:S(2)}, u32[]{:S(2)}) collective-permute-start(f32[3,32,128]{2,1,0:T(8,128)S(1)} %get-tuple-element.17), channel_id=1, source_target_pairs={{2,4},{4,2},{6,8},{8,6},{10,12},{12,10},{14,16},{16,14},{18,20},{2... | collective-permute-start | bytes 147464 | tf_op jit(solution)/shard_map/ppermute | solution.py:21
  22.5 7.0 %collective-permute-start.3 = (f32[96,128]{1,0:T(8,128)S(1)}, f32[96,128]{1,0:T(8,128)S(1)}, u32[]{:S(2)}, u32[]{:S(2)}) collective-permute-start(f32[96,128]{1,0:T(8,128)S(1)} %get-tuple-element.18), channel_id=1, source_target_pairs={{32,64},{64,32},{96,128},{128,96},{160,192},{192,160},{224,256},{2... | collective-permute-start | bytes 147464 | tf_op jit(solution)/shard_map/ppermute | solution.py:21
  26.2 20.7 %copy-start.8 = (s32[512,96]{0,1:T(8,128)S(1)}, s32[512,96]{0,1:T(8,128)}, u32[]{:S(2)}) copy-start(s32[512,96]{0,1:T(8,128)} %param.16) | copy-start | bytes 589828
  26.2 4.1 %collective-permute-start.4 = (f32[96,128]{1,0:T(8,128)S(1)}, f32[96,128]{1,0:T(8,128)S(1)}, u32[]{:S(2)}, u32[]{:S(2)}) collective-permute-start(f32[96,128]{1,0:T(8,128)S(1)} %get-tuple-element.19), channel_id=1, source_target_pairs={{0,32},{32,0},{64,96},{96,64},{128,160},{160,128},{192,224},{224,1... | collective-permute-start | bytes 147464 | tf_op jit(solution)/shard_map/ppermute | solution.py:21
  36.9 19.3 %all-to-all-start = ((f32[32,40,128]{2,1,0:T(8,128)}), f32[32,40,128]{2,1,0:T(8,128)S(1)}, u32[]{:S(2)}, u32[]{:S(2)}) async-start(f32[32,40,128]{2,1,0:T(8,128)} %bitcast), calls=%async_computation | async-start | bytes 1310720 | tf_op jit(solution)/shard_map/all_to_all | solution.py:318
  42.1 14.0 %collective-permute-start.5 = (f32[256,128]{1,0:T(8,128)S(1)}, f32[256,128]{1,0:T(8,128)S(1)}, u32[]{:S(2)}, u32[]{:S(2)}) collective-permute-start(f32[256,128]{1,0:T(8,128)S(1)} %get-tuple-element.21), channel_id=1, source_target_pairs={{0,1},{1,0},{2,3},{3,2},{4,5},{5,4},{6,7},{7,6},{8,9},{9,8},{10,11... | collective-permute-start | bytes 393224 | tf_op jit(solution)/shard_map/ppermute | solution.py:13
  57.4 19.0 %all-to-all-start.1 = ((f32[16,7,4,128]{3,2,1,0:T(4,128)}), f32[16,7,4,128]{3,2,1,0:T(4,128)S(1)}, u32[]{:S(2)}, u32[]{:S(2)}) async-start(f32[16,7,4,128]{3,2,1,0:T(4,128)} %copy.20), calls=%async_computation.1 | async-start | bytes 458752 | tf_op jit(solution)/shard_map/all_to_all | solution.py:318
  70.1 6.4 %collective-permute-start.6 = (f32[48,128]{1,0:T(8,128)S(1)}, f32[48,128]{1,0:T(8,128)S(1)}, u32[]{:S(2)}, u32[]{:S(2)}) collective-permute-start(f32[48,128]{1,0:T(8,128)S(1)} %bitcast.30), channel_id=1, source_target_pairs={{0,1},{1,0},{2,3},{3,2},{4,5},{5,4},{6,7},{7,6},{8,9},{9,8},{10,11... | collective-permute-start | bytes 73736 | tf_op jit(solution)/shard_map/ppermute | solution.py:13
  77.2 23.9 %all-to-all-start.2 = ((f32[16,16,128]{2,1,0:T(8,128)}), f32[16,16,128]{2,1,0:T(8,128)S(1)}, u32[]{:S(2)}, u32[]{:S(2)}) async-start(f32[16,16,128]{2,1,0:T(8,128)} %broadcast_in_dim.8), calls=%async_computation.2 | async-start | bytes 262144 | tf_op jit(solution)/shard_map/all_to_all | solution.py:318
  95.2 5.2 %collective-permute-start.7 = (f32[112,128]{1,0:T(8,128)S(1)}, f32[112,128]{1,0:T(8,128)S(1)}, u32[]{:S(2)}, u32[]{:S(2)}) collective-permute-start(f32[112,128]{1,0:T(8,128)S(1)} %pad_maximum_fusion.1.own), channel_id=1, source_target_pairs={{0,128},{32,160},{64,192},{96,224},{128,0},{160,32},{192,64},{224,... | collective-permute-start | bytes 172040 | tf_op jit(solution)/shard_map/ppermute | solution.py:279

commit v11 on v10

--- a/solution.py
+++ b/solution.py
@@ -21,24 +21,37 @@
     return lax.ppermute(cells, axis, pairs)
 
 
-def pack_kernel(vel, near, x_even, x_odd, y_even, y_odd):
+def rims_kernel(vel, near, y_even, y_odd, head, tail, sems):
     gz = lax.axis_index("gz")
+    odd_y = lax.rem(lax.axis_index("gy"), 2) == 1
+    copies = [
+        pltpu.make_async_copy(vel.at[:, pl.ds(14 * (1 - gz), 2)], near, sems.at[0]),
+        pltpu.make_async_copy(vel.at[:, :, pl.ds(0, 8), :], head, sems.at[1]),
+        pltpu.make_async_copy(vel.at[:, :, pl.ds(88, 8), :], tail, sems.at[2]),
+    ]
+    for copy in copies:
+        copy.start()
+    for copy in copies:
+        copy.wait()
+    for c in range(3):
+        for k in range(16):
+            first = head[c, k, 0:2, :]
+            last = tail[c, k, 6:8, :]
+            y_even[c, 2 * k : 2 * k + 2, :] = jnp.where(odd_y, first, last)
+            y_odd[c, 2 * k : 2 * k + 2, :] = jnp.where(odd_y, last, first)
+
+
+def pack_kernel(vel, x_even, x_odd):
     odd_x = lax.rem(lax.axis_index("gx"), 2) == 1
-    odd_y = lax.rem(lax.axis_index("gy"), 2) == 1
     lane = lax.broadcasted_iota(jnp.int32, (96, 128), 1)
     high = jnp.zeros((96, 128), jnp.float32)
     low = jnp.zeros((96, 128), jnp.float32)
     for c in range(3):
-        near[c] = vel[c, pl.ds(14 * (1 - gz), 2)]
         for k in range(16):
             spot = 2 * (16 * c + k)
             turned = pltpu.roll(vel[c, k], spot + 2, 1)
             high = jnp.where((lane >= spot) & (lane < spot + 2), turned, high)
             low = jnp.where((lane >= spot + 2) & (lane < spot + 4), turned, low)
-            first = vel[c, k, 0:2, :]
-            last = vel[c, k, 94:96, :]
-            y_even[c, 2 * k : 2 * k + 2, :] = jnp.where(odd_y, first, last)
-            y_odd[c, 2 * k : 2 * k + 2, :] = jnp.where(odd_y, last, first)
     x_even[...] = jnp.where(odd_x, low, high)
     x_odd[...] = jnp.where(odd_x, high, low)
 
@@ -47,14 +60,28 @@
     rims = jax.ShapeDtypeStruct((96, 128), jnp.float32)
     rows = jax.ShapeDtypeStruct((3, 32, 128), jnp.float32)
     whole = pl.BlockSpec(memory_space=pltpu.VMEM)
-    return pl.pallas_call(
+    near, y_even, y_odd = pl.pallas_call(
+        rims_kernel,
+        in_specs=[pl.BlockSpec(memory_space=pl.ANY)],
+        out_specs=[whole] * 3,
+        out_shape=[jax.ShapeDtypeStruct((3, 2, 96, 128), jnp.float32), rows, rows],
+        scratch_shapes=[
+            pltpu.VMEM((3, 16, 8, 128), jnp.float32),
+            pltpu.VMEM((3, 16, 8, 128), jnp.float32),
+            pltpu.SemaphoreType.DMA((3,)),
+        ],
+        compiler_params=pltpu.CompilerParams(vmem_limit_bytes=62 * 1024 * 1024),
+        name="pack_rims",
+    )(velocity)
+    x_even, x_odd = pl.pallas_call(
         pack_kernel,
         in_specs=[whole],
-        out_specs=[whole] * 5,
-        out_shape=[jax.ShapeDtypeStruct((3, 2, 96, 128), jnp.float32), rims, rims, rows, rows],
+        out_specs=[whole] * 2,
+        out_shape=[rims, rims],
         compiler_params=pltpu.CompilerParams(vmem_limit_bytes=32 * 1024 * 1024),
         name="pack_halos",
     )(velocity)
+    return near, x_even, x_odd, y_even, y_odd
 
 
 def field_kernel(

time: 104 us -> 106 us (1.019)
  Pallas kernels: 7.88 us -> 9.8 us
    pallas_call x1 -> x2, Pallas kernels: 0.7 us -> 2.64 us  [the longest x1 1.96 us: pack(): pl.pallas_call(rims_kernel, in_specs=[pl.BlockSpec(memory_space=pl.ANY)],...]
where the time goes in v11:
time: 106 us; the launch traced here: 104 us
  starting transfers between devices  58.9 us (56%)
  waiting for transfers between devices  15.9 us (15%)
  blocking collectives  13.2 us (12%)
  Pallas kernels  9.8 us (9%)
  local copies, waits for them, and re-layouts  3.9 us (4%)
    all_to_all x3, starting transfers between devices, exchange(): return lax.all_to_all(rows, axes, 0, 0, tiled=True)  22.7 us
    ppermute x4, starting transfers between devices, edge_swap(): return lax.ppermute(cells, axis, pairs)  20.7 us
    all_gather x2, blocking collectives, gather(): lax.all_gather(rows, 'gx', axis=0, tiled=True, axis_index_groups=NEAR)  13.2 us
    ppermute x3, starting transfers between devices, shift_permute(): lax.ppermute(cells, axis, [(i, (i + step) % count) for i in range(count)])  13.1 us
    ppermute x3, waiting for transfers between devices, shift_permute(): lax.ppermute(cells, axis, [(i, (i + step) % count) for i in range(count)])  12.9 us
    pallas_call x1, Pallas kernels, field(): pl.pallas_call(field_kernel, in_specs=[outside] * 13, out_specs=[whole] *...  6.49 us
    ppermute x1, starting transfers between devices, pair_swap(): return lax.ppermute(rows, 'gx', [(i, i ^ 4) for i in range(16)])  2.39 us
    ppermute x1, waiting for transfers between devices, pair_swap(): return lax.ppermute(rows, 'gx', [(i, i ^ 4) for i in range(16)])  2.19 us
  transfers between devices with their start and end apart: 11, of which 4 were waited for; matrix products, arithmetic and copies ran while one was open for 1% of the time, Pallas kernels for 1%

profile of v11, /device:TPU:1, one launch (start us, length us, event | category | flops | bytes accessed | tf_op | source)
XLA Modules:
  0.0 103.7 jit_solution(5708883940646770676)
XLA Ops:
  0.6 0.0 copy-start.1
  0.6 0.0 copy-start.2
  0.7 0.0 copy-start.4
  0.7 0.0 copy-start.5
  0.7 0.0 copy-start.6
  0.7 0.0 copy-start.3
  0.7 0.0 copy-start.7
  0.7 2.0 %pack_rims.1 = (f32[3,2,96,128]{3,2,1,0:T(8,128)}, f32[3,32,128]{2,1,0:T(8,128)}, f32[3,32,128]{2,1,0:T(8,128)}) custom-call(f32[3,16,96,128]{3,2,1,0:T(8,128)} %vel.5), custom_call_target="tpu_custom_call" | custom-call | tf_op jit(solution)/shard_map/pack_rims/pallas_call | solution.py:63
  2.7 5.7 %collective-permute-start = (f32[3,2,96,128]{3,2,1,0:T(8,128)}, f32[3,2,96,128]{3,2,1,0:T(8,128)S(1)}, u32[]{:S(2)}, u32[]{:S(2)}) collective-permute-start(f32[3,2,96,128]{3,2,1,0:T(8,128)} %get-tuple-element.15), channel_id=1, source_target_pairs={{0,1},{1,0},{2,3},{3,2},{4,5},{5,4},{6,7},{7,6},{8,9},{9,8},{10,11... | collective-permute-start | bytes 884744 | tf_op jit(solution)/shard_map/ppermute | solution.py:13
  8.3 3.5 %collective-permute-start.1 = (f32[3,32,128]{2,1,0:T(8,128)}, f32[3,32,128]{2,1,0:T(8,128)S(1)}, u32[]{:S(2)}, u32[]{:S(2)}) collective-permute-start(f32[3,32,128]{2,1,0:T(8,128)} %get-tuple-element.16), channel_id=1, source_target_pairs={{0,2},{2,0},{4,6},{6,4},{8,10},{10,8},{12,14},{14,12},{16,18},{18,... | collective-permute-start | bytes 147464 | tf_op jit(solution)/shard_map/ppermute | solution.py:21
  11.9 10.2 %collective-permute-start.2 = (f32[3,32,128]{2,1,0:T(8,128)}, f32[3,32,128]{2,1,0:T(8,128)S(1)}, u32[]{:S(2)}, u32[]{:S(2)}) collective-permute-start(f32[3,32,128]{2,1,0:T(8,128)} %get-tuple-element.17), channel_id=1, source_target_pairs={{2,4},{4,2},{6,8},{8,6},{10,12},{12,10},{14,16},{16,14},{18,20},{2... | collective-permute-start | bytes 147464 | tf_op jit(solution)/shard_map/ppermute | solution.py:21
  22.1 0.0 copy-start
  22.1 1.7 %copy-done = f32[3,16,96,128]{3,2,1,0:T(8,128)S(1)} copy-done((f32[3,16,96,128]{3,2,1,0:T(8,128)S(1)}, f32[3,16,96,128]{3,2,1,0:T(8,128)}, u32[]{:S(2)}) %copy-start) | copy-done | bytes 2359320
  23.8 0.7 pack_halos.1
  24.5 3.7 %collective-permute-start.3 = (f32[96,128]{1,0:T(8,128)S(1)}, f32[96,128]{1,0:T(8,128)S(1)}, u32[]{:S(2)}, u32[]{:S(2)}) collective-permute-start(f32[96,128]{1,0:T(8,128)S(1)} %get-tuple-element.18), channel_id=1, source_target_pairs={{32,64},{64,32},{96,128},{128,96},{160,192},{192,160},{224,256},{2... | collective-permute-start | bytes 147464 | tf_op jit(solution)/shard_map/ppermute | solution.py:21
  28.2 0.0 copy-start.8
  28.2 3.2 %collective-permute-start.4 = (f32[96,128]{1,0:T(8,128)S(1)}, f32[96,128]{1,0:T(8,128)S(1)}, u32[]{:S(2)}, u32[]{:S(2)}) collective-permute-start(f32[96,128]{1,0:T(8,128)S(1)} %get-tuple-element.19), channel_id=1, source_target_pairs={{0,32},{32,0},{64,96},{96,64},{128,160},{160,128},{192,224},{224,1... | collective-permute-start | bytes 147464 | tf_op jit(solution)/shard_map/ppermute | solution.py:21
  31.4 0.0 collective-permute-done.1.y_even
  31.4 0.0 collective-permute-done.2.y_odd
  31.4 0.0 collective-permute-done.3.x_odd
  31.5 0.8 collective-permute-done.4.x_even
  32.3 0.0 collective-permute-done.far
  32.3 0.0 copy-done.1
  32.3 0.0 copy-done.2
  32.3 0.0 copy-done.4
  32.3 6.5 %field_products.1 = (f32[1280,128]{1,0:T(8,128)}, f32[256,128]{1,0:T(8,128)S(1)}) custom-call(f32[3,16,96,128]{3,2,1,0:T(8,128)S(1)} %copy-done, f32[3,2,96,128]{3,2,1,0:T(8,128)S(1)} %collective-permute-done.far, f32[3,2,96,128]{3,2,1,0:T(8,128)S(1)} %copy-done.1, f32[3,2,96,128]{3,2,1,0:T(8,128)S(1)} %copy-done.2, ...), custom_call_target="tpu_custom_call" | custom-call | tf_op jit(solution)/shard_map/field_products/pallas_call | solution.py:262
  38.8 5.2 %all-to-all-start = ((f32[32,40,128]{2,1,0:T(8,128)}), f32[32,40,128]{2,1,0:T(8,128)S(1)}, u32[]{:S(2)}, u32[]{:S(2)}) async-start(f32[32,40,128]{2,1,0:T(8,128)} %bitcast), calls=%async_computation | async-start | bytes 1310720 | tf_op jit(solution)/shard_map/all_to_all | solution.py:345
  44.1 4.8 %collective-permute-start.5 = (f32[256,128]{1,0:T(8,128)S(1)}, f32[256,128]{1,0:T(8,128)S(1)}, u32[]{:S(2)}, u32[]{:S(2)}) collective-permute-start(f32[256,128]{1,0:T(8,128)S(1)} %get-tuple-element.21), channel_id=1, source_target_pairs={{0,1},{1,0},{2,3},{3,2},{4,5},{5,4},{6,7},{7,6},{8,9},{9,8},{10,11... | collective-permute-start | bytes 393224 | tf_op jit(solution)/shard_map/ppermute | solution.py:13
  48.9 9.2 %collective-permute-done.5 = f32[256,128]{1,0:T(8,128)S(1)} collective-permute-done((f32[256,128]{1,0:T(8,128)S(1)}, f32[256,128]{1,0:T(8,128)S(1)}, u32[]{:S(2)}, u32[]{:S(2)}) %collective-permute-start.5) | collective-permute-done | bytes 131104 | tf_op jit(solution)/shard_map/ppermute | solution.py:13
  58.2 0.0 all-to-all-done
  58.3 0.1 fusion.19
  58.3 0.1 fusion.3
  58.6 0.8 copy.20
  59.4 6.0 %all-to-all-start.1 = ((f32[16,7,4,128]{3,2,1,0:T(4,128)}), f32[16,7,4,128]{3,2,1,0:T(4,128)S(1)}, u32[]{:S(2)}, u32[]{:S(2)}) async-start(f32[16,7,4,128]{3,2,1,0:T(4,128)} %copy.20), calls=%async_computation.1 | async-start | bytes 458752 | tf_op jit(solution)/shard_map/all_to_all | solution.py:345
  65.4 6.6 %all-gather = f32[1,48,128]{2,0,1:T(1,128)S(1)} all-gather(f32[1,12,128]{2,0,1:T(1,128)S(1)} %copy.21), channel_id=2, replica_groups={{0,32,64,96},{128,160,192,224},{256,288,320,352},{384,416,448,480},{1,3..., dimensions={1}, use_global_device_ids=true | all-gather | bytes 30720 | tf_op jit(solution)/shard_map/all_gather | solution.py:302
  72.0 2.7 %collective-permute-start.6 = (f32[48,128]{1,0:T(8,128)S(1)}, f32[48,128]{1,0:T(8,128)S(1)}, u32[]{:S(2)}, u32[]{:S(2)}) collective-permute-start(f32[48,128]{1,0:T(8,128)S(1)} %bitcast.30), channel_id=1, source_target_pairs={{0,1},{1,0},{2,3},{3,2},{4,5},{5,4},{6,7},{7,6},{8,9},{9,8},{10,11... | collective-permute-start | bytes 73736 | tf_op jit(solution)/shard_map/ppermute | solution.py:13
  74.7 3.7 %collective-permute-done.6 = f32[48,128]{1,0:T(8,128)S(1)} collective-permute-done((f32[48,128]{1,0:T(8,128)S(1)}, f32[48,128]{1,0:T(8,128)S(1)}, u32[]{:S(2)}, u32[]{:S(2)}) %collective-permute-start.6) | collective-permute-done | bytes 24608 | tf_op jit(solution)/shard_map/ppermute | solution.py:13
  78.4 0.0 all-to-all-done.1
  78.4 0.1 reduce_sum.19
  78.5 0.7 broadcast_in_dim.8
  79.1 11.4 %all-to-all-start.2 = ((f32[16,16,128]{2,1,0:T(8,128)}), f32[16,16,128]{2,1,0:T(8,128)S(1)}, u32[]{:S(2)}, u32[]{:S(2)}) async-start(f32[16,16,128]{2,1,0:T(8,128)} %broadcast_in_dim.8), calls=%async_computation.2 | async-start | bytes 262144 | tf_op jit(solution)/shard_map/all_to_all | solution.py:345
  90.6 6.6 %all-gather.1 = f32[4,4,128]{2,1,0:T(4,128)S(1)} all-gather(f32[1,4,128]{2,1,0:T(4,128)S(1)} %slice_bitcast_fusion.1), channel_id=1, replica_groups={{0,32,64,96},{128,160,192,224},{256,288,320,352},{384,416,448,480},{1,3..., dimensions={0}, use_global_device_ids=true | all-gather | bytes 10240 | tf_op jit(solution)/shard_map/all_gather | solution.py:302
  97.2 2.4 %collective-permute-start.7 = (f32[112,128]{1,0:T(8,128)S(1)}, f32[112,128]{1,0:T(8,128)S(1)}, u32[]{:S(2)}, u32[]{:S(2)}) collective-permute-start(f32[112,128]{1,0:T(8,128)S(1)} %pad_maximum_fusion.1.own), channel_id=1, source_target_pairs={{0,128},{32,160},{64,192},{96,224},{128,0},{160,32},{192,64},{224,... | collective-permute-start | bytes 172040 | tf_op jit(solution)/shard_map/ppermute | solution.py:306
  99.6 0.6 mul.39
  100.2 2.2 %collective-permute-done.7.beside = f32[112,128]{1,0:T(8,128)S(1)} collective-permute-done((f32[112,128]{1,0:T(8,128)S(1)}, f32[112,128]{1,0:T(8,128)S(1)}, u32[]{:S(2)}, u32[]{:S(2)}) %collective-permute-start.7) | collective-permute-done | bytes 57376 | tf_op jit(solution)/shard_map/ppermute | solution.py:306
  102.4 0.7 unfold_factors.1
  103.1 0.0 all-to-all-done.2
  103.1 0.7 multiply_bitcast_fusion
  (26 shorter events, 0.3 us)
Async XLA Ops:
  0.6 31.7 %copy-start.1 = (f32[3,2,96,128]{3,2,1,0:T(8,128)S(1)}, f32[3,2,96,128]{3,2,1,0:T(8,128)}, u32[]{:S(2)}) copy-start(f32[3,2,96,128]{3,2,1,0:T(8,128)} %below.1) | copy-start | bytes 884740
  0.6 31.6 %copy-start.2 = (f32[3,2,96,128]{3,2,1,0:T(8,128)S(1)}, f32[3,2,96,128]{3,2,1,0:T(8,128)}, u32[]{:S(2)}) copy-start(f32[3,2,96,128]{3,2,1,0:T(8,128)} %above.1) | copy-start | bytes 884740
  0.7 31.6 %copy-start.4 = (s32[128,256]{1,0:T(8,128)S(1)}, s32[128,256]{1,0:T(8,128)}, u32[]{:S(2)}) copy-start(s32[128,256]{1,0:T(8,128)} %omega_x.1) | copy-start | bytes 393220
  0.7 31.6 %copy-start.5 = (s32[96,256]{1,0:T(8,128)S(1)}, s32[96,256]{1,0:T(8,128)}, u32[]{:S(2)}) copy-start(s32[96,256]{1,0:T(8,128)} %omega_y.1) | copy-start | bytes 294916
  0.7 31.6 %copy-start.6 = (s32[16,256]{1,0:T(8,128)S(1)}, s32[16,256]{1,0:T(8,128)}, u32[]{:S(2)}) copy-start(s32[16,256]{1,0:T(8,128)} %omega_z.1) | copy-start | bytes 49156
  0.7 31.6 %copy-start.3 = (s32[512,128]{1,0:T(8,128)S(1)}, s32[512,128]{1,0:T(8,128)}, u32[]{:S(2)}) copy-start(s32[512,128]{1,0:T(8,128)} %phi_x.1) | copy-start | bytes 786436
  0.7 31.6 %copy-start.7 = (s32[2,16]{1,0:T(2,128)S(1)}, s32[2,16]{1,0:T(2,128)}, u32[]{:S(2)}) copy-start(s32[2,16]{1,0:T(2,128)} %phi_z.1) | copy-start | bytes 388
  2.7 29.6 %collective-permute-start = (f32[3,2,96,128]{3,2,1,0:T(8,128)}, f32[3,2,96,128]{3,2,1,0:T(8,128)S(1)}, u32[]{:S(2)}, u32[]{:S(2)}) collective-permute-start(f32[3,2,96,128]{3,2,1,0:T(8,128)} %get-tuple-element.15), channel_id=1, source_target_pairs={{0,1},{1,0},{2,3},{3,2},{4,5},{5,4},{6,7},{7,6},{8,9},{9,8},{10,11... | collective-permute-start | bytes 884744 | tf_op jit(solution)/shard_map/ppermute | solution.py:13
  8.3 23.1 %collective-permute-start.1 = (f32[3,32,128]{2,1,0:T(8,128)}, f32[3,32,128]{2,1,0:T(8,128)S(1)}, u32[]{:S(2)}, u32[]{:S(2)}) collective-permute-start(f32[3,32,128]{2,1,0:T(8,128)} %get-tuple-element.16), channel_id=1, source_target_pairs={{0,2},{2,0},{4,6},{6,4},{8,10},{10,8},{12,14},{14,12},{16,18},{18,... | collective-permute-start | bytes 147464 | tf_op jit(solution)/shard_map/ppermute | solution.py:21
  11.9 19.6 %collective-permute-start.2 = (f32[3,32,128]{2,1,0:T(8,128)}, f32[3,32,128]{2,1,0:T(8,128)S(1)}, u32[]{:S(2)}, u32[]{:S(2)}) collective-permute-start(f32[3,32,128]{2,1,0:T(8,128)} %get-tuple-element.17), channel_id=1, source_target_pairs={{2,4},{4,2},{6,8},{8,6},{10,12},{12,10},{14,16},{16,14},{18,20},{2... | collective-permute-start | bytes 147464 | tf_op jit(solution)/shard_map/ppermute | solution.py:21
  22.1 1.7 %copy-start = (f32[3,16,96,128]{3,2,1,0:T(8,128)S(1)}, f32[3,16,96,128]{3,2,1,0:T(8,128)}, u32[]{:S(2)}) copy-start(f32[3,16,96,128]{3,2,1,0:T(8,128)} %vel.5) | copy-start | bytes 7077892
  24.5 7.0 %collective-permute-start.3 = (f32[96,128]{1,0:T(8,128)S(1)}, f32[96,128]{1,0:T(8,128)S(1)}, u32[]{:S(2)}, u32[]{:S(2)}) collective-permute-start(f32[96,128]{1,0:T(8,128)S(1)} %get-tuple-element.18), channel_id=1, source_target_pairs={{32,64},{64,32},{96,128},{128,96},{160,192},{192,160},{224,256},{2... | collective-permute-start | bytes 147464 | tf_op jit(solution)/shard_map/ppermute | solution.py:21
  28.2 20.7 %copy-start.8 = (s32[512,96]{0,1:T(8,128)S(1)}, s32[512,96]{0,1:T(8,128)}, u32[]{:S(2)}) copy-start(s32[512,96]{0,1:T(8,128)} %param.16) | copy-start | bytes 589828
  28.2 4.1 %collective-permute-start.4 = (f32[96,128]{1,0:T(8,128)S(1)}, f32[96,128]{1,0:T(8,128)S(1)}, u32[]{:S(2)}, u32[]{:S(2)}) collective-permute-start(f32[96,128]{1,0:T(8,128)S(1)} %get-tuple-element.19), channel_id=1, source_target_pairs={{0,32},{32,0},{64,96},{96,64},{128,160},{160,128},{192,224},{224,1... | collective-permute-start | bytes 147464 | tf_op jit(solution)/shard_map/ppermute | solution.py:21
  38.8 19.3 %all-to-all-start = ((f32[32,40,128]{2,1,0:T(8,128)}), f32[32,40,128]{2,1,0:T(8,128)S(1)}, u32[]{:S(2)}, u32[]{:S(2)}) async-start(f32[32,40,128]{2,1,0:T(8,128)} %bitcast), calls=%async_computation | async-start | bytes 1310720 | tf_op jit(solution)/shard_map/all_to_all | solution.py:345
  44.1 14.0 %collective-permute-start.5 = (f32[256,128]{1,0:T(8,128)S(1)}, f32[256,128]{1,0:T(8,128)S(1)}, u32[]{:S(2)}, u32[]{:S(2)}) collective-permute-start(f32[256,128]{1,0:T(8,128)S(1)} %get-tuple-element.21), channel_id=1, source_target_pairs={{0,1},{1,0},{2,3},{3,2},{4,5},{5,4},{6,7},{7,6},{8,9},{9,8},{10,11... | collective-permute-start | bytes 393224 | tf_op jit(solution)/shard_map/ppermute | solution.py:13
  59.4 19.0 %all-to-all-start.1 = ((f32[16,7,4,128]{3,2,1,0:T(4,128)}), f32[16,7,4,128]{3,2,1,0:T(4,128)S(1)}, u32[]{:S(2)}, u32[]{:S(2)}) async-start(f32[16,7,4,128]{3,2,1,0:T(4,128)} %copy.20), calls=%async_computation.1 | async-start | bytes 458752 | tf_op jit(solution)/shard_map/all_to_all | solution.py:345
  72.0 6.4 %collective-permute-start.6 = (f32[48,128]{1,0:T(8,128)S(1)}, f32[48,128]{1,0:T(8,128)S(1)}, u32[]{:S(2)}, u32[]{:S(2)}) collective-permute-start(f32[48,128]{1,0:T(8,128)S(1)} %bitcast.30), channel_id=1, source_target_pairs={{0,1},{1,0},{2,3},{3,2},{4,5},{5,4},{6,7},{7,6},{8,9},{9,8},{10,11... | collective-permute-start | bytes 73736 | tf_op jit(solution)/shard_map/ppermute | solution.py:13
  79.1 23.9 %all-to-all-start.2 = ((f32[16,16,128]{2,1,0:T(8,128)}), f32[16,16,128]{2,1,0:T(8,128)S(1)}, u32[]{:S(2)}, u32[]{:S(2)}) async-start(f32[16,16,128]{2,1,0:T(8,128)} %broadcast_in_dim.8), calls=%async_computation.2 | async-start | bytes 262144 | tf_op jit(solution)/shard_map/all_to_all | solution.py:345
  97.2 5.2 %collective-permute-start.7 = (f32[112,128]{1,0:T(8,128)S(1)}, f32[112,128]{1,0:T(8,128)S(1)}, u32[]{:S(2)}, u32[]{:S(2)}) collective-permute-start(f32[112,128]{1,0:T(8,128)S(1)} %pad_maximum_fusion.1.own), channel_id=1, source_target_pairs={{0,128},{32,160},{64,192},{96,224},{128,0},{160,32},{192,64},{224,... | collective-permute-start | bytes 172040 | tf_op jit(solution)/shard_map/ppermute | solution.py:306
